TPU v7x, 32 devices: a whole 2x2x4 slice. The times are simulated.
32 devices in a mesh: section: 4 (over x, core), expert: 4 (over z), dp: 2 (over y).
Axes of the slice: x: 2, y: 2, z: 4, core: 2. Of those that a mesh axis runs over, the one named last changes fastest.
Arguments:
- fwd_in: bfloat16 [4, 384, 2048], P('section', 'expert'), may hold values from -6 to 6
- fwd_routes: int32 [4, 384, 8], P('section', 'expert'), may hold values from 0 to 31, all different within a row; in each aligned block of 96 rows (0 to 95, 96 to 191, ..., all dimensions but the last counted through in order) at most 26 rows name the same one
- fwd_numer: int32 [4, 384, 8], P('section', 'expert'), may hold values from 1 to 255
- bwd_saved: bfloat16 [4, 384, 2048], P('section', 'expert'), may hold values from -6 to 6
- bwd_routes: int32 [4, 384, 8], P('section', 'expert'), may hold values from 0 to 31, all different within a row; in each aligned block of 96 rows (0 to 95, 96 to 191, ..., all dimensions but the last counted through in order) at most 26 rows name the same one
- bwd_numer: int32 [4, 384, 8], P('section', 'expert'), may hold values from 1 to 255
- bwd_grad: bfloat16 [4, 384, 2048], P('section', 'expert'), may hold values from -6 to 6
- w_gate: bfloat16 [4, 32, 2048, 768], P('section', 'expert', None, 'dp'), may hold values from -0.125 to 0.125
- w_up: bfloat16 [4, 32, 2048, 768], P('section', 'expert', None, 'dp'), may hold values from -0.125 to 0.125
- w_down: bfloat16 [4, 32, 768, 2048], P('section', 'expert', 'dp'), may hold values from -0.21875 to 0.21875
Outputs:
- next_fwd: bfloat16 [4, 384, 2048], P('section', 'expert')
- next_bwd: bfloat16 [4, 384, 2048], P('section', 'expert')
- grad_gate: bfloat16 [4, 32, 2048, 768], P('section', 'expert', None, 'dp')
- grad_up: bfloat16 [4, 32, 2048, 768], P('section', 'expert', None, 'dp')
- grad_down: bfloat16 [4, 32, 768, 2048], P('section', 'expert', 'dp')
Inputs may be any that keep to these rules, and one draw needn't show every extreme that they name: `fwd_routes`: each token names 8 different experts. In each aligned block of 96 rows (the tokens of one index of expert of one section) no expert is named more than 26 times; in some blocks some expert is named exactly 26 times. `bwd_routes`: each token names 8 different experts. In each aligned block of 96 rows (the tokens of one index of expert of one section) no expert is named more than 26 times; in some blocks some expert is named exactly 26 times.
All inputs are finite; a program needn't handle non-finite values.
Results may differ from a plain program's by a relative error of at most 0.0058.
Values may be sent and summed in bfloat16 or wider, within the bound.
No kernel may reach another device: no remote copies, remote signals or barrier semaphores. Data moves between devices by JAX's collectives and lax.ppermute only.
A program may use at most 192 MiB of HBM per device.

v0:
```python
import jax
import jax.numpy as jnp
from jax import lax
from jax.sharding import PartitionSpec as P

EXPERTS = 32
MOST = 26


def passed_along(block, axis, distance):
    devices = range(lax.axis_size(axis))
    route = [((i - distance) % len(devices), i) for i in devices]
    return lax.ppermute(block, axis, route)


def slot_ranks(routes):
    flat_routes = routes.reshape(-1)
    onehot_table = (flat_routes[:, None] == jnp.arange(EXPERTS, dtype=jnp.int32)[None, :]).astype(
        jnp.int32
    )
    earlier = jnp.cumsum(onehot_table, 0) - onehot_table
    return (flat_routes, jnp.sum(earlier * onehot_table, 1))


def combine_weights(numerators):
    counted = numerators.astype(jnp.float32)
    return counted / jnp.sum(counted, -1, keepdims=True)


def packed_rows(rows, positions, groups):
    filled = jnp.zeros((EXPERTS * MOST, rows.shape[-1]), rows.dtype).at[positions].set(rows)
    return filled.reshape(groups, EXPERTS // groups, MOST, rows.shape[-1])


def handoff(value, direction):
    return passed_along(value, "section", direction)


def project(rows, gate_weight, up_weight):
    gate_value = jnp.einsum("semd,edf->semf", rows, gate_weight, preferred_element_type=jnp.float32)
    up_value = jnp.einsum("semd,edf->semf", rows, up_weight, preferred_element_type=jnp.float32)
    return (gate_value, up_value)


def local_backward(gate_value, up_value, grad_rows, down_weight):
    silu_gate = jax.nn.silu(gate_value)
    sigmoid_gate = jax.nn.sigmoid(gate_value)
    hidden = (silu_gate * up_value).astype(jnp.bfloat16)
    hidden_grad = jnp.einsum(
        "semd,efd->semf", grad_rows, down_weight, preferred_element_type=jnp.float32
    )
    up_grad = (hidden_grad * silu_gate).astype(jnp.bfloat16)
    gate_grad = (
        hidden_grad * up_value * sigmoid_gate * (1.0 + gate_value * (1.0 - sigmoid_gate))
    ).astype(jnp.bfloat16)
    return (hidden, gate_grad, up_grad)


def rows_back(gate_grad, up_grad, gate_weight, up_weight):
    return jnp.einsum(
        "semf,edf->semd", gate_grad, gate_weight, preferred_element_type=jnp.float32
    ) + jnp.einsum("semf,edf->semd", up_grad, up_weight, preferred_element_type=jnp.float32)


def weight_terms(saved_rows, grad_rows, back_hidden, gate_grad, up_grad):
    gate_term = jnp.einsum(
        "semd,semf->edf", saved_rows, gate_grad, preferred_element_type=jnp.float32
    )
    up_term = jnp.einsum("semd,semf->edf", saved_rows, up_grad, preferred_element_type=jnp.float32)
    down_term = jnp.einsum(
        "semf,semd->efd", back_hidden, grad_rows, preferred_element_type=jnp.float32
    )
    return (gate_term, up_term, down_term)


def mix_rows(base, returned, positions, weights, choices_per):
    width = base.shape[-1]
    picked = (
        returned.reshape(-1, width)[positions].reshape(-1, choices_per, width).astype(jnp.float32)
    )
    return (base.astype(jnp.float32) + jnp.sum(weights[:, :, None] * picked, 1)).astype(
        jnp.bfloat16
    )


def local(
    fwd_in, fwd_routes, fwd_numer, bwd_saved, bwd_routes, bwd_numer, bwd_grad, w_gate, w_up, w_down
):
    groups = lax.axis_size("expert")
    inputs = fwd_in[0]
    saved = bwd_saved[0]
    grad_in = bwd_grad[0]
    model_width = inputs.shape[-1]
    choices_per = fwd_routes.shape[-1]
    fwd_flat, fwd_rank = slot_ranks(fwd_routes[0])
    back_flat, back_rank = slot_ranks(bwd_routes[0])
    fwd_positions = fwd_flat * MOST + fwd_rank
    back_positions = back_flat * MOST + back_rank
    mixing = combine_weights(fwd_numer[0])
    back_mixing = combine_weights(bwd_numer[0])
    unit_weights = jnp.ones_like(back_mixing)
    scaled_grad = (back_mixing[:, :, None] * grad_in.astype(jnp.float32)[:, None, :]).astype(
        jnp.bfloat16
    )
    send_inputs = packed_rows(jnp.repeat(inputs, choices_per, 0), fwd_positions, groups)
    send_saved = packed_rows(jnp.repeat(saved, choices_per, 0), back_positions, groups)
    send_grad = packed_rows(scaled_grad.reshape(-1, model_width), back_positions, groups)
    gate_half = w_gate[0]
    up_half = w_up[0]
    down_half = w_down[0]
    recv_inputs, recv_saved, recv_grad = (
        lax.all_to_all(send_inputs, "expert", split_axis=0, concat_axis=0, tiled=True),
        lax.all_to_all(send_saved, "expert", split_axis=0, concat_axis=0, tiled=True),
        lax.all_to_all(send_grad, "expert", split_axis=0, concat_axis=0, tiled=True),
    )
    gate_value, up_value = project(recv_inputs, gate_half, up_half)
    hidden = (jax.nn.silu(gate_value) * up_value).astype(jnp.bfloat16)
    out_term = jnp.einsum("semf,efd->semd", hidden, down_half, preferred_element_type=jnp.float32)
    back_gate, back_up = project(recv_saved, gate_half, up_half)
    back_hidden, gate_grad, up_grad = local_backward(back_gate, back_up, recv_grad, down_half)
    grad_term = rows_back(gate_grad, up_grad, gate_half, up_half)
    gate_term, up_term, down_term = weight_terms(
        recv_saved, recv_grad, back_hidden, gate_grad, up_grad
    )
    gate_sum = gate_term.astype(jnp.bfloat16)
    up_sum = up_term.astype(jnp.bfloat16)
    down_sum = down_term.astype(jnp.bfloat16)
    out_total, grad_total = (
        lax.psum_scatter(out_term, "dp", scatter_dimension=3, tiled=True),
        lax.psum_scatter(grad_term, "dp", scatter_dimension=3, tiled=True),
    )
    out_part = out_total.astype(jnp.bfloat16)
    grad_part = grad_total.astype(jnp.bfloat16)
    out_rows, row_grad = (
        lax.all_gather(out_part, "dp", axis=3, tiled=True),
        lax.all_gather(grad_part, "dp", axis=3, tiled=True),
    )
    back_out, back_grad = (
        lax.all_to_all(out_rows, "expert", split_axis=0, concat_axis=0, tiled=True),
        lax.all_to_all(row_grad, "expert", split_axis=0, concat_axis=0, tiled=True),
    )
    layer_out = mix_rows(inputs, back_out, fwd_positions, mixing, choices_per)
    input_grad = mix_rows(grad_in, back_grad, back_positions, unit_weights, choices_per)
    next_fwd = handoff(layer_out[None], 1)
    next_bwd = handoff(input_grad[None], -1)
    return (next_fwd, next_bwd, gate_sum[None], up_sum[None], down_sum[None])


def solution(mesh):
    in_specs = (
        P("section", "expert", None),
        P("section", "expert", None),
        P("section", "expert", None),
        P("section", "expert", None),
        P("section", "expert", None),
        P("section", "expert", None),
        P("section", "expert", None),
        P("section", "expert", None, "dp"),
        P("section", "expert", None, "dp"),
        P("section", "expert", "dp", None),
    )
    out_specs = (
        P("section", "expert", None),
        P("section", "expert", None),
        P("section", "expert", None, "dp"),
        P("section", "expert", None, "dp"),
        P("section", "expert", "dp", None),
    )
    return jax.shard_map(local, mesh=mesh, in_specs=in_specs, out_specs=out_specs, check_vma=False)
```

profile of v0, /device:TPU:0, one launch (start us, length us, event | category | flops | bytes accessed | tf_op | source)
XLA Modules:
  0.0 648.7 jit_solution(9601240652703570069)
XLA Ops:
  11.3 9.4 %scatter_custom_fusion = bf16[832,2048]{1,0:T(8,128)(2,1)} fusion(s32[768]{0:T(1024)S(1)} %fusion.75, bf16[]{:T(256)} %constant.9.clone.1, bf16[96,2048]{1,0:T(8,128)(2,1)} %bitcast.198), kind=kCustom, calls=%fused_computation.45 | custom fusion | bytes 3801090 | tf_op jit(solution)/shard_map/scatter | solution.py:31
  20.7 4.8 reshape.184
  29.6 82.7 %all_to_all.25 = bf16[4,8,26,2048]{3,1,2,0:T(8,128)(2,1)S(1)} all-to-all(bf16[4,8,26,2048]{3,1,2,0:T(8,128)(2,1)S(1)} %copy.36), channel_id=1, replica_groups=mesh['section'=4,'expert'=4,'dp'=2] {'expert'}, dimensions={0} | all-to-all | bytes 6815744 | tf_op jit(solution)/shard_map/all_to_all | solution.py:112
  112.2 9.6 %fusion.7 = f32[8,4,26,384]{3,2,1,0:T(8,128)S(1)} fusion(bf16[1,8,2048,384]{3,2,1,0:T(8,128)(2,1)} %param.17, bf16[4,8,26,2048]{3,1,2,0:T(8,128)(2,1)S(1)} %all_to_all.25), kind=kOutput, calls=%fused_computation.15 | convolution fusion | flops 1308622848 | bytes 17268736 | tf_op jit(solution)/shard_map/semd,edf->semf/dot_general | solution.py:40
  121.9 5.0 fusion.54
  126.9 10.8 %fusion.21 = f32[4,8,26,2048]{3,2,0,1:T(8,128)} fusion(bf16[4,8,26,384]{3,2,0,1:T(8,128)(2,1)S(1)} %fusion.54, bf16[1,8,384,2048]{3,2,1,0:T(8,128)(2,1)} %param.19), kind=kOutput, calls=%fused_computation.33 | convolution fusion | flops 1308622848 | bytes 20037632 | tf_op jit(solution)/shard_map/semf,efd->semd/dot_general | solution.py:118
  141.0 9.0 %scatter_custom_fusion.2 = bf16[832,2048]{1,0:T(8,128)(2,1)} fusion(s32[768]{0:T(1024)S(1)} %fusion.76, bf16[]{:T(256)} %constant.9.clone.1, bf16[96,2048]{1,0:T(8,128)(2,1)S(1)} %bitcast.195), kind=kCustom, calls=%fused_computation.43 | custom fusion | bytes 3801090 | tf_op jit(solution)/shard_map/scatter | solution.py:31
  150.0 4.9 reshape.189
  154.9 5.9 copy.48
  167.3 13.0 %scatter_custom_fusion.1 = bf16[832,2048]{1,0:T(8,128)(2,1)} fusion(s32[768]{0:T(1024)S(1)} %fusion.76, f32[96,2048]{1,0:T(8,128)} %convert_bitcast_fusion, f32[768]{0:T(1024)S(1)} %div.39, bf16[]{:T(256)} %constant.9.clone.1), kind=kCustom, calls=%fused_computation.42 | custom fusion | flops 3145728 | bytes 4198402 | tf_op jit(solution)/shard_map/scatter | solution.py:31
  180.3 4.9 reshape.187
  185.1 6.1 copy.46
  191.3 48.9 %all-to-all-done.3 = bf16[4,8,26,2048]{3,1,2,0:T(8,128)(2,1)S(1)} async-done(((bf16[4,8,26,2048]{3,1,2,0:T(8,128)(2,1)}), bf16[4,8,26,2048]{3,1,2,0:T(8,128)(2,1)S(1)}, u32[]{:S(2)}, u32[]{:S(2)}) %all-to-all-start.3) | async-done | bytes 3407904 | tf_op jit(solution)/shard_map/all_to_all | solution.py:113
  240.2 4.7 all-to-all-start.2
  245.2 10.6 %fusion.5 = f32[8,4,26,384]{3,2,1,0:T(8,128)} fusion(bf16[1,8,2048,384]{3,2,1,0:T(8,128)(2,1)} %param.17, bf16[4,8,26,2048]{3,1,2,0:T(8,128)(2,1)S(1)} %all-to-all-done.3), kind=kOutput, calls=%fused_computation.13 | convolution fusion | flops 1308622848 | bytes 17268736 | tf_op jit(solution)/shard_map/semd,edf->semf/dot_general | solution.py:40
  255.8 10.6 %fusion.11 = f32[8,4,26,384]{3,2,1,0:T(8,128)} fusion(bf16[1,8,2048,384]{3,2,1,0:T(8,128)(2,1)} %param.18, bf16[4,8,26,2048]{3,1,2,0:T(8,128)(2,1)S(1)} %all-to-all-done.3), kind=kOutput, calls=%fused_computation.19 | convolution fusion | flops 1308622848 | bytes 17268736 | tf_op jit(solution)/shard_map/semd,edf->semf/dot_general | solution.py:41
  270.8 49.9 %all-to-all-done.2 = bf16[4,8,26,2048]{3,1,2,0:T(8,128)(2,1)} async-done(((bf16[4,8,26,2048]{3,1,2,0:T(8,128)(2,1)}), bf16[4,8,26,2048]{3,1,2,0:T(8,128)(2,1)}, u32[]{:S(2)}, u32[]{:S(2)}) %all-to-all-start.2) | async-done | bytes 3407904 | tf_op jit(solution)/shard_map/all_to_all | solution.py:114
  320.8 13.4 %fusion.53 = (bf16[4,8,26,384]{3,2,0,1:T(8,128)(2,1)}, bf16[4,8,26,384]{3,2,0,1:T(8,128)(2,1)}) fusion(f32[8,4,26,384]{3,2,1,0:T(8,128)} %fusion.5, f32[8,4,26,384]{3,2,1,0:T(8,128)} %fusion.11, bf16[1,8,384,2048]{3,2,1,0:T(8,128)(2,1)} %param.19, bf16[4,8,26,2048]{3,1,2,0:T(8,128)(2,1)} %all-to-all-done.2), kind=kOutput, calls=%fused_computation.66 | convolution fusion | flops 1312776192 | bytes 19824640 | tf_op jit(solution)/shard_map/semd,efd->semf/dot_general | solution.py:49
  334.1 12.2 %fusion.3 = f32[8,4,26,2048]{3,2,1,0:T(8,128)} fusion(bf16[4,8,26,384]{3,2,0,1:T(8,128)(2,1)} %get-tuple-element.6, bf16[1,8,2048,384]{3,2,1,0:T(8,128)(2,1)} %param.17), kind=kOutput, calls=%fused_computation.11 | convolution fusion | flops 1308622848 | bytes 20037632 | tf_op jit(solution)/shard_map/semf,edf->semd/dot_general | solution.py:60
  346.4 14.8 %add_bitcast_fusion = f32[4,8,26,2048]{3,2,0,1:T(8,128)} fusion(f32[8,4,26,2048]{3,2,1,0:T(8,128)} %fusion.3, bf16[4,8,26,384]{3,2,0,1:T(8,128)(2,1)} %get-tuple-element.5, bf16[1,8,2048,384]{3,2,1,0:T(8,128)(2,1)} %param.18), kind=kOutput, calls=%fused_computation.27 | convolution fusion | flops 1310326784 | bytes 26853376 | tf_op jit(solution)/shard_map/semf,edf->semd/dot_general | solution.py:62
  361.2 6.1 copy.39
  372.0 87.7 %reduce-scatter.5.cloned.1.call-done = f32[4,8,26,1024]{3,2,0,1:T(8,128)} async-done(((f32[4,8,26,2048]{3,2,0,1:T(8,128)}), f32[4,8,26,1024]{3,2,0,1:T(8,128)}) %reduce-scatter.5.cloned.1.call-update) | async-done | bytes 3407888 | tf_op jit(solution)/shard_map/reduce_scatter | solution.py:130
  463.6 56.9 %all-gather.5.cloned.1.call-done = bf16[4,8,26,2048]{3,2,0,1:T(8,128)(2,1)} async-done(((bf16[4,8,26,1024]{3,2,0,1:T(8,128)(2,1)}), bf16[4,8,26,2048]{3,2,0,1:T(8,128)(2,1)}) %all-gather.5.cloned.1.call-update) | async-done | bytes 3407888 | tf_op jit(solution)/shard_map/all_gather | solution.py:136
  520.5 5.9 copy.51
  526.4 4.8 all-to-all-start.4
  531.4 11.3 %fusion.1 = bf16[1,8,2048,384]{3,2,1,0:T(8,128)(2,1)} fusion(bf16[4,8,26,384]{3,2,0,1:T(8,128)(2,1)} %get-tuple-element.5, bf16[4,8,26,2048]{3,1,2,0:T(8,128)(2,1)S(1)} %all-to-all-done.3), kind=kOutput, calls=%fused_computation.9 | convolution fusion | flops 1314914304 | bytes 16629760 | tf_op jit(solution)/shard_map/semd,semf->edf/dot_general | solution.py:69
  542.8 13.1 %fusion.2 = bf16[1,8,384,2048]{3,2,1,0:T(8,128)(2,1)} fusion(bf16[4,8,26,2048]{3,1,2,0:T(8,128)(2,1)} %all-to-all-done.2, f32[8,4,26,384]{3,2,1,0:T(8,128)} %fusion.11, f32[8,4,26,384]{3,2,1,0:T(8,128)} %fusion.5), kind=kOutput, calls=%fused_computation.10 | convolution fusion | flops 1316831232 | bytes 18546688 | tf_op jit(solution)/shard_map/semf,semd->efd/dot_general | solution.py:70
  555.9 6.0 copy.40
  569.7 4.9 fusion.19
  575.5 32.4 %all-to-all-done.4 = bf16[4,8,26,2048]{3,1,2,0:T(8,128)(2,1)} async-done(((bf16[4,8,26,2048]{3,1,2,0:T(8,128)(2,1)}), bf16[4,8,26,2048]{3,1,2,0:T(8,128)(2,1)}, u32[]{:S(2)}, u32[]{:S(2)}) %all-to-all-start.4) | async-done | bytes 3407904 | tf_op jit(solution)/shard_map/all_to_all | solution.py:140
  607.9 6.0 copy.52
  626.2 13.0 %fusion = bf16[1,8,2048,384]{3,2,1,0:T(8,128)(2,1)} fusion(bf16[4,8,26,384]{3,2,0,1:T(8,128)(2,1)S(1)} %copy-done.3, bf16[4,8,26,2048]{3,1,2,0:T(8,128)(2,1)} %copy-done.2), kind=kOutput, calls=%fused_computation.8 | convolution fusion | flops 1314914304 | bytes 16629760 | tf_op jit(solution)/shard_map/semd,semf->edf/dot_general | solution.py:66
  (91 shorter events, 54.7 us)
Async XLA Ops:
  7.2 133.8 %copy-start = (bf16[1,96,2048]{2,1,0:T(8,128)(2,1)S(1)}, bf16[1,96,2048]{2,1,0:T(8,128)(2,1)}, u32[]{:S(2)}) copy-start(bf16[1,96,2048]{2,1,0:T(8,128)(2,1)} %param.13) | copy-start | bytes 1179652
  7.2 259.2 %reduce-scatter.3.cloned.1.call-start = ((), (), s32[]{:S(2)}) async-start(), calls=%async_computation.7 | async-start | bytes 12582912 | tf_op jit(solution)/shard_map/reduce_scatter | solution.py:129
  29.6 92.3 %slice-start = ((s8[12582912]{0:T(1024)(128)(4,1)}), s8[4194304]{0:T(1024)(128)(4,1)S(1)}, s32[]{:S(2)}) async-start(s8[12582912]{0:T(1024)(128)(4,1)} %bitcast.196), calls=%async_computation.11 | async-start | bytes 8388608
  112.2 9.6 %slice-start.1 = ((s8[12582912]{0:T(1024)(128)(4,1)}), s8[4194304]{0:T(1024)(128)(4,1)S(1)}, s32[]{:S(2)}) async-start(s8[12582912]{0:T(1024)(128)(4,1)} %bitcast.196), calls=%async_computation.12 | async-start | bytes 8388608
  112.2 9.7 %slice-start.2 = ((s8[12582912]{0:T(1024)(128)(4,1)}), s8[4194304]{0:T(1024)(128)(4,1)S(1)}, s32[]{:S(2)}) async-start(s8[12582912]{0:T(1024)(128)(4,1)} %bitcast.196), calls=%async_computation.13 | async-start | bytes 8388608
  137.6 0.7 copy-start.8
  160.8 4.1 copy-start.6
  160.8 79.4 %all-to-all-start.3 = ((bf16[4,8,26,2048]{3,1,2,0:T(8,128)(2,1)}), bf16[4,8,26,2048]{3,1,2,0:T(8,128)(2,1)S(1)}, u32[]{:S(2)}, u32[]{:S(2)}) async-start(bf16[4,8,26,2048]{3,1,2,0:T(8,128)(2,1)} %copy.48), calls=%async_computation.4 | async-start | bytes 6815744 | tf_op jit(solution)/shard_map/all_to_all | solution.py:113
  240.2 291.2 %copy-start.2 = (bf16[4,8,26,2048]{3,1,2,0:T(8,128)(2,1)}, bf16[4,8,26,2048]{3,1,2,0:T(8,128)(2,1)S(1)}, u32[]{:S(2)}) copy-start(bf16[4,8,26,2048]{3,1,2,0:T(8,128)(2,1)S(1)} %all-to-all-done.3) | copy-start | bytes 10223620
  240.2 80.6 %all-to-all-start.2 = ((bf16[4,8,26,2048]{3,1,2,0:T(8,128)(2,1)}), bf16[4,8,26,2048]{3,1,2,0:T(8,128)(2,1)}, u32[]{:S(2)}, u32[]{:S(2)}) async-start(bf16[4,8,26,2048]{3,1,2,0:T(8,128)(2,1)} %copy.46), calls=%async_computation.3 | async-start | bytes 6815744 | tf_op jit(solution)/shard_map/all_to_all | solution.py:114
  244.9 116.3 %all-gather.3.cloned.1.call-start = ((), (), s32[]{:S(2)}) async-start(), calls=%async_computation.8 | async-start | bytes 6291456 | tf_op jit(solution)/shard_map/all_gather | solution.py:135
  270.3 189.5 %reduce-scatter.5.cloned.1.call-start = ((), (), s32[]{:S(2)}) async-start(), calls=%async_computation.9 | async-start | bytes 12582912 | tf_op jit(solution)/shard_map/reduce_scatter | solution.py:130
  367.3 159.1 %all-to-all-start.1 = ((bf16[4,8,26,2048]{3,1,2,0:T(8,128)(2,1)}), bf16[4,8,26,2048]{3,1,2,0:T(8,128)(2,1)}, u32[]{:S(2)}, u32[]{:S(2)}) async-start(bf16[4,8,26,2048]{3,1,2,0:T(8,128)(2,1)} %copy.39), calls=%async_computation.2 | async-start | bytes 6815744 | tf_op jit(solution)/shard_map/all_to_all | solution.py:139
  372.0 148.5 %all-gather.5.cloned.1.call-start = ((), (), s32[]{:S(2)}) async-start(), calls=%async_computation.10 | async-start | bytes 6291456 | tf_op jit(solution)/shard_map/all_gather | solution.py:136
  526.4 4.8 copy-start.7
  526.4 81.5 %all-to-all-start.4 = ((bf16[4,8,26,2048]{3,1,2,0:T(8,128)(2,1)}), bf16[4,8,26,2048]{3,1,2,0:T(8,128)(2,1)}, u32[]{:S(2)}, u32[]{:S(2)}) async-start(bf16[4,8,26,2048]{3,1,2,0:T(8,128)(2,1)} %copy.51), calls=%async_computation.6 | async-start | bytes 6815744 | tf_op jit(solution)/shard_map/all_to_all | solution.py:140
  569.7 5.0 copy-start.4
  575.5 63.7 %collective-permute-start = (bf16[1,96,2048]{2,1,0:T(8,128)(2,1)}, bf16[1,96,2048]{2,1,0:T(8,128)(2,1)}, u32[]{:S(2)}, u32[]{:S(2)}) collective-permute-start(bf16[1,96,2048]{2,1,0:T(8,128)(2,1)} %fusion.66), channel_id=1, source_target_pairs={{24,0},{0,8},{8,16},{16,24},{25,1},{1,9},{9,17},{17,25},{26,2},{2,... | collective-permute-start | bytes 1179656 | tf_op jit(solution)/shard_map/ppermute | solution.py:13
  621.5 4.1 copy-start.5
  621.5 4.7 copy-start.3
  625.7 13.4 %collective-permute-start.1 = (bf16[1,96,2048]{2,1,0:T(8,128)(2,1)S(1)}, bf16[1,96,2048]{2,1,0:T(8,128)(2,1)S(1)}, u32[]{:S(2)}, u32[]{:S(2)}) collective-permute-start(bf16[1,96,2048]{2,1,0:T(8,128)(2,1)S(1)} %fusion.64), channel_id=1, source_target_pairs={{8,0},{16,8},{24,16},{0,24},{9,1},{17,9},{25,17},{1,25},{10,2},{18... | collective-permute-start | bytes 1179656 | tf_op jit(solution)/shard_map/ppermute | solution.py:13
  626.2 15.5 %copy-start.1 = (bf16[1,96,2048]{2,1,0:T(8,128)(2,1)S(1)}, bf16[1,96,2048]{2,1,0:T(8,128)(2,1)}, u32[]{:S(2)}) copy-start(bf16[1,96,2048]{2,1,0:T(8,128)(2,1)} %param.13) | copy-start | bytes 1179652
Sparse Core Ops, SparseCore 0:
  137.8 98.5 reduce-scatter.2
  270.4 58.2 all-gather.2
  361.3 98.4 reduce-scatter.4
  463.8 56.7 all-gather.4
where the time goes:
time: 656 us; the launch traced here: 649 us
  waiting for transfers between devices  276 us (42%)
  matrix products  124 us (19%)
  local copies, waits for them, and re-layouts  94.2 us (14%)
  blocking collectives  82.7 us (13%)
  other arithmetic  37.2 us (6%)
  starting transfers between devices  19.7 us (3%)
  between operations  14.6 us (2%)
    reduce_scatter x1, waiting for transfers between devices, local(): lax.psum_scatter(grad_term, 'dp', scatter_dimension=3, tiled=True)  87.7 us
    all_to_all x1, blocking collectives, local(): lax.all_to_all(send_inputs, 'expert', split_axis=0, concat_axis=0, tiled=...  82.7 us
    all_gather x1, waiting for transfers between devices, local(): lax.all_gather(grad_part, 'dp', axis=3, tiled=True)  56.9 us
    all_to_all x1, waiting for transfers between devices, local(): lax.all_to_all(send_grad, 'expert', split_axis=0, concat_axis=0, tiled=True)  49.9 us
    all_to_all x1, waiting for transfers between devices, local(): lax.all_to_all(send_saved, 'expert', split_axis=0, concat_axis=0, tiled=T...  48.9 us
    all_to_all x1, waiting for transfers between devices, local(): lax.all_to_all(row_grad, 'expert', split_axis=0, concat_axis=0, tiled=True)  32.4 us
    reshape x6, local copies, waits for them, and re-layouts, packed_rows(): return filled.reshape(groups, EXPERTS // groups, MOST, rows.shape[-1])  30.7 us
    dot_general x2, matrix products, project(): jnp.einsum('semd,edf->semf', rows, gate_weight, preferred_element_type=jn...  20.3 us
  transfers between devices with their start and end apart: 10, of which 5 were waited for; matrix products, arithmetic and copies ran while one was open for 32% of the time, Pallas kernels for 0%

commit v1 on v0

v1 whole, which is shorter than its diff:
```python
import functools

import jax
import jax.numpy as jnp
from jax import lax
from jax.experimental import pallas as pl
from jax.experimental.pallas import tpu as pltpu
from jax.sharding import PartitionSpec as P

EXPERTS = 32
MOST = 26
ROTATED = 8
BF16 = jnp.bfloat16
F32 = jnp.float32
MIB = 1 << 20

NN = (((1,), (0,)), ((), ()))
NT = (((1,), (1,)), ((), ()))
TN = (((0,), (0,)), ((), ()))


def dot(a, b, dims=NN):
    return lax.dot_general(a, b, dims, preferred_element_type=F32)


def rotate(block, axis, distance):
    n = lax.axis_size(axis)
    return lax.ppermute(block, axis, [(i, (i + distance) % n) for i in range(n)])


def params(mib=40):
    return pltpu.CompilerParams(vmem_limit_bytes=mib * MIB)


def cost(flops, nbytes):
    return pl.CostEstimate(flops=int(flops), bytes_accessed=int(nbytes), transcendentals=0)


def fill_onehot(dest_ref, onehot_ref, slots):
    local, tokens = dest_ref.shape
    place = lax.broadcasted_iota(jnp.int32, (slots, tokens), 0)
    for l in range(local):
        onehot_ref[l * slots : (l + 1) * slots, :] = (
            jnp.where(place == dest_ref[l : l + 1, :], 1.0, 0.0).astype(BF16)
        )


def stack_pieces(pieces, rows_ref):
    at = 0
    for piece in pieces:
        rows_ref[at : at + piece.shape[0], :] = piece[...]
        at += piece.shape[0]


def order_kernel(n_pieces, n_arrays, slots, *refs):
    dest_ref, weight_ref = refs[:2]
    pieces = refs[2 : 2 + n_pieces * n_arrays]
    outs = refs[2 + n_pieces * n_arrays : 2 + n_pieces * n_arrays + n_arrays]
    onehot_ref, rows_ref, slot_weight_ref = refs[2 + n_pieces * n_arrays + n_arrays :]
    local, tokens = dest_ref.shape

    @pl.when(pl.program_id(0) == 0)
    def _():
        fill_onehot(dest_ref, onehot_ref, slots)
        if n_arrays > 1:
            for l in range(local):
                part = slice(l * slots, (l + 1) * slots)
                slot_weight_ref[part, :] = jnp.sum(
                    onehot_ref[part, :].astype(F32) * weight_ref[l : l + 1, :], 1, keepdims=True
                )

    for a in range(n_arrays):
        stack_pieces(pieces[a * n_pieces : (a + 1) * n_pieces], rows_ref)
        ordered = dot(onehot_ref[...], rows_ref[...])
        if a == 1:
            ordered = ordered * slot_weight_ref[...]
        outs[a][...] = ordered.astype(BF16)


def in_expert_order(dest, weight, arrays, slots):
    local, tokens = dest.shape
    width = arrays[0][0].shape[1]
    chunk = min(512, width)
    n_pieces, n_arrays = len(arrays[0]), len(arrays)
    whole = pl.BlockSpec((local, tokens), lambda c: (0, 0))
    flat = [piece for pieces in arrays for piece in pieces]
    total = local * slots
    return pl.pallas_call(
        functools.partial(order_kernel, n_pieces, n_arrays, slots),
        grid=(width // chunk,),
        in_specs=[whole, whole]
        + [pl.BlockSpec((piece.shape[0], chunk), lambda c: (0, c)) for piece in flat],
        out_specs=[pl.BlockSpec((total, chunk), lambda c: (0, c))] * n_arrays,
        out_shape=[jax.ShapeDtypeStruct((total, width), BF16)] * n_arrays,
        scratch_shapes=[
            pltpu.VMEM((total, tokens), BF16),
            pltpu.VMEM((tokens, chunk), BF16),
            pltpu.VMEM((total, 1), F32),
        ],
        compiler_params=params(),
        cost_estimate=cost(
            2 * total * tokens * width * n_arrays, 2 * (total + tokens) * width * n_arrays
        ),
        name="order_rows",
    )(dest, weight, *flat)


def combine_kernel(weighted, slots, dest_ref, weight_ref, rows_ref, keep_ref, send_ref, mix_ref):
    tokens, local = dest_ref.shape
    total = rows_ref.shape[0]

    @pl.when(pl.program_id(0) == 0)
    def _():
        slot = lax.broadcasted_iota(jnp.int32, (tokens, total), 1)
        mix = jnp.zeros((tokens, total), F32)
        for l in range(local):
            here = dest_ref[:, l : l + 1]
            here = jnp.where(here >= 0, here + l * slots, -1)
            value = weight_ref[:, l : l + 1] if weighted else 1.0
            mix = jnp.where(slot == here, value, mix)
        mix_ref[...] = mix.astype(BF16)

    half = tokens // 2
    summed = dot(mix_ref[...], rows_ref[...]).astype(BF16)
    keep_ref[...] = summed[:half]
    send_ref[...] = summed[half:]


def token_sums(dest, weight, rows, slots, weighted, part, parts):
    tokens, local = dest.shape
    total, width = rows.shape
    width = width // parts
    chunk = min(512, width)
    steps = width // chunk
    whole = pl.BlockSpec((tokens, local), lambda c: (0, 0))
    return pl.pallas_call(
        functools.partial(combine_kernel, weighted, slots),
        grid=(steps,),
        in_specs=[
            whole,
            whole,
            pl.BlockSpec((total, chunk), lambda c: (0, c + part * steps)),
        ],
        out_specs=[pl.BlockSpec((tokens // 2, chunk), lambda c: (0, c))] * 2,
        out_shape=[jax.ShapeDtypeStruct((tokens // 2, width), BF16)] * 2,
        scratch_shapes=[pltpu.VMEM((tokens, total), BF16)],
        compiler_params=params(),
        cost_estimate=cost(2 * total * tokens * width, 2 * (total + tokens) * width),
        name="token_sums",
    )(dest, weight, rows)


def forward_kernel(rows_ref, gate_ref, up_ref, down_ref, out_ref):
    rows = rows_ref[...]
    gate_value = dot(rows, gate_ref[0])
    up_value = dot(rows, up_ref[0])
    hidden = (gate_value / (1.0 + jnp.exp(-gate_value)) * up_value).astype(BF16)
    out_ref[...] = dot(hidden, down_ref[0]).astype(BF16)


def backward_kernel(
    rows_ref, grad_ref, gate_ref, up_ref, down_ref, hidden_ref, gate_grad_ref, up_grad_ref, out_ref
):
    rows = rows_ref[...]
    gate_value = dot(rows, gate_ref[0])
    up_value = dot(rows, up_ref[0])
    hidden_grad = dot(grad_ref[...], down_ref[0], NT)
    sig = 1.0 / (1.0 + jnp.exp(-gate_value))
    silu = gate_value * sig
    hidden_ref[...] = (silu * up_value).astype(BF16)
    up_grad = (hidden_grad * silu).astype(BF16)
    gate_grad = (hidden_grad * up_value * sig * (1.0 + gate_value * (1.0 - sig))).astype(BF16)
    up_grad_ref[...] = up_grad
    gate_grad_ref[...] = gate_grad
    out_ref[...] = (dot(gate_grad, gate_ref[0], NT) + dot(up_grad, up_ref[0], NT)).astype(BF16)


def weights_kernel(
    rows_ref, grad_ref, hidden_ref, gate_grad_ref, up_grad_ref, gate_ref, up_ref, down_ref
):
    rows = rows_ref[...]
    gate_ref[0] = dot(rows, gate_grad_ref[...], TN).astype(BF16)
    up_ref[0] = dot(rows, up_grad_ref[...], TN).astype(BF16)
    down_ref[0] = dot(hidden_ref[...], grad_ref[...], TN).astype(BF16)


def expert_specs(local, slots, width, hidden):
    wide = pl.BlockSpec((slots, width), lambda e: (e, 0))
    narrow = pl.BlockSpec((slots, hidden), lambda e: (e, 0))
    column = pl.BlockSpec((1, width, hidden), lambda e: (e, 0, 0))
    row = pl.BlockSpec((1, hidden, width), lambda e: (e, 0, 0))
    return wide, narrow, column, row


def forward_experts(rows, gate, up, down):
    local, width, hidden = gate.shape
    slots = rows.shape[0] // local
    wide, narrow, column, row = expert_specs(local, slots, width, hidden)
    return pl.pallas_call(
        forward_kernel,
        grid=(local,),
        in_specs=[wide, column, column, row],
        out_specs=wide,
        out_shape=jax.ShapeDtypeStruct(rows.shape, BF16),
        compiler_params=params(),
        cost_estimate=cost(6 * rows.shape[0] * width * hidden, 6 * local * width * hidden),
        name="forward_experts",
    )(rows, gate, up, down)


def backward_experts(rows, grads, gate, up, down):
    local, width, hidden = gate.shape
    slots = rows.shape[0] // local
    wide, narrow, column, row = expert_specs(local, slots, width, hidden)
    small = jax.ShapeDtypeStruct((rows.shape[0], hidden), BF16)
    return pl.pallas_call(
        backward_kernel,
        grid=(local,),
        in_specs=[wide, wide, column, column, row],
        out_specs=[narrow, narrow, narrow, wide],
        out_shape=[small, small, small, jax.ShapeDtypeStruct(rows.shape, BF16)],
        compiler_params=params(),
        cost_estimate=cost(10 * rows.shape[0] * width * hidden, 6 * local * width * hidden),
        name="backward_experts",
    )(rows, grads, gate, up, down)


def weight_grads(rows, grads, hidden_rows, gate_grad, up_grad, local):
    width, hidden = rows.shape[1], gate_grad.shape[1]
    slots = rows.shape[0] // local
    wide, narrow, column, row = expert_specs(local, slots, width, hidden)
    return pl.pallas_call(
        weights_kernel,
        grid=(local,),
        in_specs=[wide, wide, narrow, narrow, narrow],
        out_specs=[column, column, row],
        out_shape=[
            jax.ShapeDtypeStruct((local, width, hidden), BF16),
            jax.ShapeDtypeStruct((local, width, hidden), BF16),
            jax.ShapeDtypeStruct((local, hidden, width), BF16),
        ],
        compiler_params=params(),
        cost_estimate=cost(6 * rows.shape[0] * width * hidden, 6 * local * width * hidden),
        name="weight_grads",
    )(rows, grads, hidden_rows, gate_grad, up_grad)


def halves(block, dp_index):
    half = block.shape[0] // 2
    mine = lax.dynamic_slice_in_dim(block, dp_index * half, half, 0)
    other = lax.dynamic_slice_in_dim(block, (1 - dp_index) * half, half, 0)
    return mine, other


def spread(mine, other, groups):
    if groups > ROTATED:
        near = lax.all_gather(mine, "expert", tiled=True)
        return [near, rotate(near, "dp", 1)]
    near = [rotate(mine, "expert", r) for r in range(1, groups)]
    far = [rotate(piece, "dp", 1) for piece in near]
    return [mine] + near + [other] + far


def spread_meta(meta, dp_index, groups):
    half = meta.shape[0] // 2
    both = jnp.concatenate(halves(meta, dp_index), 0)
    if groups > ROTATED:
        metas = list(lax.all_gather(both, "expert"))
    else:
        metas = [both] + [rotate(both, "expert", r) for r in range(1, groups)]
    return jnp.concatenate([m[:half] for m in metas] + [m[half:] for m in metas], 0)


def sums_home(keep, send, groups):
    half = keep.shape[0] // groups
    pair = (keep.astype(F32) + rotate(send, "dp", 1).astype(F32)).astype(BF16)
    pair = pair.reshape(groups, half, -1)
    if groups > ROTATED:
        return jnp.sum(lax.all_to_all(pair, "expert", 0, 0, tiled=True).astype(F32), 0)
    total = pair[0].astype(F32)
    for r in range(1, groups):
        total = total + rotate(pair[r], "expert", -r).astype(F32)
    return total


def to_section(mine, direction, dp_index):
    n, m = lax.axis_size("section"), lax.axis_size("dp")
    same = rotate(mine, "section", direction)
    route = [
        (s * m + d, ((s + direction) % n) * m + (m - 1 - d)) for s in range(n) for d in range(m)
    ]
    cross = lax.ppermute(mine, ("section", "dp"), route)
    first = jnp.where(dp_index == 0, same, cross)
    second = jnp.where(dp_index == 0, cross, same)
    return jnp.concatenate([first, second], 0)


def slot_tables(meta, choices, base, local):
    tokens = meta.shape[0]
    meta = meta.reshape(tokens, 2, 2, choices)
    routes, counted = meta[:, :, 0], meta[:, :, 1].astype(F32)
    mixing = counted / jnp.sum(counted, -1, keepdims=True)
    hit = (routes[..., None] - base) == jnp.arange(local, dtype=jnp.int32)
    weight = jnp.sum(jnp.where(hit, mixing[..., None], 0.0), 2)
    chosen = jnp.any(hit, 2).astype(jnp.int32)
    rank = jnp.cumsum(chosen, 0) - chosen
    return jnp.where(chosen > 0, rank, -1), weight


def local(
    fwd_in, fwd_routes, fwd_numer, bwd_saved, bwd_routes, bwd_numer, bwd_grad, w_gate, w_up, w_down
):
    groups = lax.axis_size("expert")
    group, dp_index = lax.axis_index("expert"), lax.axis_index("dp")
    gate, up, down = w_gate[0], w_up[0], w_down[0]
    n_local = gate.shape[0]
    choices = fwd_routes.shape[-1]
    slots = -(-groups * MOST // 16) * 16

    meta = jnp.concatenate([fwd_routes[0], fwd_numer[0], bwd_routes[0], bwd_numer[0]], -1)
    meta_all = spread_meta(meta, dp_index, groups)
    dest, weight = slot_tables(meta_all, choices, group * n_local, n_local)
    fwd_dest, back_dest = dest[:, 0], dest[:, 1]
    fwd_weight, back_weight = weight[:, 0], weight[:, 1]

    saved_mine, saved_other = halves(bwd_saved[0], dp_index)
    grad_mine, grad_other = halves(bwd_grad[0], dp_index)
    in_mine, in_other = halves(fwd_in[0], dp_index)
    saved = spread(saved_mine, saved_other, groups)
    grads = spread(grad_mine, grad_other, groups)
    inputs = spread(in_mine, in_other, groups)

    saved_rows, grad_rows = in_expert_order(back_dest.T, back_weight.T, [saved, grads], slots)
    hidden, gate_grad, up_grad, row_grad = backward_experts(saved_rows, grad_rows, gate, up, down)
    (in_rows,) = in_expert_order(fwd_dest.T, fwd_weight.T, [inputs], slots)
    out_rows = forward_experts(in_rows, gate, up, down)

    parts = 2

    def returned(dest, weight, rows, weighted):
        return jnp.concatenate(
            [
                sums_home(*token_sums(dest, weight, rows, slots, weighted, part, parts), groups)
                for part in range(parts)
            ],
            1,
        )

    back_sum = returned(back_dest, back_weight, row_grad, False)
    out_sum = returned(fwd_dest, fwd_weight, out_rows, True)
    input_grad = (grad_mine.astype(F32) + back_sum).astype(BF16)
    layer_out = (in_mine.astype(F32) + out_sum).astype(BF16)
    next_bwd = to_section(input_grad, -1, dp_index)
    next_fwd = to_section(layer_out, 1, dp_index)

    gate_sum, up_sum, down_sum = weight_grads(
        saved_rows, grad_rows, hidden, gate_grad, up_grad, n_local
    )
    return (next_fwd[None], next_bwd[None], gate_sum[None], up_sum[None], down_sum[None])


def solution(mesh):
    in_specs = (
        P("section", "expert", None),
        P("section", "expert", None),
        P("section", "expert", None),
        P("section", "expert", None),
        P("section", "expert", None),
        P("section", "expert", None),
        P("section", "expert", None),
        P("section", "expert", None, "dp"),
        P("section", "expert", None, "dp"),
        P("section", "expert", "dp", None),
    )
    out_specs = (
        P("section", "expert", None),
        P("section", "expert", None),
        P("section", "expert", None, "dp"),
        P("section", "expert", None, "dp"),
        P("section", "expert", "dp", None),
    )
    return jax.shard_map(local, mesh=mesh, in_specs=in_specs, out_specs=out_specs, check_vma=False)
```

time: 656 us -> 180 us (0.27); the launches traced: 649 us -> 179 us
  waiting for transfers between devices: 276 us -> 42.9 us
  matrix products: 124 us -> 0 us
  local copies, waits for them, and re-layouts: 94.2 us -> 7.49 us
  blocking collectives: 82.7 us -> 0 us
  Pallas kernels: 0 us -> 73.5 us
  other arithmetic: 37.2 us -> 5.21 us
  starting transfers between devices: 19.7 us -> 49.2 us
  between operations: 14.6 us -> 1.09 us
    all_to_all x4 -> x0, waiting for transfers between devices: 131 us -> none  [the longest x1 49.9 us: local(): lax.all_to_all(send_grad, 'expert', split_axis=0, concat_axis=0, tiled=True)]
    dot_general x11 -> x0, matrix products: 124 us -> none  [the longest x2 20.3 us: project(): jnp.einsum('semd,edf->semf', rows, gate_weight, preferred_element_type=jn...]
    reduce_scatter x2 -> x0, waiting for transfers between devices: 87.7 us -> none  [the longest x1 87.7 us: local(): lax.psum_scatter(grad_term, 'dp', scatter_dimension=3, tiled=True)]
    all_to_all x1 -> x0, blocking collectives: 82.7 us -> none  [local(): lax.all_to_all(send_inputs, 'expert', split_axis=0, concat_axis=0, tiled=...]
    pallas_call x0 -> x9, Pallas kernels: none -> 73.5 us  [the longest x1 20.8 us: backward_experts(): pl.pallas_call(backward_kernel, grid=(local,), in_specs=[wide, wide, colu...]
    all_gather x2 -> x0, waiting for transfers between devices: 56.9 us -> none  [the longest x1 56.9 us: local(): lax.all_gather(grad_part, 'dp', axis=3, tiled=True)]
    ppermute x2 -> x41, starting transfers between devices: 0.47 us -> 49.2 us  [the longest x39 49.1 us: rotate(): lax.ppermute(block, axis, [(i, (i + distance) % n) for i in range(n)])]
    ppermute x2 -> x41, waiting for transfers between devices: 0.01 us -> 42.9 us  [the longest x39 42.9 us: rotate(): lax.ppermute(block, axis, [(i, (i + distance) % n) for i in range(n)])]
  transfers between devices with their start and end apart: 10 -> 41, of which waited for: 5 -> 10; matrix products, arithmetic and copies ran while one was open for 32% -> 6% of each run, Pallas kernels for 0% -> 41%
where the time goes in v1:
time: 180 us; the launch traced here: 179 us
  Pallas kernels  73.5 us (41%)
  starting transfers between devices  49.2 us (27%)
  waiting for transfers between devices  42.9 us (24%)
  local copies, waits for them, and re-layouts  7.49 us (4%)
  other arithmetic  5.21 us (3%)
    ppermute x39, starting transfers between devices, rotate(): lax.ppermute(block, axis, [(i, (i + distance) % n) for i in range(n)])  49.1 us
    ppermute x39, waiting for transfers between devices, rotate(): lax.ppermute(block, axis, [(i, (i + distance) % n) for i in range(n)])  42.9 us
    pallas_call x1, Pallas kernels, backward_experts(): pl.pallas_call(backward_kernel, grid=(local,), in_specs=[wide, wide, colu...  20.8 us
    pallas_call x1, Pallas kernels, forward_experts(): pl.pallas_call(forward_kernel, grid=(local,), in_specs=[wide, column, col...  15.6 us
    pallas_call x1, Pallas kernels, weight_grads(): pl.pallas_call(weights_kernel, grid=(local,), in_specs=[wide, wide, narro...  14 us
    pallas_call x4, Pallas kernels, token_sums(): pl.pallas_call(functools.partial(combine_kernel, weighted, slots), grid=(...  13.3 us
    pallas_call x2, Pallas kernels, in_expert_order(): pl.pallas_call(functools.partial(order_kernel, n_pieces, n_arrays, slots)...  9.81 us
  transfers between devices with their start and end apart: 41, of which 10 were waited for; matrix products, arithmetic and copies ran while one was open for 6% of the time, Pallas kernels for 41%

profile of v1, /device:TPU:0, one launch (start us, length us, event | category | flops | bytes accessed | tf_op | source)
XLA Modules:
  0.0 179.4 jit_solution(4277436648968299858)
XLA Ops:
  1.5 5.1 %collective-permute-start.2 = (s32[96,32]{0,1:T(8,128)S(1)}, s32[96,32]{0,1:T(8,128)S(1)}, u32[]{:S(2)}, u32[]{:S(2)}) collective-permute-start(s32[96,32]{0,1:T(8,128)S(1)} %pad_add_fusion.1), channel_id=1, source_target_pairs={{0,6},{2,0},{4,2},{6,4},{1,7},{3,1},{5,3},{7,5},{8,14},{10,8},{12,... | collective-permute-start | bytes 36872 | tf_op jit(solution)/shard_map/ppermute | solution.py:28
  8.7 2.9 %collective-permute-start.5 = (bf16[48,2048]{1,0:T(8,128)(2,1)S(1)}, bf16[48,2048]{1,0:T(8,128)(2,1)S(1)}, u32[]{:S(2)}, u32[]{:S(2)}) collective-permute-start(bf16[48,2048]{1,0:T(8,128)(2,1)S(1)} %get-tuple-element.64.refs_2_), channel_id=1, source_target_pairs={{0,6},{2,0},{4,2},{6,4},{1,7},{3,1},{5,3},{7,5},{8,14},{10,8},{12,... | collective-permute-start | bytes 589832 | tf_op jit(solution)/shard_map/ppermute | solution.py:28
  14.9 3.8 %collective-permute-start.21 = (bf16[48,2048]{1,0:T(8,128)(2,1)S(1)}, bf16[48,2048]{1,0:T(8,128)(2,1)S(1)}, u32[]{:S(2)}, u32[]{:S(2)}) collective-permute-start(bf16[48,2048]{1,0:T(8,128)(2,1)S(1)} %get-tuple-element.50.refs_2_), channel_id=1, source_target_pairs={{0,6},{2,0},{4,2},{6,4},{1,7},{3,1},{5,3},{7,5},{8,14},{10,8},{12,... | collective-permute-start | bytes 589832 | tf_op jit(solution)/shard_map/ppermute | solution.py:28
  19.5 1.7 reduce-window.6
  21.8 1.6 collective-permute-start.8
  23.4 14.1 %collective-permute-done.4.refs_4_ = bf16[48,2048]{1,0:T(8,128)(2,1)S(1)} collective-permute-done((bf16[48,2048]{1,0:T(8,128)(2,1)S(1)}, bf16[48,2048]{1,0:T(8,128)(2,1)S(1)}, u32[]{:S(2)}, u32[]{:S(2)}) %collective-permute-start.4) | collective-permute-done | bytes 196640 | tf_op jit(solution)/shard_map/ppermute | solution.py:28
  40.3 2.0 %collective-permute-start.19 = (bf16[48,2048]{1,0:T(8,128)(2,1)S(1)}, bf16[48,2048]{1,0:T(8,128)(2,1)}, u32[]{:S(2)}, u32[]{:S(2)}) collective-permute-start(bf16[48,2048]{1,0:T(8,128)(2,1)S(1)} %get-tuple-element.50.refs_2_), channel_id=1, source_target_pairs={{0,2},{2,4},{4,6},{6,0},{1,3},{3,5},{5,7},{7,1},{8,10},{10,12},{12... | collective-permute-start | bytes 589832 | tf_op jit(solution)/shard_map/ppermute | solution.py:28
  42.2 2.8 %collective-permute-done.20.refs_4_ = bf16[48,2048]{1,0:T(8,128)(2,1)S(1)} collective-permute-done((bf16[48,2048]{1,0:T(8,128)(2,1)S(1)}, bf16[48,2048]{1,0:T(8,128)(2,1)S(1)}, u32[]{:S(2)}, u32[]{:S(2)}) %collective-permute-start.20) | collective-permute-done | bytes 196640 | tf_op jit(solution)/shard_map/ppermute | solution.py:28
  45.2 2.2 %collective-permute-start.25 = (bf16[48,2048]{1,0:T(8,128)(2,1)S(1)}, bf16[48,2048]{1,0:T(8,128)(2,1)}, u32[]{:S(2)}, u32[]{:S(2)}) collective-permute-start(bf16[48,2048]{1,0:T(8,128)(2,1)S(1)} %get-tuple-element.48.refs_10_), channel_id=1, source_target_pairs={{0,2},{2,4},{4,6},{6,0},{1,3},{3,5},{5,7},{7,1},{8,10},{10,12},{12... | collective-permute-start | bytes 589832 | tf_op jit(solution)/shard_map/ppermute | solution.py:28
  47.4 1.5 collective-permute-start.24
  51.2 3.2 %order_rows.2.rows_ref = bf16[896,2048]{1,0:T(8,128)(2,1)S(1)} custom-call(s32[8,384]{1,0:T(8,128)S(1)} %copy.37.refs_0_, f32[8,384]{1,0:T(8,128)S(1)} %get-tuple-element.66.refs_1_, bf16[48,2048]{1,0:T(8,128)(2,1)S(1)} %get-tuple-element.64.refs_2_, bf16[48,2048]{1,0:T(8,128)(2,1)S(1)} %collective-permute-done.3.refs_3_, ...), custom_call_target="tpu_custom_call" | custom-call | flops 1409286144 | bytes 5242880 | tf_op jit(solution)/shard_map/order_rows/pallas_call | solution.py:88
  55.0 1.6 collective-permute-start.22
  56.5 6.5 %collective-permute-done.26.refs_12_ = bf16[48,2048]{1,0:T(8,128)(2,1)} collective-permute-done((bf16[48,2048]{1,0:T(8,128)(2,1)S(1)}, bf16[48,2048]{1,0:T(8,128)(2,1)}, u32[]{:S(2)}, u32[]{:S(2)}) %collective-permute-start.26) | collective-permute-done | bytes 196640 | tf_op jit(solution)/shard_map/ppermute | solution.py:28
  66.5 15.6 %forward_experts.1.rows_ref = bf16[896,2048]{1,0:T(8,128)(2,1)S(1)} custom-call(bf16[896,2048]{1,0:T(8,128)(2,1)S(1)} %order_rows.2.rows_ref, bf16[8,2048,384]{2,1,0:T(8,128)(2,1)} %bitcast.79, bf16[8,2048,384]{2,1,0:T(8,128)(2,1)} %bitcast.81, bf16[8,384,2048]{2,1,0:T(8,128)(2,1)} %bitcast.83), custom_call_target="tpu_custom_call" | custom-call | flops 4227858432 | bytes 37748736 | tf_op jit(solution)/shard_map/forward_experts/pallas_call | solution.py:199
  82.1 3.7 %token_sums.5 = (bf16[192,1024]{1,0:T(8,128)(2,1)S(1)}, bf16[192,1024]{1,0:T(8,128)(2,1)S(1)}) custom-call(s32[384,8]{1,0:T(8,128)S(1)} %get-tuple-element.54.dest_ref, f32[384,8]{1,0:T(8,128)S(1)} %bitcast.77, bf16[896,2048]{1,0:T(8,128)(2,1)S(1)} %forward_experts.1.rows_ref), custom_call_target="tpu_custom_call" | custom-call | flops 704643072 | bytes 2621440 | tf_op jit(solution)/shard_map/token_sums/pallas_call | solution.py:136
  85.8 3.6 %token_sums.4 = (bf16[192,1024]{1,0:T(8,128)(2,1)S(1)}, bf16[192,1024]{1,0:T(8,128)(2,1)S(1)}) custom-call(s32[384,8]{1,0:T(8,128)S(1)} %get-tuple-element.54.dest_ref, f32[384,8]{1,0:T(8,128)S(1)} %bitcast.78, bf16[896,2048]{1,0:T(8,128)(2,1)S(1)} %forward_experts.1.rows_ref), custom_call_target="tpu_custom_call" | custom-call | flops 704643072 | bytes 2621440 | tf_op jit(solution)/shard_map/token_sums/pallas_call | solution.py:136
  91.6 6.6 %order_rows.3 = (bf16[896,2048]{1,0:T(8,128)(2,1)S(1)}, bf16[896,2048]{1,0:T(8,128)(2,1)S(1)}) custom-call(s32[8,384]{1,0:T(8,128)S(1)} %copy.40.refs_0_, f32[8,384]{1,0:T(8,128)S(1)} %get-tuple-element.65.refs_1_, bf16[48,2048]{1,0:T(8,128)(2,1)S(1)} %get-tuple-element.50.refs_2_, bf16[48,2048]{1,0:T(8,128)(2,1)} %collective-permute-done.19.refs_3_, ...), custom_call_target="tpu_custom_call" | custom-call | flops 2818572288 | bytes 10485760 | tf_op jit(solution)/shard_map/order_rows/pallas_call | solution.py:88
  98.2 20.8 %backward_experts.1 = (bf16[896,384]{1,0:T(8,128)(2,1)S(1)}, bf16[896,384]{1,0:T(8,128)(2,1)S(1)}, bf16[896,384]{1,0:T(8,128)(2,1)S(1)}, bf16[896,2048]{1,0:T(8,128)(2,1)S(1)}) custom-call(bf16[896,2048]{1,0:T(8,128)(2,1)S(1)} %get-tuple-element.26.rows_ref, bf16[896,2048]{1,0:T(8,128)(2,1)S(1)} %get-tuple-element.27.grad_ref, ...), custom_call_target="tpu_custom_call" | custom-call | flops 7046430720 | bytes 37748736 | tf_op jit(solution)/shard_map/backward_experts/pallas_call | solution.py:216
  119.0 3.1 %token_sums.7 = (bf16[192,1024]{1,0:T(8,128)(2,1)S(1)}, bf16[192,1024]{1,0:T(8,128)(2,1)S(1)}) custom-call(s32[384,8]{1,0:T(8,128)S(1)} %get-tuple-element.53.dest_ref, f32[384,8]{1,0:T(8,128)S(1)} %bitcast.75, bf16[896,2048]{1,0:T(8,128)(2,1)S(1)} %get-tuple-element.28.rows_ref), custom_call_target="tpu_custom_call" | custom-call | flops 704643072 | bytes 2621440 | tf_op jit(solution)/shard_map/token_sums/pallas_call | solution.py:136
  122.7 2.9 %token_sums.6 = (bf16[192,1024]{1,0:T(8,128)(2,1)S(1)}, bf16[192,1024]{1,0:T(8,128)(2,1)S(1)}) custom-call(s32[384,8]{1,0:T(8,128)S(1)} %get-tuple-element.53.dest_ref, f32[384,8]{1,0:T(8,128)S(1)} %bitcast.76, bf16[896,2048]{1,0:T(8,128)(2,1)S(1)} %get-tuple-element.28.rows_ref), custom_call_target="tpu_custom_call" | custom-call | flops 704643072 | bytes 2621440 | tf_op jit(solution)/shard_map/token_sums/pallas_call | solution.py:136
  125.6 1.6 collective-permute-start.31
  127.4 2.0 %collective-permute-start.16 = (bf16[48,1024]{1,0:T(8,128)(2,1)S(1)}, bf16[48,1024]{1,0:T(8,128)(2,1)S(1)}, u32[]{:S(2)}, u32[]{:S(2)}) collective-permute-start(bf16[48,1024]{1,0:T(8,128)(2,1)S(1)} %get-tuple-element.61), channel_id=1, source_target_pairs={{0,2},{2,4},{4,6},{6,0},{1,3},{3,5},{5,7},{7,1},{8,10},{10,12},{12... | collective-permute-start | bytes 294920 | tf_op jit(solution)/shard_map/ppermute | solution.py:28
  129.8 4.4 %collective-permute-done.35 = bf16[192,1024]{1,0:T(8,128)(2,1)S(1)} collective-permute-done((bf16[192,1024]{1,0:T(8,128)(2,1)S(1)}, bf16[192,1024]{1,0:T(8,128)(2,1)S(1)}, u32[]{:S(2)}, u32[]{:S(2)}) %collective-permute-start.35) | collective-permute-done | bytes 393248 | tf_op jit(solution)/shard_map/ppermute | solution.py:28
  134.4 4.0 %collective-permute-done.31 = bf16[192,1024]{1,0:T(8,128)(2,1)S(1)} collective-permute-done((bf16[192,1024]{1,0:T(8,128)(2,1)S(1)}, bf16[192,1024]{1,0:T(8,128)(2,1)S(1)}, u32[]{:S(2)}, u32[]{:S(2)}) %collective-permute-start.31) | collective-permute-done | bytes 393248 | tf_op jit(solution)/shard_map/ppermute | solution.py:28
  139.4 3.2 %collective-permute-start.36 = (bf16[48,1024]{1,0:T(8,128)(2,1)S(1)}, bf16[48,1024]{1,0:T(8,128)(2,1)S(1)}, u32[]{:S(2)}, u32[]{:S(2)}) collective-permute-start(bf16[48,1024]{1,0:T(8,128)(2,1)S(1)} %get-tuple-element.44), channel_id=1, source_target_pairs={{0,6},{2,0},{4,2},{6,4},{1,7},{3,1},{5,3},{7,5},{8,14},{10,8},{12,... | collective-permute-start | bytes 294920 | tf_op jit(solution)/shard_map/ppermute | solution.py:28
  146.0 1.6 collective-permute-start.32
  147.6 5.4 %collective-permute-done.11 = bf16[48,1024]{1,0:T(8,128)(2,1)S(1)} collective-permute-done((bf16[48,1024]{1,0:T(8,128)(2,1)S(1)}, bf16[48,1024]{1,0:T(8,128)(2,1)S(1)}, u32[]{:S(2)}, u32[]{:S(2)}) %collective-permute-start.11) | collective-permute-done | bytes 98336 | tf_op jit(solution)/shard_map/ppermute | solution.py:28
  154.6 2.4 %collective-permute-done.37 = bf16[48,1024]{1,0:T(8,128)(2,1)S(1)} collective-permute-done((bf16[48,1024]{1,0:T(8,128)(2,1)S(1)}, bf16[48,1024]{1,0:T(8,128)(2,1)S(1)}, u32[]{:S(2)}, u32[]{:S(2)}) %collective-permute-start.37) | collective-permute-done | bytes 98336 | tf_op jit(solution)/shard_map/ppermute | solution.py:28
  157.0 2.3 %collective-permute-start.17 = (bf16[48,2048]{1,0:T(8,128)(2,1)S(1)}, bf16[48,2048]{1,0:T(8,128)(2,1)S(1)}, u32[]{:S(2)}, u32[]{:S(2)}) collective-permute-start(bf16[48,2048]{1,0:T(8,128)(2,1)S(1)} %fusion), channel_id=1, source_target_pairs={{0,8},{8,16},{16,24},{24,0},{1,9},{9,17},{17,25},{25,1},{2,10},{10... | collective-permute-start | bytes 589832 | tf_op jit(solution)/shard_map/ppermute | solution.py:28
  159.4 1.8 collective-permute-done.33
  161.4 2.3 %collective-permute-start.39 = (bf16[48,2048]{1,0:T(8,128)(2,1)S(1)}, bf16[48,2048]{1,0:T(8,128)(2,1)S(1)}, u32[]{:S(2)}, u32[]{:S(2)}) collective-permute-start(bf16[48,2048]{1,0:T(8,128)(2,1)S(1)} %fusion.1), channel_id=1, source_target_pairs={{0,24},{8,0},{16,8},{24,16},{1,25},{9,1},{17,9},{25,17},{2,26},{10... | collective-permute-start | bytes 589832 | tf_op jit(solution)/shard_map/ppermute | solution.py:28
  163.7 14.0 %weight_grads.1 = (bf16[8,2048,384]{2,1,0:T(8,128)(2,1)}, bf16[8,2048,384]{2,1,0:T(8,128)(2,1)}, bf16[8,384,2048]{2,1,0:T(8,128)(2,1)}) custom-call(bf16[896,2048]{1,0:T(8,128)(2,1)S(1)} %get-tuple-element.26.rows_ref, bf16[896,2048]{1,0:T(8,128)(2,1)S(1)} %get-tuple-element.27.grad_ref, bf16[896,384]{1,0:T(8,128)(2,1)S(1)} %get-tuple-element.33.hidden_ref, ...), custom_call_target="tpu_custom_call" | custom-call | flops 4227858432 | bytes 37748736 | tf_op jit(solution)/shard_map/weight_grads/pallas_call | solution.py:232
  (111 shorter events, 28.2 us)
Async XLA Ops:
  1.5 13.2 %collective-permute-start.2 = (s32[96,32]{0,1:T(8,128)S(1)}, s32[96,32]{0,1:T(8,128)S(1)}, u32[]{:S(2)}, u32[]{:S(2)}) collective-permute-start(s32[96,32]{0,1:T(8,128)S(1)} %pad_add_fusion.1), channel_id=1, source_target_pairs={{0,6},{2,0},{4,2},{6,4},{1,7},{3,1},{5,3},{7,5},{8,14},{10,8},{12,... | collective-permute-start | bytes 36872 | tf_op jit(solution)/shard_map/ppermute | solution.py:28
  6.6 12.2 %collective-permute-start = (s32[96,32]{0,1:T(8,128)S(1)}, s32[96,32]{0,1:T(8,128)S(1)}, u32[]{:S(2)}, u32[]{:S(2)}) collective-permute-start(s32[96,32]{0,1:T(8,128)S(1)} %pad_add_fusion.1), channel_id=1, source_target_pairs={{0,2},{2,4},{4,6},{6,0},{1,3},{3,5},{5,7},{7,1},{8,10},{10,12},{12... | collective-permute-start | bytes 36872 | tf_op jit(solution)/shard_map/ppermute | solution.py:28
  8.7 13.2 %collective-permute-start.5 = (bf16[48,2048]{1,0:T(8,128)(2,1)S(1)}, bf16[48,2048]{1,0:T(8,128)(2,1)S(1)}, u32[]{:S(2)}, u32[]{:S(2)}) collective-permute-start(bf16[48,2048]{1,0:T(8,128)(2,1)S(1)} %get-tuple-element.64.refs_2_), channel_id=1, source_target_pairs={{0,6},{2,0},{4,2},{6,4},{1,7},{3,1},{5,3},{7,5},{8,14},{10,8},{12,... | collective-permute-start | bytes 589832 | tf_op jit(solution)/shard_map/ppermute | solution.py:28
  11.5 25.9 %collective-permute-start.4 = (bf16[48,2048]{1,0:T(8,128)(2,1)S(1)}, bf16[48,2048]{1,0:T(8,128)(2,1)S(1)}, u32[]{:S(2)}, u32[]{:S(2)}) collective-permute-start(bf16[48,2048]{1,0:T(8,128)(2,1)S(1)} %get-tuple-element.64.refs_2_), channel_id=1, source_target_pairs={{0,4},{2,6},{4,0},{6,2},{1,5},{3,7},{5,1},{7,3},{8,12},{10,14},{12... | collective-permute-start | bytes 589832 | tf_op jit(solution)/shard_map/ppermute | solution.py:28
  14.8 24.2 %collective-permute-start.3 = (bf16[48,2048]{1,0:T(8,128)(2,1)S(1)}, bf16[48,2048]{1,0:T(8,128)(2,1)S(1)}, u32[]{:S(2)}, u32[]{:S(2)}) collective-permute-start(bf16[48,2048]{1,0:T(8,128)(2,1)S(1)} %get-tuple-element.64.refs_2_), channel_id=1, source_target_pairs={{0,2},{2,4},{4,6},{6,0},{1,3},{3,5},{5,7},{7,1},{8,10},{10,12},{12... | collective-permute-start | bytes 589832 | tf_op jit(solution)/shard_map/ppermute | solution.py:28
  14.9 25.4 %collective-permute-start.21 = (bf16[48,2048]{1,0:T(8,128)(2,1)S(1)}, bf16[48,2048]{1,0:T(8,128)(2,1)S(1)}, u32[]{:S(2)}, u32[]{:S(2)}) collective-permute-start(bf16[48,2048]{1,0:T(8,128)(2,1)S(1)} %get-tuple-element.50.refs_2_), channel_id=1, source_target_pairs={{0,6},{2,0},{4,2},{6,4},{1,7},{3,1},{5,3},{7,5},{8,14},{10,8},{12,... | collective-permute-start | bytes 589832 | tf_op jit(solution)/shard_map/ppermute | solution.py:28
  18.8 26.3 %collective-permute-start.20 = (bf16[48,2048]{1,0:T(8,128)(2,1)S(1)}, bf16[48,2048]{1,0:T(8,128)(2,1)S(1)}, u32[]{:S(2)}, u32[]{:S(2)}) collective-permute-start(bf16[48,2048]{1,0:T(8,128)(2,1)S(1)} %get-tuple-element.50.refs_2_), channel_id=1, source_target_pairs={{0,4},{2,6},{4,0},{6,2},{1,5},{3,7},{5,1},{7,3},{8,12},{10,14},{12... | collective-permute-start | bytes 589832 | tf_op jit(solution)/shard_map/ppermute | solution.py:28
  21.8 23.3 %collective-permute-start.8 = (bf16[48,2048]{1,0:T(8,128)(2,1)S(1)}, bf16[48,2048]{1,0:T(8,128)(2,1)S(1)}, u32[]{:S(2)}, u32[]{:S(2)}) collective-permute-start(bf16[48,2048]{1,0:T(8,128)(2,1)S(1)} %collective-permute-done.5.refs_5_), channel_id=1, source_target_pairs={{0,1},{1,0},{2,3},{3,2},{4,5},{5,4},{6,7},{7,6},{8,9},{9,8},{10,11... | collective-permute-start | bytes 589832 | tf_op jit(solution)/shard_map/ppermute | solution.py:28
  40.3 14.1 %collective-permute-start.19 = (bf16[48,2048]{1,0:T(8,128)(2,1)S(1)}, bf16[48,2048]{1,0:T(8,128)(2,1)}, u32[]{:S(2)}, u32[]{:S(2)}) collective-permute-start(bf16[48,2048]{1,0:T(8,128)(2,1)S(1)} %get-tuple-element.50.refs_2_), channel_id=1, source_target_pairs={{0,2},{2,4},{4,6},{6,0},{1,3},{3,5},{5,7},{7,1},{8,10},{10,12},{12... | collective-permute-start | bytes 589832 | tf_op jit(solution)/shard_map/ppermute | solution.py:28
  45.1 17.9 %collective-permute-start.26 = (bf16[48,2048]{1,0:T(8,128)(2,1)S(1)}, bf16[48,2048]{1,0:T(8,128)(2,1)}, u32[]{:S(2)}, u32[]{:S(2)}) collective-permute-start(bf16[48,2048]{1,0:T(8,128)(2,1)S(1)} %get-tuple-element.48.refs_10_), channel_id=1, source_target_pairs={{0,4},{2,6},{4,0},{6,2},{1,5},{3,7},{5,1},{7,3},{8,12},{10,14},{12... | collective-permute-start | bytes 589832 | tf_op jit(solution)/shard_map/ppermute | solution.py:28
  45.2 19.3 %collective-permute-start.25 = (bf16[48,2048]{1,0:T(8,128)(2,1)S(1)}, bf16[48,2048]{1,0:T(8,128)(2,1)}, u32[]{:S(2)}, u32[]{:S(2)}) collective-permute-start(bf16[48,2048]{1,0:T(8,128)(2,1)S(1)} %get-tuple-element.48.refs_10_), channel_id=1, source_target_pairs={{0,2},{2,4},{4,6},{6,0},{1,3},{3,5},{5,7},{7,1},{8,10},{10,12},{12... | collective-permute-start | bytes 589832 | tf_op jit(solution)/shard_map/ppermute | solution.py:28
  47.4 17.6 %collective-permute-start.24 = (bf16[48,2048]{1,0:T(8,128)(2,1)S(1)}, bf16[48,2048]{1,0:T(8,128)(2,1)}, u32[]{:S(2)}, u32[]{:S(2)}) collective-permute-start(bf16[48,2048]{1,0:T(8,128)(2,1)S(1)} %collective-permute-done.21.refs_5_), channel_id=1, source_target_pairs={{0,1},{1,0},{2,3},{3,2},{4,5},{5,4},{6,7},{7,6},{8,9},{9,8},{10,11... | collective-permute-start | bytes 589832 | tf_op jit(solution)/shard_map/ppermute | solution.py:28
  54.4 35.0 %collective-permute-start.23 = (bf16[48,2048]{1,0:T(8,128)(2,1)}, bf16[48,2048]{1,0:T(8,128)(2,1)S(1)}, u32[]{:S(2)}, u32[]{:S(2)}) collective-permute-start(bf16[48,2048]{1,0:T(8,128)(2,1)} %copy-done), channel_id=1, source_target_pairs={{0,1},{1,0},{2,3},{3,2},{4,5},{5,4},{6,7},{7,6},{8,9},{9,8},{10,11... | collective-permute-start | bytes 589832 | tf_op jit(solution)/shard_map/ppermute | solution.py:28
  55.0 35.1 %collective-permute-start.22 = (bf16[48,2048]{1,0:T(8,128)(2,1)}, bf16[48,2048]{1,0:T(8,128)(2,1)S(1)}, u32[]{:S(2)}, u32[]{:S(2)}) collective-permute-start(bf16[48,2048]{1,0:T(8,128)(2,1)} %collective-permute-done.19.refs_3_), channel_id=1, source_target_pairs={{0,1},{1,0},{2,3},{3,2},{4,5},{5,4},{6,7},{7,6},{8,9},{9,8},{10,11... | collective-permute-start | bytes 589832 | tf_op jit(solution)/shard_map/ppermute | solution.py:28
  63.0 28.6 %collective-permute-start.30 = (bf16[48,2048]{1,0:T(8,128)(2,1)}, bf16[48,2048]{1,0:T(8,128)(2,1)S(1)}, u32[]{:S(2)}, u32[]{:S(2)}) collective-permute-start(bf16[48,2048]{1,0:T(8,128)(2,1)} %collective-permute-done.27.refs_13_), channel_id=1, source_target_pairs={{0,1},{1,0},{2,3},{3,2},{4,5},{5,4},{6,7},{7,6},{8,9},{9,8},{10,11... | collective-permute-start | bytes 589832 | tf_op jit(solution)/shard_map/ppermute | solution.py:28
  64.5 27.1 %collective-permute-start.29 = (bf16[48,2048]{1,0:T(8,128)(2,1)}, bf16[48,2048]{1,0:T(8,128)(2,1)S(1)}, u32[]{:S(2)}, u32[]{:S(2)}) collective-permute-start(bf16[48,2048]{1,0:T(8,128)(2,1)} %collective-permute-done.26.refs_12_), channel_id=1, source_target_pairs={{0,1},{1,0},{2,3},{3,2},{4,5},{5,4},{6,7},{7,6},{8,9},{9,8},{10,11... | collective-permute-start | bytes 589832 | tf_op jit(solution)/shard_map/ppermute | solution.py:28
  65.0 26.6 %collective-permute-start.28 = (bf16[48,2048]{1,0:T(8,128)(2,1)}, bf16[48,2048]{1,0:T(8,128)(2,1)S(1)}, u32[]{:S(2)}, u32[]{:S(2)}) collective-permute-start(bf16[48,2048]{1,0:T(8,128)(2,1)} %collective-permute-done.25.refs_11_), channel_id=1, source_target_pairs={{0,1},{1,0},{2,3},{3,2},{4,5},{5,4},{6,7},{7,6},{8,9},{9,8},{10,11... | collective-permute-start | bytes 589832 | tf_op jit(solution)/shard_map/ppermute | solution.py:28
  89.5 37.7 %collective-permute-start.13 = (bf16[192,1024]{1,0:T(8,128)(2,1)S(1)}, bf16[192,1024]{1,0:T(8,128)(2,1)S(1)}, u32[]{:S(2)}, u32[]{:S(2)}) collective-permute-start(bf16[192,1024]{1,0:T(8,128)(2,1)S(1)} %get-tuple-element.25), channel_id=1, source_target_pairs={{0,1},{1,0},{2,3},{3,2},{4,5},{5,4},{6,7},{7,6},{8,9},{9,8},{10,11... | collective-permute-start | bytes 1179656 | tf_op jit(solution)/shard_map/ppermute | solution.py:28
  90.0 39.4 %collective-permute-start.9 = (bf16[192,1024]{1,0:T(8,128)(2,1)S(1)}, bf16[192,1024]{1,0:T(8,128)(2,1)S(1)}, u32[]{:S(2)}, u32[]{:S(2)}) collective-permute-start(bf16[192,1024]{1,0:T(8,128)(2,1)S(1)} %get-tuple-element.23), channel_id=1, source_target_pairs={{0,1},{1,0},{2,3},{3,2},{4,5},{5,4},{6,7},{7,6},{8,9},{9,8},{10,11... | collective-permute-start | bytes 1179656 | tf_op jit(solution)/shard_map/ppermute | solution.py:28
  122.1 12.1 %collective-permute-start.35 = (bf16[192,1024]{1,0:T(8,128)(2,1)S(1)}, bf16[192,1024]{1,0:T(8,128)(2,1)S(1)}, u32[]{:S(2)}, u32[]{:S(2)}) collective-permute-start(bf16[192,1024]{1,0:T(8,128)(2,1)S(1)} %get-tuple-element.32), channel_id=1, source_target_pairs={{0,1},{1,0},{2,3},{3,2},{4,5},{5,4},{6,7},{7,6},{8,9},{9,8},{10,11... | collective-permute-start | bytes 1179656 | tf_op jit(solution)/shard_map/ppermute | solution.py:28
  125.6 12.8 %collective-permute-start.31 = (bf16[192,1024]{1,0:T(8,128)(2,1)S(1)}, bf16[192,1024]{1,0:T(8,128)(2,1)S(1)}, u32[]{:S(2)}, u32[]{:S(2)}) collective-permute-start(bf16[192,1024]{1,0:T(8,128)(2,1)S(1)} %get-tuple-element.30), channel_id=1, source_target_pairs={{0,1},{1,0},{2,3},{3,2},{4,5},{5,4},{6,7},{7,6},{8,9},{9,8},{10,11... | collective-permute-start | bytes 1179656 | tf_op jit(solution)/shard_map/ppermute | solution.py:28
  127.4 12.0 %collective-permute-start.16 = (bf16[48,1024]{1,0:T(8,128)(2,1)S(1)}, bf16[48,1024]{1,0:T(8,128)(2,1)S(1)}, u32[]{:S(2)}, u32[]{:S(2)}) collective-permute-start(bf16[48,1024]{1,0:T(8,128)(2,1)S(1)} %get-tuple-element.61), channel_id=1, source_target_pairs={{0,2},{2,4},{4,6},{6,0},{1,3},{3,5},{5,7},{7,1},{8,10},{10,12},{12... | collective-permute-start | bytes 294920 | tf_op jit(solution)/shard_map/ppermute | solution.py:28
  129.4 13.1 %collective-permute-start.15 = (bf16[48,1024]{1,0:T(8,128)(2,1)S(1)}, bf16[48,1024]{1,0:T(8,128)(2,1)S(1)}, u32[]{:S(2)}, u32[]{:S(2)}) collective-permute-start(bf16[48,1024]{1,0:T(8,128)(2,1)S(1)} %get-tuple-element.62), channel_id=1, source_target_pairs={{0,4},{2,6},{4,0},{6,2},{1,5},{3,7},{5,1},{7,3},{8,12},{10,14},{12... | collective-permute-start | bytes 294920 | tf_op jit(solution)/shard_map/ppermute | solution.py:28
  138.6 14.3 %collective-permute-start.11 = (bf16[48,1024]{1,0:T(8,128)(2,1)S(1)}, bf16[48,1024]{1,0:T(8,128)(2,1)S(1)}, u32[]{:S(2)}, u32[]{:S(2)}) collective-permute-start(bf16[48,1024]{1,0:T(8,128)(2,1)S(1)} %get-tuple-element.59), channel_id=1, source_target_pairs={{0,4},{2,6},{4,0},{6,2},{1,5},{3,7},{5,1},{7,3},{8,12},{10,14},{12... | collective-permute-start | bytes 294920 | tf_op jit(solution)/shard_map/ppermute | solution.py:28
  139.4 13.7 %collective-permute-start.36 = (bf16[48,1024]{1,0:T(8,128)(2,1)S(1)}, bf16[48,1024]{1,0:T(8,128)(2,1)S(1)}, u32[]{:S(2)}, u32[]{:S(2)}) collective-permute-start(bf16[48,1024]{1,0:T(8,128)(2,1)S(1)} %get-tuple-element.44), channel_id=1, source_target_pairs={{0,6},{2,0},{4,2},{6,4},{1,7},{3,1},{5,3},{7,5},{8,14},{10,8},{12,... | collective-permute-start | bytes 294920 | tf_op jit(solution)/shard_map/ppermute | solution.py:28
  142.6 12.0 %collective-permute-start.38 = (bf16[48,1024]{1,0:T(8,128)(2,1)S(1)}, bf16[48,1024]{1,0:T(8,128)(2,1)S(1)}, u32[]{:S(2)}, u32[]{:S(2)}) collective-permute-start(bf16[48,1024]{1,0:T(8,128)(2,1)S(1)} %get-tuple-element.45), channel_id=1, source_target_pairs={{0,2},{2,4},{4,6},{6,0},{1,3},{3,5},{5,7},{7,1},{8,10},{10,12},{12... | collective-permute-start | bytes 294920 | tf_op jit(solution)/shard_map/ppermute | solution.py:28
  143.2 13.8 %collective-permute-start.37 = (bf16[48,1024]{1,0:T(8,128)(2,1)S(1)}, bf16[48,1024]{1,0:T(8,128)(2,1)S(1)}, u32[]{:S(2)}, u32[]{:S(2)}) collective-permute-start(bf16[48,1024]{1,0:T(8,128)(2,1)S(1)} %get-tuple-element.46), channel_id=1, source_target_pairs={{0,4},{2,6},{4,0},{6,2},{1,5},{3,7},{5,1},{7,3},{8,12},{10,14},{12... | collective-permute-start | bytes 294920 | tf_op jit(solution)/shard_map/ppermute | solution.py:28
  146.0 13.3 %collective-permute-start.32 = (bf16[48,1024]{1,0:T(8,128)(2,1)S(1)}, bf16[48,1024]{1,0:T(8,128)(2,1)S(1)}, u32[]{:S(2)}, u32[]{:S(2)}) collective-permute-start(bf16[48,1024]{1,0:T(8,128)(2,1)S(1)} %get-tuple-element.41), channel_id=1, source_target_pairs={{0,6},{2,0},{4,2},{6,4},{1,7},{3,1},{5,3},{7,5},{8,14},{10,8},{12,... | collective-permute-start | bytes 294920 | tf_op jit(solution)/shard_map/ppermute | solution.py:28
  154.6 23.1 %collective-permute-start.18 = (bf16[48,2048]{1,0:T(8,128)(2,1)S(1)}, bf16[48,2048]{1,0:T(8,128)(2,1)S(1)}, u32[]{:S(2)}, u32[]{:S(2)}) collective-permute-start(bf16[48,2048]{1,0:T(8,128)(2,1)S(1)} %fusion), channel_id=1, source_target_pairs={{0,9},{1,8},{8,17},{9,16},{16,25},{17,24},{24,1},{25,0},{2,11},{3,... | collective-permute-start | bytes 589832 | tf_op jit(solution)/shard_map/ppermute | solution.py:292
  157.0 20.7 %collective-permute-start.17 = (bf16[48,2048]{1,0:T(8,128)(2,1)S(1)}, bf16[48,2048]{1,0:T(8,128)(2,1)S(1)}, u32[]{:S(2)}, u32[]{:S(2)}) collective-permute-start(bf16[48,2048]{1,0:T(8,128)(2,1)S(1)} %fusion), channel_id=1, source_target_pairs={{0,8},{8,16},{16,24},{24,0},{1,9},{9,17},{17,25},{25,1},{2,10},{10... | collective-permute-start | bytes 589832 | tf_op jit(solution)/shard_map/ppermute | solution.py:28
  161.3 16.4 %collective-permute-start.40 = (bf16[48,2048]{1,0:T(8,128)(2,1)S(1)}, bf16[48,2048]{1,0:T(8,128)(2,1)S(1)}, u32[]{:S(2)}, u32[]{:S(2)}) collective-permute-start(bf16[48,2048]{1,0:T(8,128)(2,1)S(1)} %fusion.1), channel_id=1, source_target_pairs={{0,25},{1,24},{8,1},{9,0},{16,9},{17,8},{24,17},{25,16},{2,27},{3,... | collective-permute-start | bytes 589832 | tf_op jit(solution)/shard_map/ppermute | solution.py:292
  161.4 16.4 %collective-permute-start.39 = (bf16[48,2048]{1,0:T(8,128)(2,1)S(1)}, bf16[48,2048]{1,0:T(8,128)(2,1)S(1)}, u32[]{:S(2)}, u32[]{:S(2)}) collective-permute-start(bf16[48,2048]{1,0:T(8,128)(2,1)S(1)} %fusion.1), channel_id=1, source_target_pairs={{0,24},{8,0},{16,8},{24,16},{1,25},{9,1},{17,9},{25,17},{2,26},{10... | collective-permute-start | bytes 589832 | tf_op jit(solution)/shard_map/ppermute | solution.py:28
  (11 other events, 105.6 us)

commit v2 on v1

v2 whole, which is shorter than its diff:
```python
import functools

import jax
import jax.numpy as jnp
from jax import lax
from jax.experimental import pallas as pl
from jax.experimental.pallas import tpu as pltpu
from jax.sharding import PartitionSpec as P

EXPERTS = 32
MOST = 26
BF16 = jnp.bfloat16
F32 = jnp.float32
MIB = 1 << 20

NN = (((1,), (0,)), ((), ()))
NT = (((1,), (1,)), ((), ()))
TN = (((0,), (0,)), ((), ()))


def dot(a, b, dims=NN):
    return lax.dot_general(a, b, dims, preferred_element_type=F32)


def rotate(block, axis, distance):
    n = lax.axis_size(axis)
    return lax.ppermute(block, axis, [(i, (i + distance) % n) for i in range(n)])


def swap(block, axis, mask):
    n = lax.axis_size(axis)
    return lax.ppermute(block, axis, [(i, i ^ mask) for i in range(n)])


def after(value, *others):
    return lax.optimization_barrier((value, *others))[0]


def params(mib=40):
    return pltpu.CompilerParams(vmem_limit_bytes=mib * MIB)


def cost(flops, nbytes):
    return pl.CostEstimate(flops=int(flops), bytes_accessed=int(nbytes), transcendentals=0)


def routing_kernel(slots, dest_ref, weight_ref, dest_col_ref, weight_col_ref, *refs):
    ordered_refs, mix_refs, slot_weight_ref = refs[:2], refs[2:4], refs[4]
    total, tokens = ordered_refs[0].shape
    local = total // slots
    place = lax.broadcasted_iota(jnp.int32, (slots, tokens), 0)
    slot = lax.broadcasted_iota(jnp.int32, (tokens, total), 1)
    for way in range(2):
        mix = jnp.zeros((tokens, total), F32)
        for l in range(local):
            at = way * local + l
            part = slice(l * slots, (l + 1) * slots)
            hit = place == dest_ref[at : at + 1, :]
            ordered_refs[way][part, :] = jnp.where(hit, 1.0, 0.0).astype(BF16)
            if way == 1:
                slot_weight_ref[part, :] = jnp.sum(
                    jnp.where(hit, weight_ref[at : at + 1, :], 0.0), 1, keepdims=True
                )
            here = dest_col_ref[:, at : at + 1]
            here = jnp.where(here >= 0, here + l * slots, -1)
            value = weight_col_ref[:, at : at + 1] if way == 0 else 1.0
            mix = jnp.where(slot == here, value, mix)
        mix_refs[way][...] = mix.astype(BF16)


def routing_matrices(dest, weight, slots):
    tokens, both = dest.shape
    total = both // 2 * slots
    return pl.pallas_call(
        functools.partial(routing_kernel, slots),
        out_shape=[jax.ShapeDtypeStruct((total, tokens), BF16)] * 2
        + [jax.ShapeDtypeStruct((tokens, total), BF16)] * 2
        + [jax.ShapeDtypeStruct((total, 1), F32)],
        compiler_params=params(48),
        cost_estimate=cost(0, 8 * total * tokens),
        name="routing",
    )(dest.T, weight.T, dest, weight)


def order_kernel(n_pieces, onehot_ref, *refs):
    *pieces, out_ref, rows_ref = refs
    at = 0
    for piece in pieces:
        rows_ref[at : at + piece.shape[0], :] = piece[...]
        at += piece.shape[0]
    out_ref[...] = dot(onehot_ref[...], rows_ref[...]).astype(BF16)


def weighted_order_kernel(n_pieces, plain, onehot_ref, slot_weight_ref, *refs):
    *pieces, out_ref, rows_ref = refs
    at = 0
    for piece in pieces:
        rows_ref[at : at + piece.shape[0], :] = piece[...]
        at += piece.shape[0]
    ordered = dot(onehot_ref[...], rows_ref[...])
    scale = jnp.where(pl.program_id(0) < plain, 1.0, slot_weight_ref[...])
    out_ref[...] = (ordered * scale).astype(BF16)


def in_expert_order(onehot, pieces, slot_weight=None):
    total, tokens = onehot.shape
    width = pieces[0].shape[1]
    chunk = min(512, width)
    steps = width // chunk
    in_specs = [pl.BlockSpec((total, tokens), lambda c: (0, 0))]
    operands = [onehot]
    if slot_weight is None:
        kernel = functools.partial(order_kernel, len(pieces))
    else:
        kernel = functools.partial(weighted_order_kernel, len(pieces), steps // 2)
        in_specs.append(pl.BlockSpec((total, 1), lambda c: (0, 0)))
        operands.append(slot_weight)
    in_specs += [pl.BlockSpec((piece.shape[0], chunk), lambda c: (0, c)) for piece in pieces]
    return pl.pallas_call(
        kernel,
        grid=(steps,),
        in_specs=in_specs,
        out_specs=pl.BlockSpec((total, chunk), lambda c: (0, c)),
        out_shape=jax.ShapeDtypeStruct((total, width), BF16),
        scratch_shapes=[pltpu.VMEM((tokens, chunk), BF16)],
        compiler_params=params(),
        cost_estimate=cost(2 * total * tokens * width, 2 * (total + tokens) * width),
        name="order_rows",
    )(*operands, *pieces)


def combine_kernel(mix_ref, rows_ref, keep_ref, send_ref):
    half = mix_ref.shape[0] // 2
    summed = dot(mix_ref[...], rows_ref[...]).astype(BF16)
    keep_ref[...] = summed[:half]
    send_ref[...] = summed[half:]


def token_sums(mix, rows, part, parts):
    tokens, total = mix.shape
    width = rows.shape[1] // parts
    chunk = min(512, width)
    steps = width // chunk
    return pl.pallas_call(
        combine_kernel,
        grid=(steps,),
        in_specs=[
            pl.BlockSpec((tokens, total), lambda c: (0, 0)),
            pl.BlockSpec((total, chunk), lambda c: (0, c + part * steps)),
        ],
        out_specs=[pl.BlockSpec((tokens // 2, chunk), lambda c: (0, c))] * 2,
        out_shape=[jax.ShapeDtypeStruct((tokens // 2, width), BF16)] * 2,
        compiler_params=params(),
        cost_estimate=cost(2 * total * tokens * width, 2 * (total + tokens) * width),
        name="token_sums",
    )(mix, rows)


def forward_kernel(rows_ref, gate_ref, up_ref, down_ref, out_ref):
    rows = rows_ref[...]
    gate_value = dot(rows, gate_ref[0])
    up_value = dot(rows, up_ref[0])
    hidden = (gate_value / (1.0 + jnp.exp(-gate_value)) * up_value).astype(BF16)
    out_ref[...] = dot(hidden, down_ref[0]).astype(BF16)


def backward_kernel(
    rows_ref, grad_ref, gate_ref, up_ref, down_ref, hidden_ref, gate_grad_ref, up_grad_ref, out_ref
):
    rows = rows_ref[...]
    gate_value = dot(rows, gate_ref[0])
    up_value = dot(rows, up_ref[0])
    hidden_grad = dot(grad_ref[...], down_ref[0], NT)
    sig = 1.0 / (1.0 + jnp.exp(-gate_value))
    silu = gate_value * sig
    hidden_ref[...] = (silu * up_value).astype(BF16)
    up_grad = (hidden_grad * silu).astype(BF16)
    gate_grad = (hidden_grad * up_value * sig * (1.0 + gate_value * (1.0 - sig))).astype(BF16)
    up_grad_ref[...] = up_grad
    gate_grad_ref[...] = gate_grad
    out_ref[...] = (dot(gate_grad, gate_ref[0], NT) + dot(up_grad, up_ref[0], NT)).astype(BF16)


def weights_kernel(
    rows_ref, grad_ref, hidden_ref, gate_grad_ref, up_grad_ref, gate_ref, up_ref, down_ref
):
    rows = rows_ref[...]
    gate_ref[0] = dot(rows, gate_grad_ref[...], TN).astype(BF16)
    up_ref[0] = dot(rows, up_grad_ref[...], TN).astype(BF16)
    down_ref[0] = dot(hidden_ref[...], grad_ref[...], TN).astype(BF16)


def expert_specs(local, slots, width, hidden):
    wide = pl.BlockSpec((slots, width), lambda e: (e, 0))
    narrow = pl.BlockSpec((slots, hidden), lambda e: (e, 0))
    column = pl.BlockSpec((1, width, hidden), lambda e: (e, 0, 0))
    row = pl.BlockSpec((1, hidden, width), lambda e: (e, 0, 0))
    return wide, narrow, column, row


def forward_experts(rows, gate, up, down):
    local, width, hidden = gate.shape
    slots = rows.shape[0] // local
    wide, narrow, column, row = expert_specs(local, slots, width, hidden)
    return pl.pallas_call(
        forward_kernel,
        grid=(local,),
        in_specs=[wide, column, column, row],
        out_specs=wide,
        out_shape=jax.ShapeDtypeStruct(rows.shape, BF16),
        compiler_params=params(),
        cost_estimate=cost(6 * rows.shape[0] * width * hidden, 6 * local * width * hidden),
        name="forward_experts",
    )(rows, gate, up, down)


def backward_experts(both, gate, up, down):
    local, width, hidden = gate.shape
    total = both.shape[0]
    slots = total // local
    wide, narrow, column, row = expert_specs(local, slots, width, hidden)
    grad_wide = pl.BlockSpec((slots, width), lambda e: (e, 1))
    small = jax.ShapeDtypeStruct((total, hidden), BF16)
    return pl.pallas_call(
        backward_kernel,
        grid=(local,),
        in_specs=[wide, grad_wide, column, column, row],
        out_specs=[narrow, narrow, narrow, wide],
        out_shape=[small, small, small, jax.ShapeDtypeStruct((total, width), BF16)],
        compiler_params=params(),
        cost_estimate=cost(10 * total * width * hidden, 6 * local * width * hidden),
        name="backward_experts",
    )(both, both, gate, up, down)


def weight_grads(both, hidden_rows, gate_grad, up_grad, local):
    total, hidden = gate_grad.shape
    width = both.shape[1] // 2
    slots = total // local
    grad_wide = pl.BlockSpec((slots, width), lambda e: (e, 1))
    wide, narrow, column, row = expert_specs(local, slots, width, hidden)
    return pl.pallas_call(
        weights_kernel,
        grid=(local,),
        in_specs=[wide, grad_wide, narrow, narrow, narrow],
        out_specs=[column, column, row],
        out_shape=[
            jax.ShapeDtypeStruct((local, width, hidden), BF16),
            jax.ShapeDtypeStruct((local, width, hidden), BF16),
            jax.ShapeDtypeStruct((local, hidden, width), BF16),
        ],
        compiler_params=params(),
        cost_estimate=cost(6 * total * width * hidden, 6 * local * width * hidden),
        name="weight_grads",
    )(both, both, hidden_rows, gate_grad, up_grad)


def halves(block, dp_index):
    half = block.shape[0] // 2
    mine = lax.dynamic_slice_in_dim(block, dp_index * half, half, 0)
    other = lax.dynamic_slice_in_dim(block, (1 - dp_index) * half, half, 0)
    return mine, other


def spread_near(mine, groups):
    if groups != 4:
        return [lax.all_gather(mine, "expert", tiled=True)]
    return [swap(mine, "expert", 1), swap(mine, "expert", 2)]


def spread_far(near, groups):
    if groups == 4:
        near = near + [swap(near[1], "expert", 1)]
    return near, [swap(piece, "dp", 1) for piece in near]


def pieces(mine, near, other, far, groups):
    if groups != 4:
        return near + far
    return [mine] + near + [other] + far


def spread_meta(meta, dp_index, groups):
    half = meta.shape[0] // 2
    both = jnp.concatenate(halves(meta, dp_index), 0)
    if groups != 4:
        metas = list(lax.all_gather(both, "expert"))
    else:
        metas = [both] + [swap(both, "expert", r) for r in range(1, groups)]
    return jnp.concatenate([m[:half] for m in metas] + [m[half:] for m in metas], 0)


def sums_sent(keep, received, groups):
    pair = (keep.astype(F32) + received.astype(F32)).astype(BF16)
    pair = pair.reshape(groups, keep.shape[0] // groups, -1)
    if groups != 4:
        return [lax.all_to_all(pair, "expert", 0, 0, tiled=True)]
    return [pair[0]] + [swap(pair[r], "expert", r) for r in range(1, groups)]


def sums_home(base, sent):
    total = base.astype(F32)
    for piece in sent:
        piece = piece.astype(F32)
        total = total + (jnp.sum(piece, 0) if piece.ndim == 3 else piece)
    return total.astype(BF16)


def to_section(mine, direction, dp_index):
    n, m = lax.axis_size("section"), lax.axis_size("dp")
    same = rotate(mine, "section", direction)
    route = [
        (s * m + d, ((s + direction) % n) * m + (m - 1 - d)) for s in range(n) for d in range(m)
    ]
    cross = lax.ppermute(mine, ("section", "dp"), route)
    first = jnp.where(dp_index == 0, same, cross)
    second = jnp.where(dp_index == 0, cross, same)
    return jnp.concatenate([first, second], 0)


def slot_tables(meta, choices, base, local):
    tokens = meta.shape[0]
    meta = meta.reshape(tokens, 2, 2, choices)
    routes, counted = meta[:, :, 0], meta[:, :, 1].astype(F32)
    mixing = counted / jnp.sum(counted, -1, keepdims=True)
    hit = (routes[..., None] - base) == jnp.arange(local, dtype=jnp.int32)
    weight = jnp.sum(jnp.where(hit, mixing[..., None], 0.0), 2)
    chosen = jnp.any(hit, 2).astype(jnp.int32)
    rank = jnp.cumsum(chosen, 0) - chosen
    dest = jnp.where(chosen > 0, rank, -1)
    return dest.reshape(tokens, -1), weight.reshape(tokens, -1)


def local(
    fwd_in, fwd_routes, fwd_numer, bwd_saved, bwd_routes, bwd_numer, bwd_grad, w_gate, w_up, w_down
):
    groups = lax.axis_size("expert")
    group, dp_index = lax.axis_index("expert"), lax.axis_index("dp")
    gate, up, down = w_gate[0], w_up[0], w_down[0]
    n_local = gate.shape[0]
    choices = fwd_routes.shape[-1]
    slots = -(-groups * MOST // 16) * 16

    meta = jnp.concatenate([fwd_routes[0], fwd_numer[0], bwd_routes[0], bwd_numer[0]], -1)
    meta_all = spread_meta(meta, dp_index, groups)
    dest, weight = slot_tables(meta_all, choices, group * n_local, n_local)

    in_mine, in_other = halves(fwd_in[0], dp_index)
    grad_mine, _ = halves(bwd_grad[0], dp_index)
    back_mine, back_other = halves(jnp.concatenate([bwd_saved[0], bwd_grad[0]], 1), dp_index)

    near = spread_near(in_mine, groups)
    back_near = spread_near(after(back_mine, *near), groups)
    near, far = spread_far(near, groups)

    ordered, back_ordered, mix, back_mix, slot_weight = routing_matrices(dest, weight, slots)
    in_rows = in_expert_order(ordered, pieces(in_mine, near, in_other, far, groups))
    in_rows, *back_near = lax.optimization_barrier((in_rows, *back_near))
    back_near, back_far = spread_far(back_near, groups)
    out_rows = forward_experts(in_rows, gate, up, down)
    out_keep, out_send = token_sums(mix, out_rows, 0, 1)
    out_received = swap(after(out_send, back_far[-1]), "dp", 1)

    back_rows = in_expert_order(
        back_ordered, pieces(back_mine, back_near, back_other, back_far, groups), slot_weight
    )
    hidden, gate_grad, up_grad, row_grad = backward_experts(back_rows, gate, up, down)
    row_grad, out_received = lax.optimization_barrier((row_grad, out_received))
    out_sent = sums_sent(out_keep, out_received, groups)
    keep, send = token_sums(back_mix, row_grad, 0, 1)
    received = swap(send, "dp", 1)
    gate_grad = after(gate_grad, keep)
    gate_sum, up_sum, down_sum = weight_grads(back_rows, hidden, gate_grad, up_grad, n_local)
    gate_sum, received, *out_sent = lax.optimization_barrier((gate_sum, received, *out_sent))
    sent = sums_sent(keep, received, groups)
    next_fwd = to_section(sums_home(in_mine, out_sent), 1, dp_index)
    next_bwd = to_section(sums_home(grad_mine, sent), -1, dp_index)
    return (next_fwd[None], next_bwd[None], gate_sum[None], up_sum[None], down_sum[None])


def solution(mesh):
    in_specs = (
        P("section", "expert", None),
        P("section", "expert", None),
        P("section", "expert", None),
        P("section", "expert", None),
        P("section", "expert", None),
        P("section", "expert", None),
        P("section", "expert", None),
        P("section", "expert", None, "dp"),
        P("section", "expert", None, "dp"),
        P("section", "expert", "dp", None),
    )
    out_specs = (
        P("section", "expert", None),
        P("section", "expert", None),
        P("section", "expert", None, "dp"),
        P("section", "expert", None, "dp"),
        P("section", "expert", "dp", None),
    )
    return jax.shard_map(local, mesh=mesh, in_specs=in_specs, out_specs=out_specs, check_vma=False)
```

time: 180 us -> 155 us (0.86)
  starting transfers between devices: 49.2 us -> 36.1 us
  waiting for transfers between devices: 42.9 us -> 34.3 us
  Pallas kernels: 73.5 us -> 70.9 us
    ppermute x39 -> x2, starting transfers between devices: 49.1 us -> 3.23 us  [rotate(): lax.ppermute(block, axis, [(i, (i + distance) % n) for i in range(n)])]
    ppermute x39 -> x2, waiting for transfers between devices: 42.9 us -> 0.01 us  [rotate(): lax.ppermute(block, axis, [(i, (i + distance) % n) for i in range(n)])]
    ppermute x0 -> x23, starting transfers between devices: none -> 32.7 us  [swap(): return lax.ppermute(block, axis, [(i, i ^ mask) for i in range(n)])]
    ppermute x0 -> x23, waiting for transfers between devices: none -> 29.7 us  [swap(): return lax.ppermute(block, axis, [(i, i ^ mask) for i in range(n)])]
    ppermute x2, waiting for transfers between devices: 0.01 us -> 4.66 us  [to_section(): cross = lax.ppermute(mine, ('section', 'dp'), route)]
    unnamed x6 -> x14, local copies, waits for them, and re-layouts: 0.26 us -> 3.9 us
    transpose x4 -> x0, local copies, waits for them, and re-layouts: 2.83 us -> none  [the longest x3 1.8 us: local(): saved_rows, grad_rows = in_expert_order(back_dest.T, back_weight.T, [save...]
    pallas_call x8 -> x7, Pallas kernels: 57.9 us -> 55.3 us  [the longest x1 21.2 us: backward_experts(): pl.pallas_call(backward_kernel, grid=(local,), in_specs=[wide, grad_wide,...]
  transfers between devices with their start and end apart: 41 -> 27, of which waited for: 10 -> 8; matrix products, arithmetic and copies ran while one was open for 6% -> 4% of each run, Pallas kernels for 41% -> 44%
where the time goes in v2:
time: 155 us
  Pallas kernels  70.9 us (46%)
  starting transfers between devices  36.1 us (23%)
  waiting for transfers between devices  34.3 us (22%)
  other arithmetic  6.39 us (4%)
  local copies, waits for them, and re-layouts  5.96 us (4%)
    ppermute x23, starting transfers between devices, swap(): return lax.ppermute(block, axis, [(i, i ^ mask) for i in range(n)])  32.7 us
    ppermute x23, waiting for transfers between devices, swap(): return lax.ppermute(block, axis, [(i, i ^ mask) for i in range(n)])  29.7 us
    pallas_call x1, Pallas kernels, backward_experts(): pl.pallas_call(backward_kernel, grid=(local,), in_specs=[wide, grad_wide,...  21.2 us
    pallas_call x1, Pallas kernels, forward_experts(): pl.pallas_call(forward_kernel, grid=(local,), in_specs=[wide, column, col...  15.6 us
    pallas_call x1, Pallas kernels, weight_grads(): pl.pallas_call(weights_kernel, grid=(local,), in_specs=[wide, grad_wide,...  14.3 us
    pallas_call x2, Pallas kernels, in_expert_order(): pl.pallas_call(kernel, grid=(steps,), in_specs=in_specs, out_specs=pl.Blo...  10.1 us
    pallas_call x2, Pallas kernels, token_sums(): pl.pallas_call(combine_kernel, grid=(steps,), in_specs=[pl.BlockSpec((tok...  5.4 us
    ppermute x2, waiting for transfers between devices, to_section(): cross = lax.ppermute(mine, ('section', 'dp'), route)  4.66 us
  transfers between devices with their start and end apart: 27, of which 8 were waited for; matrix products, arithmetic and copies ran while one was open for 4% of the time, Pallas kernels for 44%

profile of v2, /device:TPU:0, one launch (start us, length us, event | category | flops | bytes accessed | tf_op | source)
XLA Modules:
  0.0 154.6 jit_solution(4893123419613097428)
XLA Ops:
  1.5 5.1 %collective-permute-start.2 = (s32[96,32]{0,1:T(8,128)S(1)}, s32[96,32]{0,1:T(8,128)S(1)}, u32[]{:S(2)}, u32[]{:S(2)}) collective-permute-start(s32[96,32]{0,1:T(8,128)S(1)} %pad_add_fusion.1), channel_id=1, source_target_pairs={{0,6},{2,4},{4,2},{6,0},{1,7},{3,5},{5,3},{7,1},{8,14},{10,12},{12... | collective-permute-start | bytes 36872 | tf_op jit(solution)/shard_map/ppermute | solution.py:32
  8.3 2.4 %collective-permute-start.4 = (bf16[48,2048]{1,0:T(8,128)(2,1)S(1)}, bf16[48,2048]{1,0:T(8,128)(2,1)}, u32[]{:S(2)}, u32[]{:S(2)}) collective-permute-start(bf16[48,2048]{1,0:T(8,128)(2,1)S(1)} %get-tuple-element.79.refs_0_), channel_id=1, source_target_pairs={{0,4},{2,6},{4,0},{6,2},{1,5},{3,7},{5,1},{7,3},{8,12},{10,14},{12... | collective-permute-start | bytes 589832 | tf_op jit(solution)/shard_map/ppermute | solution.py:32
  10.6 2.0 %collective-permute-start.3 = (bf16[48,2048]{1,0:T(8,128)(2,1)S(1)}, bf16[48,2048]{1,0:T(8,128)(2,1)}, u32[]{:S(2)}, u32[]{:S(2)}) collective-permute-start(bf16[48,2048]{1,0:T(8,128)(2,1)S(1)} %get-tuple-element.79.refs_0_), channel_id=1, source_target_pairs={{0,2},{2,0},{4,6},{6,4},{1,3},{3,1},{5,7},{7,5},{8,10},{10,8},{12,... | collective-permute-start | bytes 589832 | tf_op jit(solution)/shard_map/ppermute | solution.py:32
  14.4 1.7 %reduce-window.6 = s32[8,2,3,128]{3,0,1,2:T(8,128)S(1)} reduce-window(s32[8,2,3,128]{3,0,1,2:T(8,128)S(1)} %copy_bitcast_fusion, s32[]{:T(128)} %constant.11.clone.1), window={size=1x1x1x128 pad=0_0x0_0x0_0x127_0}, to_apply=%region_1.2 | reduce-window | flops 780288 | bytes 49156 | tf_op jit(solution)/shard_map/reduce-window
  16.4 3.5 %collective-permute-done.4.refs_2_ = bf16[48,2048]{1,0:T(8,128)(2,1)} collective-permute-done((bf16[48,2048]{1,0:T(8,128)(2,1)S(1)}, bf16[48,2048]{1,0:T(8,128)(2,1)}, u32[]{:S(2)}, u32[]{:S(2)}) %collective-permute-start.4) | collective-permute-done | bytes 196640 | tf_op jit(solution)/shard_map/ppermute | solution.py:32
  20.0 3.6 %collective-permute-start.10 = (bf16[48,4096]{1,0:T(8,128)(2,1)S(1)}, bf16[48,4096]{1,0:T(8,128)(2,1)S(1)}, u32[]{:S(2)}, u32[]{:S(2)}) collective-permute-start(bf16[48,4096]{1,0:T(8,128)(2,1)S(1)} %get-tuple-element.38.refs_0_), channel_id=1, source_target_pairs={{0,4},{2,6},{4,0},{6,2},{1,5},{3,7},{5,1},{7,3},{8,12},{10,14},{12... | collective-permute-start | bytes 1179656 | tf_op jit(solution)/shard_map/ppermute | solution.py:32
  23.6 1.5 collective-permute-start.7
  25.6 6.1 %collective-permute-done.5.refs_3_ = bf16[48,2048]{1,0:T(8,128)(2,1)} collective-permute-done((bf16[48,2048]{1,0:T(8,128)(2,1)}, bf16[48,2048]{1,0:T(8,128)(2,1)}, u32[]{:S(2)}, u32[]{:S(2)}) %collective-permute-start.5) | collective-permute-done | bytes 196640 | tf_op jit(solution)/shard_map/ppermute | solution.py:32
  31.7 1.5 collective-permute-start.8
  33.5 4.3 %routing.1 = (bf16[896,384]{1,0:T(8,128)(2,1)S(1)}, bf16[896,384]{1,0:T(8,128)(2,1)S(1)}, bf16[384,896]{1,0:T(8,128)(2,1)S(1)}, bf16[384,896]{1,0:T(8,128)(2,1)S(1)}, f32[896,1]{1,0:T(8,128)S(1)}) custom-call(s32[16,384]{1,0:T(8,128)S(1)} %get-tuple-element.81.dest_ref, f32[16,384]{1,0:T(8,128)S(1)} %bitcast.77, s32[384,16]{1,0:T(8,128)S(1)} %copy.29.dest_col_ref, ...), custom_call_target="tpu_custom_call" | custom-call | bytes 2752512 | tf_op jit(solution)/shard_map/routing/pallas_call | solution.py:74
  38.6 4.0 %order_rows.2.rows_ref = bf16[896,2048]{1,0:T(8,128)(2,1)S(1)} custom-call(bf16[896,384]{1,0:T(8,128)(2,1)S(1)} %get-tuple-element.37.onehot_ref, bf16[48,2048]{1,0:T(8,128)(2,1)S(1)} %get-tuple-element.79.refs_0_, bf16[48,2048]{1,0:T(8,128)(2,1)} %collective-permute-done.3.refs_1_, bf16[48,2048]{1,0:T(8,128)(2,1)} %collective-permute-done.4.refs_2_, ...), custom_call_target="tpu_custom_call" | custom-call | flops 1409286144 | bytes 5242880 | tf_op jit(solution)/shard_map/order_rows/pallas_call | solution.py:119
  42.6 1.8 %copy-done = bf16[896,2048]{1,0:T(8,128)(2,1)} copy-done((bf16[896,2048]{1,0:T(8,128)(2,1)}, bf16[896,2048]{1,0:T(8,128)(2,1)S(1)}, u32[]{:S(2)}) %copy-start) | copy-done | bytes 3670040
  44.5 1.8 %collective-permute-start.11 = (bf16[48,4096]{1,0:T(8,128)(2,1)S(1)}, bf16[48,4096]{1,0:T(8,128)(2,1)S(1)}, u32[]{:S(2)}, u32[]{:S(2)}) collective-permute-start(bf16[48,4096]{1,0:T(8,128)(2,1)S(1)} %collective-permute-done.10.refs_2_), channel_id=1, source_target_pairs={{0,2},{2,0},{4,6},{6,4},{1,3},{3,1},{5,7},{7,5},{8,10},{10,8},{12,... | collective-permute-start | bytes 1179656 | tf_op jit(solution)/shard_map/ppermute | solution.py:32
  46.3 1.5 collective-permute-start.13
  48.3 5.8 %collective-permute-done.11.refs_3_ = bf16[48,4096]{1,0:T(8,128)(2,1)S(1)} collective-permute-done((bf16[48,4096]{1,0:T(8,128)(2,1)S(1)}, bf16[48,4096]{1,0:T(8,128)(2,1)S(1)}, u32[]{:S(2)}, u32[]{:S(2)}) %collective-permute-start.11) | collective-permute-done | bytes 393248 | tf_op jit(solution)/shard_map/ppermute | solution.py:32
  54.1 1.5 collective-permute-start.14
  55.6 2.0 %copy-done.1 = bf16[896,2048]{1,0:T(8,128)(2,1)S(1)} copy-done((bf16[896,2048]{1,0:T(8,128)(2,1)S(1)}, bf16[896,2048]{1,0:T(8,128)(2,1)}, u32[]{:S(2)}) %copy-start.1) | copy-done | bytes 3670040
  57.6 15.6 %forward_experts.1.rows_ref = bf16[896,2048]{1,0:T(8,128)(2,1)S(1)} custom-call(bf16[896,2048]{1,0:T(8,128)(2,1)S(1)} %copy-done.1, bf16[8,2048,384]{2,1,0:T(8,128)(2,1)} %bitcast.78, bf16[8,2048,384]{2,1,0:T(8,128)(2,1)} %bitcast.80, bf16[8,384,2048]{2,1,0:T(8,128)(2,1)} %bitcast.82), custom_call_target="tpu_custom_call" | custom-call | flops 4227858432 | bytes 37748736 | tf_op jit(solution)/shard_map/forward_experts/pallas_call | solution.py:205
  73.3 2.7 %token_sums.2 = (bf16[192,2048]{1,0:T(8,128)(2,1)S(1)}, bf16[192,2048]{1,0:T(8,128)(2,1)S(1)}) custom-call(bf16[384,896]{1,0:T(8,128)(2,1)S(1)} %copy-done.5, bf16[896,2048]{1,0:T(8,128)(2,1)S(1)} %forward_experts.1.rows_ref), custom_call_target="tpu_custom_call" | custom-call | flops 1409286144 | bytes 5242880 | tf_op jit(solution)/shard_map/token_sums/pallas_call | solution.py:144
  76.6 6.0 %order_rows.3.rows_ref.grad_ref = bf16[896,4096]{1,0:T(8,128)(2,1)S(1)} custom-call(bf16[896,384]{1,0:T(8,128)(2,1)S(1)} %get-tuple-element.35.onehot_ref, f32[896,1]{1,0:T(8,128)S(1)} %get-tuple-element.36.slot_weight_ref, bf16[48,4096]{1,0:T(8,128)(2,1)S(1)} %get-tuple-element.38.refs_0_, bf16[48,4096]{1,0:T(8,128)(2,1)S(1)} %collective-permute-done.9.refs_1_, ...), custom_call_target="tpu_custom_call" | custom-call | flops 2818572288 | bytes 10485760 | tf_op jit(solution)/shard_map/order_rows/pallas_call | solution.py:119
  82.6 21.2 %backward_experts.1 = (bf16[896,384]{1,0:T(8,128)(2,1)S(1)}, bf16[896,384]{1,0:T(8,128)(2,1)S(1)}, bf16[896,384]{1,0:T(8,128)(2,1)S(1)}, bf16[896,2048]{1,0:T(8,128)(2,1)S(1)}) custom-call(bf16[896,4096]{1,0:T(8,128)(2,1)S(1)} %order_rows.3.rows_ref.grad_ref, bf16[896,4096]{1,0:T(8,128)(2,1)S(1)} %order_rows.3.rows_ref.grad_ref, ...), custom_call_target="tpu_custom_call" | custom-call | flops 7046430720 | bytes 37748736 | tf_op jit(solution)/shard_map/backward_experts/pallas_call | solution.py:224
  103.8 2.7 %token_sums.3 = (bf16[192,2048]{1,0:T(8,128)(2,1)S(1)}, bf16[192,2048]{1,0:T(8,128)(2,1)S(1)}) custom-call(bf16[384,896]{1,0:T(8,128)(2,1)S(1)} %copy-done.3, bf16[896,2048]{1,0:T(8,128)(2,1)S(1)} %get-tuple-element.49.rows_ref), custom_call_target="tpu_custom_call" | custom-call | flops 1409286144 | bytes 5242880 | tf_op jit(solution)/shard_map/token_sums/pallas_call | solution.py:144
  106.5 1.6 %collective-permute-start.16 = (bf16[192,2048]{1,0:T(8,128)(2,1)S(1)}, bf16[192,2048]{1,0:T(8,128)(2,1)S(1)}, u32[]{:S(2)}, u32[]{:S(2)}) collective-permute-start(bf16[192,2048]{1,0:T(8,128)(2,1)S(1)} %get-tuple-element.54), channel_id=1, source_target_pairs={{0,1},{1,0},{2,3},{3,2},{4,5},{5,4},{6,7},{7,6},{8,9},{9,8},{10,11... | collective-permute-start | bytes 2359304 | tf_op jit(solution)/shard_map/ppermute | solution.py:32
  108.5 2.9 %collective-permute-start.19 = (bf16[48,2048]{1,0:T(8,128)(2,1)S(1)}, bf16[48,2048]{1,0:T(8,128)(2,1)S(1)}, u32[]{:S(2)}, u32[]{:S(2)}) collective-permute-start(bf16[48,2048]{1,0:T(8,128)(2,1)S(1)} %get-tuple-element.68), channel_id=1, source_target_pairs={{0,6},{2,4},{4,2},{6,0},{1,7},{3,5},{5,3},{7,1},{8,14},{10,12},{12... | collective-permute-start | bytes 589832 | tf_op jit(solution)/shard_map/ppermute | solution.py:32
  112.9 14.3 %weight_grads.1 = (bf16[8,2048,384]{2,1,0:T(8,128)(2,1)}, bf16[8,2048,384]{2,1,0:T(8,128)(2,1)}, bf16[8,384,2048]{2,1,0:T(8,128)(2,1)}) custom-call(bf16[896,4096]{1,0:T(8,128)(2,1)S(1)} %order_rows.3.rows_ref.grad_ref, bf16[896,4096]{1,0:T(8,128)(2,1)S(1)} %order_rows.3.rows_ref.grad_ref, bf16[896,384]{1,0:T(8,128)(2,1)S(1)} %get-tuple-element.41.hidden_ref, ...), custom_call_target="tpu_custom_call" | custom-call | flops 4227858432 | bytes 37748736 | tf_op jit(solution)/shard_map/weight_grads/pallas_call | solution.py:242
  128.2 2.4 %collective-permute-start.24 = (bf16[48,2048]{1,0:T(8,128)(2,1)S(1)}, bf16[48,2048]{1,0:T(8,128)(2,1)S(1)}, u32[]{:S(2)}, u32[]{:S(2)}) collective-permute-start(bf16[48,2048]{1,0:T(8,128)(2,1)S(1)} %get-tuple-element.66), channel_id=1, source_target_pairs={{0,6},{2,4},{4,2},{6,0},{1,7},{3,5},{5,3},{7,1},{8,14},{10,12},{12... | collective-permute-start | bytes 589832 | tf_op jit(solution)/shard_map/ppermute | solution.py:32
  131.4 1.5 collective-permute-start.20
  132.9 2.0 %collective-permute-done.22 = bf16[48,2048]{1,0:T(8,128)(2,1)S(1)} collective-permute-done((bf16[48,2048]{1,0:T(8,128)(2,1)S(1)}, bf16[48,2048]{1,0:T(8,128)(2,1)S(1)}, u32[]{:S(2)}, u32[]{:S(2)}) %collective-permute-start.22) | collective-permute-done | bytes 196640 | tf_op jit(solution)/shard_map/ppermute | solution.py:32
  134.9 4.2 %collective-permute-done.24 = bf16[48,2048]{1,0:T(8,128)(2,1)S(1)} collective-permute-done((bf16[48,2048]{1,0:T(8,128)(2,1)S(1)}, bf16[48,2048]{1,0:T(8,128)(2,1)S(1)}, u32[]{:S(2)}, u32[]{:S(2)}) %collective-permute-start.24) | collective-permute-done | bytes 196640 | tf_op jit(solution)/shard_map/ppermute | solution.py:32
  139.0 7.4 %collective-permute-done.23 = bf16[48,2048]{1,0:T(8,128)(2,1)S(1)} collective-permute-done((bf16[48,2048]{1,0:T(8,128)(2,1)S(1)}, bf16[48,2048]{1,0:T(8,128)(2,1)S(1)}, u32[]{:S(2)}, u32[]{:S(2)}) %collective-permute-start.23) | collective-permute-done | bytes 196640 | tf_op jit(solution)/shard_map/ppermute | solution.py:32
  146.6 1.7 %collective-permute-start.25 = (bf16[48,2048]{1,0:T(8,128)(2,1)S(1)}, bf16[48,2048]{1,0:T(8,128)(2,1)S(1)}, u32[]{:S(2)}, u32[]{:S(2)}) collective-permute-start(bf16[48,2048]{1,0:T(8,128)(2,1)S(1)} %fusion.5), channel_id=1, source_target_pairs={{0,24},{8,0},{16,8},{24,16},{1,25},{9,1},{17,9},{25,17},{2,26},{10... | collective-permute-start | bytes 589832 | tf_op jit(solution)/shard_map/ppermute | solution.py:27
  149.2 4.7 %collective-permute-done.26 = bf16[48,2048]{1,0:T(8,128)(2,1)S(1)} collective-permute-done((bf16[48,2048]{1,0:T(8,128)(2,1)S(1)}, bf16[48,2048]{1,0:T(8,128)(2,1)S(1)}, u32[]{:S(2)}, u32[]{:S(2)}) %collective-permute-start.26) | collective-permute-done | bytes 196640 | tf_op jit(solution)/shard_map/ppermute | solution.py:315
  (76 shorter events, 12.6 us)
Async XLA Ops:
  1.5 12.4 %collective-permute-start.2 = (s32[96,32]{0,1:T(8,128)S(1)}, s32[96,32]{0,1:T(8,128)S(1)}, u32[]{:S(2)}, u32[]{:S(2)}) collective-permute-start(s32[96,32]{0,1:T(8,128)S(1)} %pad_add_fusion.1), channel_id=1, source_target_pairs={{0,6},{2,4},{4,2},{6,0},{1,7},{3,5},{5,3},{7,1},{8,14},{10,12},{12... | collective-permute-start | bytes 36872 | tf_op jit(solution)/shard_map/ppermute | solution.py:32
  6.6 7.4 %collective-permute-start.1 = (s32[96,32]{0,1:T(8,128)S(1)}, s32[96,32]{0,1:T(8,128)S(1)}, u32[]{:S(2)}, u32[]{:S(2)}) collective-permute-start(s32[96,32]{0,1:T(8,128)S(1)} %pad_add_fusion.1), channel_id=1, source_target_pairs={{0,4},{2,6},{4,0},{6,2},{1,5},{3,7},{5,1},{7,3},{8,12},{10,14},{12... | collective-permute-start | bytes 36872 | tf_op jit(solution)/shard_map/ppermute | solution.py:32
  6.6 7.5 %collective-permute-start = (s32[96,32]{0,1:T(8,128)S(1)}, s32[96,32]{0,1:T(8,128)S(1)}, u32[]{:S(2)}, u32[]{:S(2)}) collective-permute-start(s32[96,32]{0,1:T(8,128)S(1)} %pad_add_fusion.1), channel_id=1, source_target_pairs={{0,2},{2,0},{4,6},{6,4},{1,3},{3,1},{5,7},{7,5},{8,10},{10,8},{12,... | collective-permute-start | bytes 36872 | tf_op jit(solution)/shard_map/ppermute | solution.py:32
  8.3 11.6 %collective-permute-start.4 = (bf16[48,2048]{1,0:T(8,128)(2,1)S(1)}, bf16[48,2048]{1,0:T(8,128)(2,1)}, u32[]{:S(2)}, u32[]{:S(2)}) collective-permute-start(bf16[48,2048]{1,0:T(8,128)(2,1)S(1)} %get-tuple-element.79.refs_0_), channel_id=1, source_target_pairs={{0,4},{2,6},{4,0},{6,2},{1,5},{3,7},{5,1},{7,3},{8,12},{10,14},{12... | collective-permute-start | bytes 589832 | tf_op jit(solution)/shard_map/ppermute | solution.py:32
  10.6 9.4 %collective-permute-start.3 = (bf16[48,2048]{1,0:T(8,128)(2,1)S(1)}, bf16[48,2048]{1,0:T(8,128)(2,1)}, u32[]{:S(2)}, u32[]{:S(2)}) collective-permute-start(bf16[48,2048]{1,0:T(8,128)(2,1)S(1)} %get-tuple-element.79.refs_0_), channel_id=1, source_target_pairs={{0,2},{2,0},{4,6},{6,4},{1,3},{3,1},{5,7},{7,5},{8,10},{10,8},{12,... | collective-permute-start | bytes 589832 | tf_op jit(solution)/shard_map/ppermute | solution.py:32
  19.9 11.8 %collective-permute-start.5 = (bf16[48,2048]{1,0:T(8,128)(2,1)}, bf16[48,2048]{1,0:T(8,128)(2,1)}, u32[]{:S(2)}, u32[]{:S(2)}) collective-permute-start(bf16[48,2048]{1,0:T(8,128)(2,1)} %collective-permute-done.4.refs_2_), channel_id=1, source_target_pairs={{0,2},{2,0},{4,6},{6,4},{1,3},{3,1},{5,7},{7,5},{8,10},{10,8},{12,... | collective-permute-start | bytes 589832 | tf_op jit(solution)/shard_map/ppermute | solution.py:32
  20.0 24.4 %collective-permute-start.10 = (bf16[48,4096]{1,0:T(8,128)(2,1)S(1)}, bf16[48,4096]{1,0:T(8,128)(2,1)S(1)}, u32[]{:S(2)}, u32[]{:S(2)}) collective-permute-start(bf16[48,4096]{1,0:T(8,128)(2,1)S(1)} %get-tuple-element.38.refs_0_), channel_id=1, source_target_pairs={{0,4},{2,6},{4,0},{6,2},{1,5},{3,7},{5,1},{7,3},{8,12},{10,14},{12... | collective-permute-start | bytes 1179656 | tf_op jit(solution)/shard_map/ppermute | solution.py:32
  23.5 20.9 %collective-permute-start.9 = (bf16[48,4096]{1,0:T(8,128)(2,1)S(1)}, bf16[48,4096]{1,0:T(8,128)(2,1)S(1)}, u32[]{:S(2)}, u32[]{:S(2)}) collective-permute-start(bf16[48,4096]{1,0:T(8,128)(2,1)S(1)} %get-tuple-element.38.refs_0_), channel_id=1, source_target_pairs={{0,2},{2,0},{4,6},{6,4},{1,3},{3,1},{5,7},{7,5},{8,10},{10,8},{12,... | collective-permute-start | bytes 1179656 | tf_op jit(solution)/shard_map/ppermute | solution.py:32
  23.6 14.3 %collective-permute-start.7 = (bf16[48,2048]{1,0:T(8,128)(2,1)}, bf16[48,2048]{1,0:T(8,128)(2,1)}, u32[]{:S(2)}, u32[]{:S(2)}) collective-permute-start(bf16[48,2048]{1,0:T(8,128)(2,1)} %collective-permute-done.4.refs_2_), channel_id=1, source_target_pairs={{0,1},{1,0},{2,3},{3,2},{4,5},{5,4},{6,7},{7,6},{8,9},{9,8},{10,11... | collective-permute-start | bytes 589832 | tf_op jit(solution)/shard_map/ppermute | solution.py:32
  25.1 12.8 %collective-permute-start.6 = (bf16[48,2048]{1,0:T(8,128)(2,1)}, bf16[48,2048]{1,0:T(8,128)(2,1)}, u32[]{:S(2)}, u32[]{:S(2)}) collective-permute-start(bf16[48,2048]{1,0:T(8,128)(2,1)} %collective-permute-done.3.refs_1_), channel_id=1, source_target_pairs={{0,1},{1,0},{2,3},{3,2},{4,5},{5,4},{6,7},{7,6},{8,9},{9,8},{10,11... | collective-permute-start | bytes 589832 | tf_op jit(solution)/shard_map/ppermute | solution.py:32
  31.7 6.8 %collective-permute-start.8 = (bf16[48,2048]{1,0:T(8,128)(2,1)}, bf16[48,2048]{1,0:T(8,128)(2,1)}, u32[]{:S(2)}, u32[]{:S(2)}) collective-permute-start(bf16[48,2048]{1,0:T(8,128)(2,1)} %collective-permute-done.5.refs_3_), channel_id=1, source_target_pairs={{0,1},{1,0},{2,3},{3,2},{4,5},{5,4},{6,7},{7,6},{8,9},{9,8},{10,11... | collective-permute-start | bytes 589832 | tf_op jit(solution)/shard_map/ppermute | solution.py:32
  37.9 6.6 %copy-start.2 = (bf16[384,896]{1,0:T(8,128)(2,1)}, bf16[384,896]{1,0:T(8,128)(2,1)S(1)}, u32[]{:S(2)}) copy-start(bf16[384,896]{1,0:T(8,128)(2,1)S(1)} %get-tuple-element.43.mix_ref) | copy-start | bytes 2064388
  37.9 6.6 %copy-start.4 = (bf16[384,896]{1,0:T(8,128)(2,1)}, bf16[384,896]{1,0:T(8,128)(2,1)S(1)}, u32[]{:S(2)}) copy-start(bf16[384,896]{1,0:T(8,128)(2,1)S(1)} %get-tuple-element.45.mix_ref) | copy-start | bytes 2064388
  44.5 9.6 %collective-permute-start.11 = (bf16[48,4096]{1,0:T(8,128)(2,1)S(1)}, bf16[48,4096]{1,0:T(8,128)(2,1)S(1)}, u32[]{:S(2)}, u32[]{:S(2)}) collective-permute-start(bf16[48,4096]{1,0:T(8,128)(2,1)S(1)} %collective-permute-done.10.refs_2_), channel_id=1, source_target_pairs={{0,2},{2,0},{4,6},{6,4},{1,3},{3,1},{5,7},{7,5},{8,10},{10,8},{12,... | collective-permute-start | bytes 1179656 | tf_op jit(solution)/shard_map/ppermute | solution.py:32
  46.3 30.3 %collective-permute-start.13 = (bf16[48,4096]{1,0:T(8,128)(2,1)S(1)}, bf16[48,4096]{1,0:T(8,128)(2,1)S(1)}, u32[]{:S(2)}, u32[]{:S(2)}) collective-permute-start(bf16[48,4096]{1,0:T(8,128)(2,1)S(1)} %collective-permute-done.10.refs_2_), channel_id=1, source_target_pairs={{0,1},{1,0},{2,3},{3,2},{4,5},{5,4},{6,7},{7,6},{8,9},{9,8},{10,11... | collective-permute-start | bytes 1179656 | tf_op jit(solution)/shard_map/ppermute | solution.py:32
  47.8 28.8 %collective-permute-start.12 = (bf16[48,4096]{1,0:T(8,128)(2,1)S(1)}, bf16[48,4096]{1,0:T(8,128)(2,1)S(1)}, u32[]{:S(2)}, u32[]{:S(2)}) collective-permute-start(bf16[48,4096]{1,0:T(8,128)(2,1)S(1)} %collective-permute-done.9.refs_1_), channel_id=1, source_target_pairs={{0,1},{1,0},{2,3},{3,2},{4,5},{5,4},{6,7},{7,6},{8,9},{9,8},{10,11... | collective-permute-start | bytes 1179656 | tf_op jit(solution)/shard_map/ppermute | solution.py:32
  54.1 21.9 %collective-permute-start.14 = (bf16[48,4096]{1,0:T(8,128)(2,1)S(1)}, bf16[48,4096]{1,0:T(8,128)(2,1)S(1)}, u32[]{:S(2)}, u32[]{:S(2)}) collective-permute-start(bf16[48,4096]{1,0:T(8,128)(2,1)S(1)} %collective-permute-done.11.refs_3_), channel_id=1, source_target_pairs={{0,1},{1,0},{2,3},{3,2},{4,5},{5,4},{6,7},{7,6},{8,9},{9,8},{10,11... | collective-permute-start | bytes 1179656 | tf_op jit(solution)/shard_map/ppermute | solution.py:32
  57.6 15.6 %copy-start.5 = (bf16[384,896]{1,0:T(8,128)(2,1)S(1)}, bf16[384,896]{1,0:T(8,128)(2,1)}, u32[]{:S(2)}) copy-start(bf16[384,896]{1,0:T(8,128)(2,1)} %copy-done.4) | copy-start | bytes 2064388
  76.0 27.8 %collective-permute-start.15 = (bf16[192,2048]{1,0:T(8,128)(2,1)S(1)}, bf16[192,2048]{1,0:T(8,128)(2,1)S(1)}, u32[]{:S(2)}, u32[]{:S(2)}) collective-permute-start(bf16[192,2048]{1,0:T(8,128)(2,1)S(1)} %get-tuple-element.48), channel_id=1, source_target_pairs={{0,1},{1,0},{2,3},{3,2},{4,5},{5,4},{6,7},{7,6},{8,9},{9,8},{10,11... | collective-permute-start | bytes 2359304 | tf_op jit(solution)/shard_map/ppermute | solution.py:32
  82.6 21.2 %copy-start.3 = (bf16[384,896]{1,0:T(8,128)(2,1)S(1)}, bf16[384,896]{1,0:T(8,128)(2,1)}, u32[]{:S(2)}) copy-start(bf16[384,896]{1,0:T(8,128)(2,1)} %copy-done.2) | copy-start | bytes 2064388
  106.5 20.7 %collective-permute-start.16 = (bf16[192,2048]{1,0:T(8,128)(2,1)S(1)}, bf16[192,2048]{1,0:T(8,128)(2,1)S(1)}, u32[]{:S(2)}, u32[]{:S(2)}) collective-permute-start(bf16[192,2048]{1,0:T(8,128)(2,1)S(1)} %get-tuple-element.54), channel_id=1, source_target_pairs={{0,1},{1,0},{2,3},{3,2},{4,5},{5,4},{6,7},{7,6},{8,9},{9,8},{10,11... | collective-permute-start | bytes 2359304 | tf_op jit(solution)/shard_map/ppermute | solution.py:32
  108.5 18.8 %collective-permute-start.19 = (bf16[48,2048]{1,0:T(8,128)(2,1)S(1)}, bf16[48,2048]{1,0:T(8,128)(2,1)S(1)}, u32[]{:S(2)}, u32[]{:S(2)}) collective-permute-start(bf16[48,2048]{1,0:T(8,128)(2,1)S(1)} %get-tuple-element.68), channel_id=1, source_target_pairs={{0,6},{2,4},{4,2},{6,0},{1,7},{3,5},{5,3},{7,1},{8,14},{10,12},{12... | collective-permute-start | bytes 589832 | tf_op jit(solution)/shard_map/ppermute | solution.py:32
  111.4 15.9 %collective-permute-start.18 = (bf16[48,2048]{1,0:T(8,128)(2,1)S(1)}, bf16[48,2048]{1,0:T(8,128)(2,1)S(1)}, u32[]{:S(2)}, u32[]{:S(2)}) collective-permute-start(bf16[48,2048]{1,0:T(8,128)(2,1)S(1)} %get-tuple-element.69), channel_id=1, source_target_pairs={{0,4},{2,6},{4,0},{6,2},{1,5},{3,7},{5,1},{7,3},{8,12},{10,14},{12... | collective-permute-start | bytes 589832 | tf_op jit(solution)/shard_map/ppermute | solution.py:32
  111.5 15.8 %collective-permute-start.17 = (bf16[48,2048]{1,0:T(8,128)(2,1)S(1)}, bf16[48,2048]{1,0:T(8,128)(2,1)S(1)}, u32[]{:S(2)}, u32[]{:S(2)}) collective-permute-start(bf16[48,2048]{1,0:T(8,128)(2,1)S(1)} %get-tuple-element.70), channel_id=1, source_target_pairs={{0,2},{2,0},{4,6},{6,4},{1,3},{3,1},{5,7},{7,5},{8,10},{10,8},{12,... | collective-permute-start | bytes 589832 | tf_op jit(solution)/shard_map/ppermute | solution.py:32
  127.2 19.2 %copy-start.6 = (bf16[1,96,2048]{2,1,0:T(8,128)(2,1)S(1)}, bf16[1,96,2048]{2,1,0:T(8,128)(2,1)}, u32[]{:S(2)}) copy-start(bf16[1,96,2048]{2,1,0:T(8,128)(2,1)} %param.16) | copy-start | bytes 1179652
  127.6 7.3 %collective-permute-start.22 = (bf16[48,2048]{1,0:T(8,128)(2,1)S(1)}, bf16[48,2048]{1,0:T(8,128)(2,1)S(1)}, u32[]{:S(2)}, u32[]{:S(2)}) collective-permute-start(bf16[48,2048]{1,0:T(8,128)(2,1)S(1)} %get-tuple-element.65), channel_id=1, source_target_pairs={{0,2},{2,0},{4,6},{6,4},{1,3},{3,1},{5,7},{7,5},{8,10},{10,8},{12,... | collective-permute-start | bytes 589832 | tf_op jit(solution)/shard_map/ppermute | solution.py:32
  128.2 10.8 %collective-permute-start.24 = (bf16[48,2048]{1,0:T(8,128)(2,1)S(1)}, bf16[48,2048]{1,0:T(8,128)(2,1)S(1)}, u32[]{:S(2)}, u32[]{:S(2)}) collective-permute-start(bf16[48,2048]{1,0:T(8,128)(2,1)S(1)} %get-tuple-element.66), channel_id=1, source_target_pairs={{0,6},{2,4},{4,2},{6,0},{1,7},{3,5},{5,3},{7,1},{8,14},{10,12},{12... | collective-permute-start | bytes 589832 | tf_op jit(solution)/shard_map/ppermute | solution.py:32
  130.6 15.9 %collective-permute-start.23 = (bf16[48,2048]{1,0:T(8,128)(2,1)S(1)}, bf16[48,2048]{1,0:T(8,128)(2,1)S(1)}, u32[]{:S(2)}, u32[]{:S(2)}) collective-permute-start(bf16[48,2048]{1,0:T(8,128)(2,1)S(1)} %get-tuple-element.67), channel_id=1, source_target_pairs={{0,4},{2,6},{4,0},{6,2},{1,5},{3,7},{5,1},{7,3},{8,12},{10,14},{12... | collective-permute-start | bytes 589832 | tf_op jit(solution)/shard_map/ppermute | solution.py:32
  131.3 17.1 %collective-permute-start.21 = (bf16[48,2048]{1,0:T(8,128)(2,1)S(1)}, bf16[48,2048]{1,0:T(8,128)(2,1)S(1)}, u32[]{:S(2)}, u32[]{:S(2)}) collective-permute-start(bf16[48,2048]{1,0:T(8,128)(2,1)S(1)} %add_convert_fusion.2), channel_id=1, source_target_pairs={{0,9},{1,8},{8,17},{9,16},{16,25},{17,24},{24,1},{25,0},{2,11},{3,... | collective-permute-start | bytes 589832 | tf_op jit(solution)/shard_map/ppermute | solution.py:315
  131.4 17.0 %collective-permute-start.20 = (bf16[48,2048]{1,0:T(8,128)(2,1)S(1)}, bf16[48,2048]{1,0:T(8,128)(2,1)S(1)}, u32[]{:S(2)}, u32[]{:S(2)}) collective-permute-start(bf16[48,2048]{1,0:T(8,128)(2,1)S(1)} %add_convert_fusion.2), channel_id=1, source_target_pairs={{0,8},{8,16},{16,24},{24,0},{1,9},{9,17},{17,25},{25,1},{2,10},{10... | collective-permute-start | bytes 589832 | tf_op jit(solution)/shard_map/ppermute | solution.py:27
  146.6 7.2 %collective-permute-start.26 = (bf16[48,2048]{1,0:T(8,128)(2,1)S(1)}, bf16[48,2048]{1,0:T(8,128)(2,1)S(1)}, u32[]{:S(2)}, u32[]{:S(2)}) collective-permute-start(bf16[48,2048]{1,0:T(8,128)(2,1)S(1)} %fusion.5), channel_id=1, source_target_pairs={{0,25},{1,24},{8,1},{9,0},{16,9},{17,8},{24,17},{25,16},{2,27},{3,... | collective-permute-start | bytes 589832 | tf_op jit(solution)/shard_map/ppermute | solution.py:315
  146.6 7.2 %collective-permute-start.25 = (bf16[48,2048]{1,0:T(8,128)(2,1)S(1)}, bf16[48,2048]{1,0:T(8,128)(2,1)S(1)}, u32[]{:S(2)}, u32[]{:S(2)}) collective-permute-start(bf16[48,2048]{1,0:T(8,128)(2,1)S(1)} %fusion.5), channel_id=1, source_target_pairs={{0,24},{8,0},{16,8},{24,16},{1,25},{9,1},{17,9},{25,17},{2,26},{10... | collective-permute-start | bytes 589832 | tf_op jit(solution)/shard_map/ppermute | solution.py:27
  (2 other events, 3.9 us)

commit v3 on v2

--- a/solution.py
+++ b/solution.py
@@ -36,8 +36,8 @@
     return lax.optimization_barrier((value, *others))[0]
 
 
-def params(mib=40):
-    return pltpu.CompilerParams(vmem_limit_bytes=mib * MIB)
+def params(slots):
+    return pltpu.CompilerParams(vmem_limit_bytes=(40 if slots <= 128 else 48) * MIB)
 
 
 def cost(flops, nbytes):
@@ -76,7 +76,7 @@
         out_shape=[jax.ShapeDtypeStruct((total, tokens), BF16)] * 2
         + [jax.ShapeDtypeStruct((tokens, total), BF16)] * 2
         + [jax.ShapeDtypeStruct((total, 1), F32)],
-        compiler_params=params(48),
+        compiler_params=params(slots),
         cost_estimate=cost(0, 8 * total * tokens),
         name="routing",
     )(dest.T, weight.T, dest, weight)
@@ -123,7 +123,7 @@
         out_specs=pl.BlockSpec((total, chunk), lambda c: (0, c)),
         out_shape=jax.ShapeDtypeStruct((total, width), BF16),
         scratch_shapes=[pltpu.VMEM((tokens, chunk), BF16)],
-        compiler_params=params(),
+        compiler_params=params(total // 8),
         cost_estimate=cost(2 * total * tokens * width, 2 * (total + tokens) * width),
         name="order_rows",
     )(*operands, *pieces)
@@ -150,7 +150,7 @@
         ],
         out_specs=[pl.BlockSpec((tokens // 2, chunk), lambda c: (0, c))] * 2,
         out_shape=[jax.ShapeDtypeStruct((tokens // 2, width), BF16)] * 2,
-        compiler_params=params(),
+        compiler_params=params(total // 8),
         cost_estimate=cost(2 * total * tokens * width, 2 * (total + tokens) * width),
         name="token_sums",
     )(mix, rows)
@@ -208,7 +208,7 @@
         in_specs=[wide, column, column, row],
         out_specs=wide,
         out_shape=jax.ShapeDtypeStruct(rows.shape, BF16),
-        compiler_params=params(),
+        compiler_params=params(slots),
         cost_estimate=cost(6 * rows.shape[0] * width * hidden, 6 * local * width * hidden),
         name="forward_experts",
     )(rows, gate, up, down)
@@ -227,7 +227,7 @@
         in_specs=[wide, grad_wide, column, column, row],
         out_specs=[narrow, narrow, narrow, wide],
         out_shape=[small, small, small, jax.ShapeDtypeStruct((total, width), BF16)],
-        compiler_params=params(),
+        compiler_params=params(slots),
         cost_estimate=cost(10 * total * width * hidden, 6 * local * width * hidden),
         name="backward_experts",
     )(both, both, gate, up, down)
@@ -249,7 +249,7 @@
             jax.ShapeDtypeStruct((local, width, hidden), BF16),
             jax.ShapeDtypeStruct((local, hidden, width), BF16),
         ],
-        compiler_params=params(),
+        compiler_params=params(slots),
         cost_estimate=cost(6 * total * width * hidden, 6 * local * width * hidden),
         name="weight_grads",
     )(both, both, hidden_rows, gate_grad, up_grad)
@@ -262,22 +262,10 @@
     return mine, other
 
 
-def spread_near(mine, groups):
-    if groups != 4:
-        return [lax.all_gather(mine, "expert", tiled=True)]
-    return [swap(mine, "expert", 1), swap(mine, "expert", 2)]
-
-
-def spread_far(near, groups):
-    if groups == 4:
-        near = near + [swap(near[1], "expert", 1)]
-    return near, [swap(piece, "dp", 1) for piece in near]
-
-
-def pieces(mine, near, other, far, groups):
-    if groups != 4:
-        return near + far
-    return [mine] + near + [other] + far
+def cross(block, axis, mask):
+    n, m = lax.axis_size(axis), lax.axis_size("dp")
+    route = [(i * m + d, (i ^ mask) * m + (m - 1 - d)) for i in range(n) for d in range(m)]
+    return lax.ppermute(block, (axis, "dp"), route)
 
 
 def spread_meta(meta, dp_index, groups):
@@ -312,9 +300,9 @@
     route = [
         (s * m + d, ((s + direction) % n) * m + (m - 1 - d)) for s in range(n) for d in range(m)
     ]
-    cross = lax.ppermute(mine, ("section", "dp"), route)
-    first = jnp.where(dp_index == 0, same, cross)
-    second = jnp.where(dp_index == 0, cross, same)
+    other = lax.ppermute(mine, ("section", "dp"), route)
+    first = jnp.where(dp_index == 0, same, other)
+    second = jnp.where(dp_index == 0, other, same)
     return jnp.concatenate([first, second], 0)
 
 
@@ -342,28 +330,41 @@
     slots = -(-groups * MOST // 16) * 16
 
     meta = jnp.concatenate([fwd_routes[0], fwd_numer[0], bwd_routes[0], bwd_numer[0]], -1)
-    meta_all = spread_meta(meta, dp_index, groups)
+    in_mine, in_other = halves(fwd_in[0], dp_index)
+    meta_all = spread_meta(after(meta, in_mine), dp_index, groups)
     dest, weight = slot_tables(meta_all, choices, group * n_local, n_local)
-
-    in_mine, in_other = halves(fwd_in[0], dp_index)
     grad_mine, _ = halves(bwd_grad[0], dp_index)
     back_mine, back_other = halves(jnp.concatenate([bwd_saved[0], bwd_grad[0]], 1), dp_index)
 
-    near = spread_near(in_mine, groups)
-    back_near = spread_near(after(back_mine, *near), groups)
-    near, far = spread_far(near, groups)
+    if groups == 4:
+        near, past = swap(in_mine, "expert", 1), swap(in_mine, "expert", 2)
+        back_near = swap(after(back_mine, near, past), "expert", 1)
+        last = swap(past, "expert", 1)
+        far = [swap(near, "dp", 1), swap(past, "dp", 1), swap(last, "dp", 1)]
+        back_past = swap(after(back_mine, last), "expert", 2)
+        in_pieces = [in_mine, near, past, last, in_other, *far]
+    else:
+        near = lax.all_gather(in_mine, "expert", tiled=True)
+        back_near = lax.all_gather(back_mine, "expert", tiled=True)
+        back_past = ()
+        in_pieces = [near, swap(near, "dp", 1)]
 
     ordered, back_ordered, mix, back_mix, slot_weight = routing_matrices(dest, weight, slots)
-    in_rows = in_expert_order(ordered, pieces(in_mine, near, in_other, far, groups))
-    in_rows, *back_near = lax.optimization_barrier((in_rows, *back_near))
-    back_near, back_far = spread_far(back_near, groups)
+    ordered, back_near = lax.optimization_barrier((ordered, back_near))
+    back_far = swap(back_near, "dp", 1)
+    in_rows = in_expert_order(ordered, in_pieces)
+    in_rows, back_past = lax.optimization_barrier((in_rows, back_past))
+    if groups == 4:
+        back_last = swap(back_past, "expert", 1)
+        back_far = [back_far, swap(back_past, "dp", 1), cross(back_past, "expert", 1)]
+        back_pieces = [back_mine, back_near, back_past, back_last, back_other, *back_far]
+    else:
+        back_pieces = [back_near, back_far]
     out_rows = forward_experts(in_rows, gate, up, down)
     out_keep, out_send = token_sums(mix, out_rows, 0, 1)
-    out_received = swap(after(out_send, back_far[-1]), "dp", 1)
-
-    back_rows = in_expert_order(
-        back_ordered, pieces(back_mine, back_near, back_other, back_far, groups), slot_weight
-    )
+    out_received = swap(after(out_send, back_pieces[-1]), "dp", 1)
+
+    back_rows = in_expert_order(back_ordered, back_pieces, slot_weight)
     hidden, gate_grad, up_grad, row_grad = backward_experts(back_rows, gate, up, down)
     row_grad, out_received = lax.optimization_barrier((row_grad, out_received))
     out_sent = sums_sent(out_keep, out_received, groups)

time: 155 us -> 145 us (0.935)
  waiting for transfers between devices: 34.3 us -> 29.5 us
  local copies, waits for them, and re-layouts: 5.96 us -> 2.07 us
    ppermute x23 -> x22, waiting for transfers between devices: 29.7 us -> 24.8 us  [swap(): return lax.ppermute(block, axis, [(i, i ^ mask) for i in range(n)])]
    unnamed x14 -> x2, local copies, waits for them, and re-layouts: 3.9 us -> 0.01 us
    ppermute x23 -> x22, starting transfers between devices: 32.7 us -> 32.1 us  [swap(): return lax.ppermute(block, axis, [(i, i ^ mask) for i in range(n)])]
    ppermute x2 -> x3, waiting for transfers between devices: 4.66 us -> 4.66 us  [the longest x2 4.66 us: to_section(): other = lax.ppermute(mine, ('section', 'dp'), route)]
  transfers between devices with their start and end apart: 27 -> 27, of which waited for: 8 -> 8; matrix products, arithmetic and copies ran while one was open for 4% -> 4% of each run, Pallas kernels for 44% -> 47%
where the time goes in v3:
time: 145 us
  Pallas kernels  70.6 us (49%)
  starting transfers between devices  35.5 us (24%)
  waiting for transfers between devices  29.5 us (20%)
  other arithmetic  6.39 us (4%)
  local copies, waits for them, and re-layouts  2.07 us (1%)
    ppermute x22, starting transfers between devices, swap(): return lax.ppermute(block, axis, [(i, i ^ mask) for i in range(n)])  32.1 us
    ppermute x22, waiting for transfers between devices, swap(): return lax.ppermute(block, axis, [(i, i ^ mask) for i in range(n)])  24.8 us
    pallas_call x1, Pallas kernels, backward_experts(): pl.pallas_call(backward_kernel, grid=(local,), in_specs=[wide, grad_wide,...  21.1 us
    pallas_call x1, Pallas kernels, forward_experts(): pl.pallas_call(forward_kernel, grid=(local,), in_specs=[wide, column, col...  15.6 us
    pallas_call x1, Pallas kernels, weight_grads(): pl.pallas_call(weights_kernel, grid=(local,), in_specs=[wide, grad_wide,...  14.3 us
    pallas_call x2, Pallas kernels, in_expert_order(): pl.pallas_call(kernel, grid=(steps,), in_specs=in_specs, out_specs=pl.Blo...  9.89 us
    pallas_call x2, Pallas kernels, token_sums(): pl.pallas_call(combine_kernel, grid=(steps,), in_specs=[pl.BlockSpec((tok...  5.4 us
    ppermute x2, waiting for transfers between devices, to_section(): other = lax.ppermute(mine, ('section', 'dp'), route)  4.66 us
  transfers between devices with their start and end apart: 27, of which 8 were waited for; matrix products, arithmetic and copies ran while one was open for 4% of the time, Pallas kernels for 47%

profile of v3, /device:TPU:0, one launch (start us, length us, event | category | flops | bytes accessed | tf_op | source)
XLA Modules:
  0.0 145.0 jit_solution(18273319635931647480)
XLA Ops:
  2.6 5.1 %collective-permute-start.2 = (s32[96,32]{0,1:T(8,128)S(1)}, s32[96,32]{0,1:T(8,128)S(1)}, u32[]{:S(2)}, u32[]{:S(2)}) collective-permute-start(s32[96,32]{0,1:T(8,128)S(1)} %pad_add_fusion.1), channel_id=1, source_target_pairs={{0,6},{2,4},{4,2},{6,0},{1,7},{3,5},{5,3},{7,1},{8,14},{10,12},{12... | collective-permute-start | bytes 36872 | tf_op jit(solution)/shard_map/ppermute | solution.py:32
  8.3 2.3 %collective-permute-start.4 = (bf16[48,2048]{1,0:T(8,128)(2,1)S(1)}, bf16[48,2048]{1,0:T(8,128)(2,1)S(1)}, u32[]{:S(2)}, u32[]{:S(2)}) collective-permute-start(bf16[48,2048]{1,0:T(8,128)(2,1)S(1)} %get-tuple-element.85.refs_0_), channel_id=1, source_target_pairs={{0,4},{2,6},{4,0},{6,2},{1,5},{3,7},{5,1},{7,3},{8,12},{10,14},{12... | collective-permute-start | bytes 589832 | tf_op jit(solution)/shard_map/ppermute | solution.py:32
  10.6 2.0 %collective-permute-start.3 = (bf16[48,2048]{1,0:T(8,128)(2,1)S(1)}, bf16[48,2048]{1,0:T(8,128)(2,1)S(1)}, u32[]{:S(2)}, u32[]{:S(2)}) collective-permute-start(bf16[48,2048]{1,0:T(8,128)(2,1)S(1)} %get-tuple-element.85.refs_0_), channel_id=1, source_target_pairs={{0,2},{2,0},{4,6},{6,4},{1,3},{3,1},{5,7},{7,5},{8,10},{10,8},{12,... | collective-permute-start | bytes 589832 | tf_op jit(solution)/shard_map/ppermute | solution.py:32
  12.6 1.3 fusion
  15.5 1.7 %reduce-window.6 = s32[8,2,3,128]{3,0,1,2:T(8,128)S(1)} reduce-window(s32[8,2,3,128]{3,0,1,2:T(8,128)S(1)} %copy_bitcast_fusion, s32[]{:T(128)} %constant.11.clone.1), window={size=1x1x1x128 pad=0_0x0_0x0_0x127_0}, to_apply=%region_1.2 | reduce-window | flops 780288 | bytes 49156 | tf_op jit(solution)/shard_map/reduce-window
  17.5 2.4 %collective-permute-done.4.refs_2_ = bf16[48,2048]{1,0:T(8,128)(2,1)S(1)} collective-permute-done((bf16[48,2048]{1,0:T(8,128)(2,1)S(1)}, bf16[48,2048]{1,0:T(8,128)(2,1)S(1)}, u32[]{:S(2)}, u32[]{:S(2)}) %collective-permute-start.4) | collective-permute-done | bytes 196640 | tf_op jit(solution)/shard_map/ppermute | solution.py:32
  19.9 2.1 %collective-permute-start.5 = (bf16[48,4096]{1,0:T(8,128)(2,1)S(1)}, bf16[48,4096]{1,0:T(8,128)(2,1)S(1)}, u32[]{:S(2)}, u32[]{:S(2)}) collective-permute-start(bf16[48,4096]{1,0:T(8,128)(2,1)S(1)} %get-tuple-element.45.refs_0_), channel_id=1, source_target_pairs={{0,2},{2,0},{4,6},{6,4},{1,3},{3,1},{5,7},{7,5},{8,10},{10,8},{12,... | collective-permute-start | bytes 1179656 | tf_op jit(solution)/shard_map/ppermute | solution.py:32
  22.0 1.6 %collective-permute-start.8 = (bf16[48,2048]{1,0:T(8,128)(2,1)S(1)}, bf16[48,2048]{1,0:T(8,128)(2,1)S(1)}, u32[]{:S(2)}, u32[]{:S(2)}) collective-permute-start(bf16[48,2048]{1,0:T(8,128)(2,1)S(1)} %collective-permute-done.4.refs_2_), channel_id=1, source_target_pairs={{0,1},{1,0},{2,3},{3,2},{4,5},{5,4},{6,7},{7,6},{8,9},{9,8},{10,11... | collective-permute-start | bytes 589832 | tf_op jit(solution)/shard_map/ppermute | solution.py:32
  24.1 3.6 %collective-permute-done.6.refs_3_ = bf16[48,2048]{1,0:T(8,128)(2,1)S(1)} collective-permute-done((bf16[48,2048]{1,0:T(8,128)(2,1)S(1)}, bf16[48,2048]{1,0:T(8,128)(2,1)S(1)}, u32[]{:S(2)}, u32[]{:S(2)}) %collective-permute-start.6) | collective-permute-done | bytes 196640 | tf_op jit(solution)/shard_map/ppermute | solution.py:32
  27.7 1.2 collective-permute-start.10
  28.9 1.5 %collective-permute-start.9 = (bf16[48,2048]{1,0:T(8,128)(2,1)S(1)}, bf16[48,2048]{1,0:T(8,128)(2,1)}, u32[]{:S(2)}, u32[]{:S(2)}) collective-permute-start(bf16[48,2048]{1,0:T(8,128)(2,1)S(1)} %collective-permute-done.6.refs_3_), channel_id=1, source_target_pairs={{0,1},{1,0},{2,3},{3,2},{4,5},{5,4},{6,7},{7,6},{8,9},{9,8},{10,11... | collective-permute-start | bytes 589832 | tf_op jit(solution)/shard_map/ppermute | solution.py:32
  30.8 4.3 %routing.1 = (bf16[896,384]{1,0:T(8,128)(2,1)S(1)}, bf16[896,384]{1,0:T(8,128)(2,1)S(1)}, bf16[384,896]{1,0:T(8,128)(2,1)S(1)}, bf16[384,896]{1,0:T(8,128)(2,1)S(1)}, f32[896,1]{1,0:T(8,128)S(1)}) custom-call(s32[16,384]{1,0:T(8,128)S(1)} %get-tuple-element.87.dest_ref, f32[16,384]{1,0:T(8,128)S(1)} %bitcast.77, s32[384,16]{1,0:T(8,128)S(1)} %copy.29.dest_col_ref, ...), custom_call_target="tpu_custom_call" | custom-call | bytes 2752512 | tf_op jit(solution)/shard_map/routing/pallas_call | solution.py:74
  35.1 6.6 %collective-permute-done.5.refs_1_ = bf16[48,4096]{1,0:T(8,128)(2,1)S(1)} collective-permute-done((bf16[48,4096]{1,0:T(8,128)(2,1)S(1)}, bf16[48,4096]{1,0:T(8,128)(2,1)S(1)}, u32[]{:S(2)}, u32[]{:S(2)}) %collective-permute-start.5) | collective-permute-done | bytes 393248 | tf_op jit(solution)/shard_map/ppermute | solution.py:32
  41.7 1.5 %collective-permute-start.12 = (bf16[48,4096]{1,0:T(8,128)(2,1)S(1)}, bf16[48,4096]{1,0:T(8,128)(2,1)S(1)}, u32[]{:S(2)}, u32[]{:S(2)}) collective-permute-start(bf16[48,4096]{1,0:T(8,128)(2,1)S(1)} %collective-permute-done.5.refs_1_), channel_id=1, source_target_pairs={{0,1},{1,0},{2,3},{3,2},{4,5},{5,4},{6,7},{7,6},{8,9},{9,8},{10,11... | collective-permute-start | bytes 1179656 | tf_op jit(solution)/shard_map/ppermute | solution.py:32
  43.2 3.8 %order_rows.2.rows_ref = bf16[896,2048]{1,0:T(8,128)(2,1)S(1)} custom-call(bf16[896,384]{1,0:T(8,128)(2,1)S(1)} %get-tuple-element.44.onehot_ref, bf16[48,2048]{1,0:T(8,128)(2,1)S(1)} %get-tuple-element.85.refs_0_, bf16[48,2048]{1,0:T(8,128)(2,1)S(1)} %collective-permute-done.3.refs_1_, bf16[48,2048]{1,0:T(8,128)(2,1)S(1)} %collective-permute-done.4.refs_2_, ...), custom_call_target="tpu_custom_call" | custom-call | flops 1409286144 | bytes 5242880 | tf_op jit(solution)/shard_map/order_rows/pallas_call | solution.py:119
  48.2 2.5 %collective-permute-start.11 = (bf16[48,4096]{1,0:T(8,128)(2,1)S(1)}, bf16[48,4096]{1,0:T(8,128)(2,1)S(1)}, u32[]{:S(2)}, u32[]{:S(2)}) collective-permute-start(bf16[48,4096]{1,0:T(8,128)(2,1)S(1)} %collective-permute-done.10.refs_2_), channel_id=1, source_target_pairs={{0,2},{2,0},{4,6},{6,4},{1,3},{3,1},{5,7},{7,5},{8,10},{10,8},{12,... | collective-permute-start | bytes 1179656 | tf_op jit(solution)/shard_map/ppermute | solution.py:32
  50.7 15.6 %forward_experts.1.rows_ref = bf16[896,2048]{1,0:T(8,128)(2,1)S(1)} custom-call(bf16[896,2048]{1,0:T(8,128)(2,1)S(1)} %order_rows.2.rows_ref, bf16[8,2048,384]{2,1,0:T(8,128)(2,1)} %bitcast.78, bf16[8,2048,384]{2,1,0:T(8,128)(2,1)} %bitcast.80, bf16[8,384,2048]{2,1,0:T(8,128)(2,1)} %bitcast.82), custom_call_target="tpu_custom_call" | custom-call | flops 4227858432 | bytes 37748736 | tf_op jit(solution)/shard_map/forward_experts/pallas_call | solution.py:205
  66.2 2.7 %token_sums.2 = (bf16[192,2048]{1,0:T(8,128)(2,1)S(1)}, bf16[192,2048]{1,0:T(8,128)(2,1)S(1)}) custom-call(bf16[384,896]{1,0:T(8,128)(2,1)S(1)} %get-tuple-element.51.mix_ref, bf16[896,2048]{1,0:T(8,128)(2,1)S(1)} %forward_experts.1.rows_ref), custom_call_target="tpu_custom_call" | custom-call | flops 1409286144 | bytes 5242880 | tf_op jit(solution)/shard_map/token_sums/pallas_call | solution.py:144
  69.5 6.0 %order_rows.3.rows_ref.grad_ref = bf16[896,4096]{1,0:T(8,128)(2,1)S(1)} custom-call(bf16[896,384]{1,0:T(8,128)(2,1)S(1)} %get-tuple-element.39.onehot_ref, f32[896,1]{1,0:T(8,128)S(1)} %get-tuple-element.40.slot_weight_ref, bf16[48,4096]{1,0:T(8,128)(2,1)S(1)} %get-tuple-element.45.refs_0_, bf16[48,4096]{1,0:T(8,128)(2,1)S(1)} %collective-permute-done.5.refs_1_, ...), custom_call_target="tpu_custom_call" | custom-call | flops 2818572288 | bytes 10485760 | tf_op jit(solution)/shard_map/order_rows/pallas_call | solution.py:119
  75.6 21.1 %backward_experts.1 = (bf16[896,384]{1,0:T(8,128)(2,1)S(1)}, bf16[896,384]{1,0:T(8,128)(2,1)S(1)}, bf16[896,384]{1,0:T(8,128)(2,1)S(1)}, bf16[896,2048]{1,0:T(8,128)(2,1)S(1)}) custom-call(bf16[896,4096]{1,0:T(8,128)(2,1)S(1)} %order_rows.3.rows_ref.grad_ref, bf16[896,4096]{1,0:T(8,128)(2,1)S(1)} %order_rows.3.rows_ref.grad_ref, ...), custom_call_target="tpu_custom_call" | custom-call | flops 7046430720 | bytes 37748736 | tf_op jit(solution)/shard_map/backward_experts/pallas_call | solution.py:224
  96.7 2.7 %token_sums.3 = (bf16[192,2048]{1,0:T(8,128)(2,1)S(1)}, bf16[192,2048]{1,0:T(8,128)(2,1)S(1)}) custom-call(bf16[384,896]{1,0:T(8,128)(2,1)S(1)} %get-tuple-element.49.mix_ref, bf16[896,2048]{1,0:T(8,128)(2,1)S(1)} %get-tuple-element.55.rows_ref), custom_call_target="tpu_custom_call" | custom-call | flops 1409286144 | bytes 5242880 | tf_op jit(solution)/shard_map/token_sums/pallas_call | solution.py:144
  99.4 1.6 %collective-permute-start.16 = (bf16[192,2048]{1,0:T(8,128)(2,1)S(1)}, bf16[192,2048]{1,0:T(8,128)(2,1)S(1)}, u32[]{:S(2)}, u32[]{:S(2)}) collective-permute-start(bf16[192,2048]{1,0:T(8,128)(2,1)S(1)} %get-tuple-element.60), channel_id=1, source_target_pairs={{0,1},{1,0},{2,3},{3,2},{4,5},{5,4},{6,7},{7,6},{8,9},{9,8},{10,11... | collective-permute-start | bytes 2359304 | tf_op jit(solution)/shard_map/ppermute | solution.py:32
  101.4 1.9 %collective-permute-start.19 = (bf16[48,2048]{1,0:T(8,128)(2,1)S(1)}, bf16[48,2048]{1,0:T(8,128)(2,1)S(1)}, u32[]{:S(2)}, u32[]{:S(2)}) collective-permute-start(bf16[48,2048]{1,0:T(8,128)(2,1)S(1)} %get-tuple-element.74), channel_id=1, source_target_pairs={{0,6},{2,4},{4,2},{6,0},{1,7},{3,5},{5,3},{7,1},{8,14},{10,12},{12... | collective-permute-start | bytes 589832 | tf_op jit(solution)/shard_map/ppermute | solution.py:32
  103.3 2.5 %collective-permute-start.17 = (bf16[48,2048]{1,0:T(8,128)(2,1)S(1)}, bf16[48,2048]{1,0:T(8,128)(2,1)S(1)}, u32[]{:S(2)}, u32[]{:S(2)}) collective-permute-start(bf16[48,2048]{1,0:T(8,128)(2,1)S(1)} %get-tuple-element.76), channel_id=1, source_target_pairs={{0,2},{2,0},{4,6},{6,4},{1,3},{3,1},{5,7},{7,5},{8,10},{10,8},{12,... | collective-permute-start | bytes 589832 | tf_op jit(solution)/shard_map/ppermute | solution.py:32
  105.8 14.3 %weight_grads.1 = (bf16[8,2048,384]{2,1,0:T(8,128)(2,1)}, bf16[8,2048,384]{2,1,0:T(8,128)(2,1)}, bf16[8,384,2048]{2,1,0:T(8,128)(2,1)}) custom-call(bf16[896,4096]{1,0:T(8,128)(2,1)S(1)} %order_rows.3.rows_ref.grad_ref, bf16[896,4096]{1,0:T(8,128)(2,1)S(1)} %order_rows.3.rows_ref.grad_ref, bf16[896,384]{1,0:T(8,128)(2,1)S(1)} %get-tuple-element.47.hidden_ref, ...), custom_call_target="tpu_custom_call" | custom-call | flops 4227858432 | bytes 37748736 | tf_op jit(solution)/shard_map/weight_grads/pallas_call | solution.py:242
  120.6 1.9 %collective-permute-start.24 = (bf16[48,2048]{1,0:T(8,128)(2,1)S(1)}, bf16[48,2048]{1,0:T(8,128)(2,1)S(1)}, u32[]{:S(2)}, u32[]{:S(2)}) collective-permute-start(bf16[48,2048]{1,0:T(8,128)(2,1)S(1)} %get-tuple-element.72), channel_id=1, source_target_pairs={{0,6},{2,4},{4,2},{6,0},{1,7},{3,5},{5,3},{7,1},{8,14},{10,12},{12... | collective-permute-start | bytes 589832 | tf_op jit(solution)/shard_map/ppermute | solution.py:32
  122.5 1.5 %collective-permute-start.23 = (bf16[48,2048]{1,0:T(8,128)(2,1)S(1)}, bf16[48,2048]{1,0:T(8,128)(2,1)S(1)}, u32[]{:S(2)}, u32[]{:S(2)}) collective-permute-start(bf16[48,2048]{1,0:T(8,128)(2,1)S(1)} %get-tuple-element.73), channel_id=1, source_target_pairs={{0,4},{2,6},{4,0},{6,2},{1,5},{3,7},{5,1},{7,3},{8,12},{10,14},{12... | collective-permute-start | bytes 589832 | tf_op jit(solution)/shard_map/ppermute | solution.py:32
  124.3 1.5 %collective-permute-start.20 = (bf16[48,2048]{1,0:T(8,128)(2,1)S(1)}, bf16[48,2048]{1,0:T(8,128)(2,1)S(1)}, u32[]{:S(2)}, u32[]{:S(2)}) collective-permute-start(bf16[48,2048]{1,0:T(8,128)(2,1)S(1)} %add_convert_fusion.2), channel_id=1, source_target_pairs={{0,8},{8,16},{16,24},{24,0},{1,9},{9,17},{17,25},{25,1},{2,10},{10... | collective-permute-start | bytes 589832 | tf_op jit(solution)/shard_map/ppermute | solution.py:27
  126.4 3.3 %collective-permute-done.24 = bf16[48,2048]{1,0:T(8,128)(2,1)S(1)} collective-permute-done((bf16[48,2048]{1,0:T(8,128)(2,1)S(1)}, bf16[48,2048]{1,0:T(8,128)(2,1)S(1)}, u32[]{:S(2)}, u32[]{:S(2)}) %collective-permute-start.24) | collective-permute-done | bytes 196640 | tf_op jit(solution)/shard_map/ppermute | solution.py:32
  129.7 7.0 %collective-permute-done.23 = bf16[48,2048]{1,0:T(8,128)(2,1)S(1)} collective-permute-done((bf16[48,2048]{1,0:T(8,128)(2,1)S(1)}, bf16[48,2048]{1,0:T(8,128)(2,1)S(1)}, u32[]{:S(2)}, u32[]{:S(2)}) %collective-permute-start.23) | collective-permute-done | bytes 196640 | tf_op jit(solution)/shard_map/ppermute | solution.py:32
  137.0 1.7 %collective-permute-start.25 = (bf16[48,2048]{1,0:T(8,128)(2,1)S(1)}, bf16[48,2048]{1,0:T(8,128)(2,1)S(1)}, u32[]{:S(2)}, u32[]{:S(2)}) collective-permute-start(bf16[48,2048]{1,0:T(8,128)(2,1)S(1)} %fusion.5), channel_id=1, source_target_pairs={{0,24},{8,0},{16,8},{24,16},{1,25},{9,1},{17,9},{25,17},{2,26},{10... | collective-permute-start | bytes 589832 | tf_op jit(solution)/shard_map/ppermute | solution.py:27
  139.5 4.7 %collective-permute-done.26 = bf16[48,2048]{1,0:T(8,128)(2,1)S(1)} collective-permute-done((bf16[48,2048]{1,0:T(8,128)(2,1)S(1)}, bf16[48,2048]{1,0:T(8,128)(2,1)S(1)}, u32[]{:S(2)}, u32[]{:S(2)}) %collective-permute-start.26) | collective-permute-done | bytes 196640 | tf_op jit(solution)/shard_map/ppermute | solution.py:303
  (64 shorter events, 10.3 us)
Async XLA Ops:
  2.6 11.3 %collective-permute-start.2 = (s32[96,32]{0,1:T(8,128)S(1)}, s32[96,32]{0,1:T(8,128)S(1)}, u32[]{:S(2)}, u32[]{:S(2)}) collective-permute-start(s32[96,32]{0,1:T(8,128)S(1)} %pad_add_fusion.1), channel_id=1, source_target_pairs={{0,6},{2,4},{4,2},{6,0},{1,7},{3,5},{5,3},{7,1},{8,14},{10,12},{12... | collective-permute-start | bytes 36872 | tf_op jit(solution)/shard_map/ppermute | solution.py:32
  7.7 7.5 %collective-permute-start.1 = (s32[96,32]{0,1:T(8,128)S(1)}, s32[96,32]{0,1:T(8,128)S(1)}, u32[]{:S(2)}, u32[]{:S(2)}) collective-permute-start(s32[96,32]{0,1:T(8,128)S(1)} %pad_add_fusion.1), channel_id=1, source_target_pairs={{0,4},{2,6},{4,0},{6,2},{1,5},{3,7},{5,1},{7,3},{8,12},{10,14},{12... | collective-permute-start | bytes 36872 | tf_op jit(solution)/shard_map/ppermute | solution.py:32
  7.7 7.6 %collective-permute-start = (s32[96,32]{0,1:T(8,128)S(1)}, s32[96,32]{0,1:T(8,128)S(1)}, u32[]{:S(2)}, u32[]{:S(2)}) collective-permute-start(s32[96,32]{0,1:T(8,128)S(1)} %pad_add_fusion.1), channel_id=1, source_target_pairs={{0,2},{2,0},{4,6},{6,4},{1,3},{3,1},{5,7},{7,5},{8,10},{10,8},{12,... | collective-permute-start | bytes 36872 | tf_op jit(solution)/shard_map/ppermute | solution.py:32
  8.3 11.6 %collective-permute-start.4 = (bf16[48,2048]{1,0:T(8,128)(2,1)S(1)}, bf16[48,2048]{1,0:T(8,128)(2,1)S(1)}, u32[]{:S(2)}, u32[]{:S(2)}) collective-permute-start(bf16[48,2048]{1,0:T(8,128)(2,1)S(1)} %get-tuple-element.85.refs_0_), channel_id=1, source_target_pairs={{0,4},{2,6},{4,0},{6,2},{1,5},{3,7},{5,1},{7,3},{8,12},{10,14},{12... | collective-permute-start | bytes 589832 | tf_op jit(solution)/shard_map/ppermute | solution.py:32
  10.6 9.4 %collective-permute-start.3 = (bf16[48,2048]{1,0:T(8,128)(2,1)S(1)}, bf16[48,2048]{1,0:T(8,128)(2,1)S(1)}, u32[]{:S(2)}, u32[]{:S(2)}) collective-permute-start(bf16[48,2048]{1,0:T(8,128)(2,1)S(1)} %get-tuple-element.85.refs_0_), channel_id=1, source_target_pairs={{0,2},{2,0},{4,6},{6,4},{1,3},{3,1},{5,7},{7,5},{8,10},{10,8},{12,... | collective-permute-start | bytes 589832 | tf_op jit(solution)/shard_map/ppermute | solution.py:32
  19.9 7.8 %collective-permute-start.6 = (bf16[48,2048]{1,0:T(8,128)(2,1)S(1)}, bf16[48,2048]{1,0:T(8,128)(2,1)S(1)}, u32[]{:S(2)}, u32[]{:S(2)}) collective-permute-start(bf16[48,2048]{1,0:T(8,128)(2,1)S(1)} %collective-permute-done.4.refs_2_), channel_id=1, source_target_pairs={{0,2},{2,0},{4,6},{6,4},{1,3},{3,1},{5,7},{7,5},{8,10},{10,8},{12,... | collective-permute-start | bytes 589832 | tf_op jit(solution)/shard_map/ppermute | solution.py:32
  19.9 21.8 %collective-permute-start.5 = (bf16[48,4096]{1,0:T(8,128)(2,1)S(1)}, bf16[48,4096]{1,0:T(8,128)(2,1)S(1)}, u32[]{:S(2)}, u32[]{:S(2)}) collective-permute-start(bf16[48,4096]{1,0:T(8,128)(2,1)S(1)} %get-tuple-element.45.refs_0_), channel_id=1, source_target_pairs={{0,2},{2,0},{4,6},{6,4},{1,3},{3,1},{5,7},{7,5},{8,10},{10,8},{12,... | collective-permute-start | bytes 1179656 | tf_op jit(solution)/shard_map/ppermute | solution.py:32
  22.0 21.2 %collective-permute-start.8 = (bf16[48,2048]{1,0:T(8,128)(2,1)S(1)}, bf16[48,2048]{1,0:T(8,128)(2,1)S(1)}, u32[]{:S(2)}, u32[]{:S(2)}) collective-permute-start(bf16[48,2048]{1,0:T(8,128)(2,1)S(1)} %collective-permute-done.4.refs_2_), channel_id=1, source_target_pairs={{0,1},{1,0},{2,3},{3,2},{4,5},{5,4},{6,7},{7,6},{8,9},{9,8},{10,11... | collective-permute-start | bytes 589832 | tf_op jit(solution)/shard_map/ppermute | solution.py:32
  23.6 19.6 %collective-permute-start.7 = (bf16[48,2048]{1,0:T(8,128)(2,1)S(1)}, bf16[48,2048]{1,0:T(8,128)(2,1)S(1)}, u32[]{:S(2)}, u32[]{:S(2)}) collective-permute-start(bf16[48,2048]{1,0:T(8,128)(2,1)S(1)} %collective-permute-done.3.refs_1_), channel_id=1, source_target_pairs={{0,1},{1,0},{2,3},{3,2},{4,5},{5,4},{6,7},{7,6},{8,9},{9,8},{10,11... | collective-permute-start | bytes 589832 | tf_op jit(solution)/shard_map/ppermute | solution.py:32
  27.7 19.4 %collective-permute-start.10 = (bf16[48,4096]{1,0:T(8,128)(2,1)S(1)}, bf16[48,4096]{1,0:T(8,128)(2,1)S(1)}, u32[]{:S(2)}, u32[]{:S(2)}) collective-permute-start(bf16[48,4096]{1,0:T(8,128)(2,1)S(1)} %get-tuple-element.45.refs_0_), channel_id=1, source_target_pairs={{0,4},{2,6},{4,0},{6,2},{1,5},{3,7},{5,1},{7,3},{8,12},{10,14},{12... | collective-permute-start | bytes 1179656 | tf_op jit(solution)/shard_map/ppermute | solution.py:32
  28.9 14.3 %collective-permute-start.9 = (bf16[48,2048]{1,0:T(8,128)(2,1)S(1)}, bf16[48,2048]{1,0:T(8,128)(2,1)}, u32[]{:S(2)}, u32[]{:S(2)}) collective-permute-start(bf16[48,2048]{1,0:T(8,128)(2,1)S(1)} %collective-permute-done.6.refs_3_), channel_id=1, source_target_pairs={{0,1},{1,0},{2,3},{3,2},{4,5},{5,4},{6,7},{7,6},{8,9},{9,8},{10,11... | collective-permute-start | bytes 589832 | tf_op jit(solution)/shard_map/ppermute | solution.py:32
  41.7 27.8 %collective-permute-start.12 = (bf16[48,4096]{1,0:T(8,128)(2,1)S(1)}, bf16[48,4096]{1,0:T(8,128)(2,1)S(1)}, u32[]{:S(2)}, u32[]{:S(2)}) collective-permute-start(bf16[48,4096]{1,0:T(8,128)(2,1)S(1)} %collective-permute-done.5.refs_1_), channel_id=1, source_target_pairs={{0,1},{1,0},{2,3},{3,2},{4,5},{5,4},{6,7},{7,6},{8,9},{9,8},{10,11... | collective-permute-start | bytes 1179656 | tf_op jit(solution)/shard_map/ppermute | solution.py:32
  47.1 21.8 %collective-permute-start.14 = (bf16[48,4096]{1,0:T(8,128)(2,1)S(1)}, bf16[48,4096]{1,0:T(8,128)(2,1)S(1)}, u32[]{:S(2)}, u32[]{:S(2)}) collective-permute-start(bf16[48,4096]{1,0:T(8,128)(2,1)S(1)} %collective-permute-done.10.refs_2_), channel_id=1, source_target_pairs={{0,3},{1,2},{2,1},{3,0},{4,7},{5,6},{6,5},{7,4},{8,11},{9,10},{10,... | collective-permute-start | bytes 1179656 | tf_op jit(solution)/shard_map/ppermute | solution.py:268
  47.2 22.3 %collective-permute-start.13 = (bf16[48,4096]{1,0:T(8,128)(2,1)S(1)}, bf16[48,4096]{1,0:T(8,128)(2,1)S(1)}, u32[]{:S(2)}, u32[]{:S(2)}) collective-permute-start(bf16[48,4096]{1,0:T(8,128)(2,1)S(1)} %collective-permute-done.10.refs_2_), channel_id=1, source_target_pairs={{0,1},{1,0},{2,3},{3,2},{4,5},{5,4},{6,7},{7,6},{8,9},{9,8},{10,11... | collective-permute-start | bytes 1179656 | tf_op jit(solution)/shard_map/ppermute | solution.py:32
  48.2 21.3 %collective-permute-start.11 = (bf16[48,4096]{1,0:T(8,128)(2,1)S(1)}, bf16[48,4096]{1,0:T(8,128)(2,1)S(1)}, u32[]{:S(2)}, u32[]{:S(2)}) collective-permute-start(bf16[48,4096]{1,0:T(8,128)(2,1)S(1)} %collective-permute-done.10.refs_2_), channel_id=1, source_target_pairs={{0,2},{2,0},{4,6},{6,4},{1,3},{3,1},{5,7},{7,5},{8,10},{10,8},{12,... | collective-permute-start | bytes 1179656 | tf_op jit(solution)/shard_map/ppermute | solution.py:32
  69.0 27.8 %collective-permute-start.15 = (bf16[192,2048]{1,0:T(8,128)(2,1)S(1)}, bf16[192,2048]{1,0:T(8,128)(2,1)S(1)}, u32[]{:S(2)}, u32[]{:S(2)}) collective-permute-start(bf16[192,2048]{1,0:T(8,128)(2,1)S(1)} %get-tuple-element.54), channel_id=1, source_target_pairs={{0,1},{1,0},{2,3},{3,2},{4,5},{5,4},{6,7},{7,6},{8,9},{9,8},{10,11... | collective-permute-start | bytes 2359304 | tf_op jit(solution)/shard_map/ppermute | solution.py:32
  99.4 20.7 %collective-permute-start.16 = (bf16[192,2048]{1,0:T(8,128)(2,1)S(1)}, bf16[192,2048]{1,0:T(8,128)(2,1)S(1)}, u32[]{:S(2)}, u32[]{:S(2)}) collective-permute-start(bf16[192,2048]{1,0:T(8,128)(2,1)S(1)} %get-tuple-element.60), channel_id=1, source_target_pairs={{0,1},{1,0},{2,3},{3,2},{4,5},{5,4},{6,7},{7,6},{8,9},{9,8},{10,11... | collective-permute-start | bytes 2359304 | tf_op jit(solution)/shard_map/ppermute | solution.py:32
  101.4 18.8 %collective-permute-start.19 = (bf16[48,2048]{1,0:T(8,128)(2,1)S(1)}, bf16[48,2048]{1,0:T(8,128)(2,1)S(1)}, u32[]{:S(2)}, u32[]{:S(2)}) collective-permute-start(bf16[48,2048]{1,0:T(8,128)(2,1)S(1)} %get-tuple-element.74), channel_id=1, source_target_pairs={{0,6},{2,4},{4,2},{6,0},{1,7},{3,5},{5,3},{7,1},{8,14},{10,12},{12... | collective-permute-start | bytes 589832 | tf_op jit(solution)/shard_map/ppermute | solution.py:32
  103.3 16.9 %collective-permute-start.18 = (bf16[48,2048]{1,0:T(8,128)(2,1)S(1)}, bf16[48,2048]{1,0:T(8,128)(2,1)S(1)}, u32[]{:S(2)}, u32[]{:S(2)}) collective-permute-start(bf16[48,2048]{1,0:T(8,128)(2,1)S(1)} %get-tuple-element.75), channel_id=1, source_target_pairs={{0,4},{2,6},{4,0},{6,2},{1,5},{3,7},{5,1},{7,3},{8,12},{10,14},{12... | collective-permute-start | bytes 589832 | tf_op jit(solution)/shard_map/ppermute | solution.py:32
  103.3 16.9 %collective-permute-start.17 = (bf16[48,2048]{1,0:T(8,128)(2,1)S(1)}, bf16[48,2048]{1,0:T(8,128)(2,1)S(1)}, u32[]{:S(2)}, u32[]{:S(2)}) collective-permute-start(bf16[48,2048]{1,0:T(8,128)(2,1)S(1)} %get-tuple-element.76), channel_id=1, source_target_pairs={{0,2},{2,0},{4,6},{6,4},{1,3},{3,1},{5,7},{7,5},{8,10},{10,8},{12,... | collective-permute-start | bytes 589832 | tf_op jit(solution)/shard_map/ppermute | solution.py:32
  120.2 16.6 %copy-start = (bf16[1,96,2048]{2,1,0:T(8,128)(2,1)S(1)}, bf16[1,96,2048]{2,1,0:T(8,128)(2,1)}, u32[]{:S(2)}) copy-start(bf16[1,96,2048]{2,1,0:T(8,128)(2,1)} %param.16) | copy-start | bytes 1179652
  120.5 5.9 %collective-permute-start.22 = (bf16[48,2048]{1,0:T(8,128)(2,1)S(1)}, bf16[48,2048]{1,0:T(8,128)(2,1)S(1)}, u32[]{:S(2)}, u32[]{:S(2)}) collective-permute-start(bf16[48,2048]{1,0:T(8,128)(2,1)S(1)} %get-tuple-element.71), channel_id=1, source_target_pairs={{0,2},{2,0},{4,6},{6,4},{1,3},{3,1},{5,7},{7,5},{8,10},{10,8},{12,... | collective-permute-start | bytes 589832 | tf_op jit(solution)/shard_map/ppermute | solution.py:32
  120.6 9.2 %collective-permute-start.24 = (bf16[48,2048]{1,0:T(8,128)(2,1)S(1)}, bf16[48,2048]{1,0:T(8,128)(2,1)S(1)}, u32[]{:S(2)}, u32[]{:S(2)}) collective-permute-start(bf16[48,2048]{1,0:T(8,128)(2,1)S(1)} %get-tuple-element.72), channel_id=1, source_target_pairs={{0,6},{2,4},{4,2},{6,0},{1,7},{3,5},{5,3},{7,1},{8,14},{10,12},{12... | collective-permute-start | bytes 589832 | tf_op jit(solution)/shard_map/ppermute | solution.py:32
  122.5 14.3 %collective-permute-start.23 = (bf16[48,2048]{1,0:T(8,128)(2,1)S(1)}, bf16[48,2048]{1,0:T(8,128)(2,1)S(1)}, u32[]{:S(2)}, u32[]{:S(2)}) collective-permute-start(bf16[48,2048]{1,0:T(8,128)(2,1)S(1)} %get-tuple-element.73), channel_id=1, source_target_pairs={{0,4},{2,6},{4,0},{6,2},{1,5},{3,7},{5,1},{7,3},{8,12},{10,14},{12... | collective-permute-start | bytes 589832 | tf_op jit(solution)/shard_map/ppermute | solution.py:32
  124.2 14.5 %collective-permute-start.21 = (bf16[48,2048]{1,0:T(8,128)(2,1)S(1)}, bf16[48,2048]{1,0:T(8,128)(2,1)S(1)}, u32[]{:S(2)}, u32[]{:S(2)}) collective-permute-start(bf16[48,2048]{1,0:T(8,128)(2,1)S(1)} %add_convert_fusion.2), channel_id=1, source_target_pairs={{0,9},{1,8},{8,17},{9,16},{16,25},{17,24},{24,1},{25,0},{2,11},{3,... | collective-permute-start | bytes 589832 | tf_op jit(solution)/shard_map/ppermute | solution.py:303
  124.3 14.4 %collective-permute-start.20 = (bf16[48,2048]{1,0:T(8,128)(2,1)S(1)}, bf16[48,2048]{1,0:T(8,128)(2,1)S(1)}, u32[]{:S(2)}, u32[]{:S(2)}) collective-permute-start(bf16[48,2048]{1,0:T(8,128)(2,1)S(1)} %add_convert_fusion.2), channel_id=1, source_target_pairs={{0,8},{8,16},{16,24},{24,0},{1,9},{9,17},{17,25},{25,1},{2,10},{10... | collective-permute-start | bytes 589832 | tf_op jit(solution)/shard_map/ppermute | solution.py:27
  136.9 7.2 %collective-permute-start.26 = (bf16[48,2048]{1,0:T(8,128)(2,1)S(1)}, bf16[48,2048]{1,0:T(8,128)(2,1)S(1)}, u32[]{:S(2)}, u32[]{:S(2)}) collective-permute-start(bf16[48,2048]{1,0:T(8,128)(2,1)S(1)} %fusion.5), channel_id=1, source_target_pairs={{0,25},{1,24},{8,1},{9,0},{16,9},{17,8},{24,17},{25,16},{2,27},{3,... | collective-permute-start | bytes 589832 | tf_op jit(solution)/shard_map/ppermute | solution.py:303
  137.0 7.2 %collective-permute-start.25 = (bf16[48,2048]{1,0:T(8,128)(2,1)S(1)}, bf16[48,2048]{1,0:T(8,128)(2,1)S(1)}, u32[]{:S(2)}, u32[]{:S(2)}) collective-permute-start(bf16[48,2048]{1,0:T(8,128)(2,1)S(1)} %fusion.5), channel_id=1, source_target_pairs={{0,24},{8,0},{16,8},{24,16},{1,25},{9,1},{17,9},{25,17},{2,26},{10... | collective-permute-start | bytes 589832 | tf_op jit(solution)/shard_map/ppermute | solution.py:27

commit v4 on v3

--- a/solution.py
+++ b/solution.py
@@ -105,7 +105,7 @@
 def in_expert_order(onehot, pieces, slot_weight=None):
     total, tokens = onehot.shape
     width = pieces[0].shape[1]
-    chunk = min(512, width)
+    chunk = min(2048 if tokens <= 512 else 512, width)
     steps = width // chunk
     in_specs = [pl.BlockSpec((total, tokens), lambda c: (0, 0))]
     operands = [onehot]
@@ -139,7 +139,7 @@
 def token_sums(mix, rows, part, parts):
     tokens, total = mix.shape
     width = rows.shape[1] // parts
-    chunk = min(512, width)
+    chunk = min(2048 if tokens <= 512 else 512, width)
     steps = width // chunk
     return pl.pallas_call(
         combine_kernel,
@@ -178,7 +178,11 @@
     gate_grad = (hidden_grad * up_value * sig * (1.0 + gate_value * (1.0 - sig))).astype(BF16)
     up_grad_ref[...] = up_grad
     gate_grad_ref[...] = gate_grad
-    out_ref[...] = (dot(gate_grad, gate_ref[0], NT) + dot(up_grad, up_ref[0], NT)).astype(BF16)
+    width = out_ref.shape[1]
+    for at in range(0, width, 512):
+        part = slice(at, min(at + 512, width))
+        row_grad = dot(gate_grad, gate_ref[0, part], NT) + dot(up_grad, up_ref[0, part], NT)
+        out_ref[:, part] = row_grad.astype(BF16)
 
 
 def weights_kernel(
@@ -331,13 +335,13 @@
 
     meta = jnp.concatenate([fwd_routes[0], fwd_numer[0], bwd_routes[0], bwd_numer[0]], -1)
     in_mine, in_other = halves(fwd_in[0], dp_index)
-    meta_all = spread_meta(after(meta, in_mine), dp_index, groups)
+    back_mine, back_other = halves(jnp.concatenate([bwd_saved[0], bwd_grad[0]], 1), dp_index)
+    meta_all = spread_meta(after(meta, back_mine), dp_index, groups)
     dest, weight = slot_tables(meta_all, choices, group * n_local, n_local)
     grad_mine, _ = halves(bwd_grad[0], dp_index)
-    back_mine, back_other = halves(jnp.concatenate([bwd_saved[0], bwd_grad[0]], 1), dp_index)
 
     if groups == 4:
-        near, past = swap(in_mine, "expert", 1), swap(in_mine, "expert", 2)
+        near, past = swap(in_mine, "expert", 1), swap(after(in_mine, back_mine), "expert", 2)
         back_near = swap(after(back_mine, near, past), "expert", 1)
         last = swap(past, "expert", 1)
         far = [swap(near, "dp", 1), swap(past, "dp", 1), swap(last, "dp", 1)]

time: 145 us -> 140 us (0.966)
  Pallas kernels: 70.6 us -> 66.1 us
  waiting for transfers between devices: 29.5 us -> 27.9 us
    ppermute x22, starting transfers between devices: 32.1 us -> 29.6 us  [swap(): return lax.ppermute(block, axis, [(i, i ^ mask) for i in range(n)])]
    ppermute x2, starting transfers between devices: 3.22 us -> 5.27 us  [rotate(): lax.ppermute(block, axis, [(i, (i + distance) % n) for i in range(n)])]
    pallas_call x2, Pallas kernels: 9.89 us -> 7.91 us  [in_expert_order(): pl.pallas_call(kernel, grid=(steps,), in_specs=in_specs, out_specs=pl.Blo...]
    pallas_call x2, Pallas kernels: 5.4 us -> 3.57 us  [token_sums(): pl.pallas_call(combine_kernel, grid=(steps,), in_specs=[pl.BlockSpec((tok...]
  transfers between devices with their start and end apart: 27 -> 27, of which waited for: 8 -> 7; matrix products, arithmetic and copies ran while one was open for 4% -> 4% of each run, Pallas kernels for 47% -> 46%
where the time goes in v4:
time: 140 us; the launch traced here: 139 us
  Pallas kernels  66.1 us (47%)
  starting transfers between devices  35.9 us (26%)
  waiting for transfers between devices  27.9 us (20%)
  other arithmetic  6.39 us (5%)
  local copies, waits for them, and re-layouts  2.07 us (1%)
    ppermute x22, starting transfers between devices, swap(): return lax.ppermute(block, axis, [(i, i ^ mask) for i in range(n)])  29.6 us
    ppermute x22, waiting for transfers between devices, swap(): return lax.ppermute(block, axis, [(i, i ^ mask) for i in range(n)])  24.2 us
    pallas_call x1, Pallas kernels, backward_experts(): pl.pallas_call(backward_kernel, grid=(local,), in_specs=[wide, grad_wide,...  20.5 us
    pallas_call x1, Pallas kernels, forward_experts(): pl.pallas_call(forward_kernel, grid=(local,), in_specs=[wide, column, col...  15.5 us
    pallas_call x1, Pallas kernels, weight_grads(): pl.pallas_call(weights_kernel, grid=(local,), in_specs=[wide, grad_wide,...  14.3 us
    pallas_call x2, Pallas kernels, in_expert_order(): pl.pallas_call(kernel, grid=(steps,), in_specs=in_specs, out_specs=pl.Blo...  7.91 us
    ppermute x2, starting transfers between devices, rotate(): lax.ppermute(block, axis, [(i, (i + distance) % n) for i in range(n)])  5.27 us
    pallas_call x1, Pallas kernels, routing_matrices(): pl.pallas_call(functools.partial(routing_kernel, slots), out_shape=[jax.S...  4.32 us
  transfers between devices with their start and end apart: 27, of which 7 were waited for; matrix products, arithmetic and copies ran while one was open for 4% of the time, Pallas kernels for 46%

profile of v4, /device:TPU:0, one launch (start us, length us, event | category | flops | bytes accessed | tf_op | source)
XLA Modules:
  0.0 139.3 jit_solution(11550507777639261588)
XLA Ops:
  1.4 1.3 fusion
  2.8 5.1 %collective-permute-start.2 = (s32[96,32]{0,1:T(8,128)S(1)}, s32[96,32]{0,1:T(8,128)S(1)}, u32[]{:S(2)}, u32[]{:S(2)}) collective-permute-start(s32[96,32]{0,1:T(8,128)S(1)} %pad_add_fusion.1), channel_id=1, source_target_pairs={{0,6},{2,4},{4,2},{6,0},{1,7},{3,5},{5,3},{7,1},{8,14},{10,12},{12... | collective-permute-start | bytes 36872 | tf_op jit(solution)/shard_map/ppermute | solution.py:32
  8.5 1.0 dynamic-slice_bitcast_fusion
  9.6 1.5 %collective-permute-start.3 = (bf16[48,2048]{1,0:T(8,128)(2,1)S(1)}, bf16[48,2048]{1,0:T(8,128)(2,1)S(1)}, u32[]{:S(2)}, u32[]{:S(2)}) collective-permute-start(bf16[48,2048]{1,0:T(8,128)(2,1)S(1)} %get-tuple-element.43.refs_0_), channel_id=1, source_target_pairs={{0,2},{2,0},{4,6},{6,4},{1,3},{3,1},{5,7},{7,5},{8,10},{10,8},{12,... | collective-permute-start | bytes 589832 | tf_op jit(solution)/shard_map/ppermute | solution.py:32
  11.0 3.0 %collective-permute-start.4 = (bf16[48,2048]{1,0:T(8,128)(2,1)S(1)}, bf16[48,2048]{1,0:T(8,128)(2,1)S(1)}, u32[]{:S(2)}, u32[]{:S(2)}) collective-permute-start(bf16[48,2048]{1,0:T(8,128)(2,1)S(1)} %get-tuple-element.43.refs_0_), channel_id=1, source_target_pairs={{0,4},{2,6},{4,0},{6,2},{1,5},{3,7},{5,1},{7,3},{8,12},{10,14},{12... | collective-permute-start | bytes 589832 | tf_op jit(solution)/shard_map/ppermute | solution.py:32
  14.4 1.7 %reduce-window.6 = s32[8,2,3,128]{3,0,1,2:T(8,128)S(1)} reduce-window(s32[8,2,3,128]{3,0,1,2:T(8,128)S(1)} %copy_bitcast_fusion, s32[]{:T(128)} %constant.11.clone.1), window={size=1x1x1x128 pad=0_0x0_0x0_0x127_0}, to_apply=%region_1.2 | reduce-window | flops 780288 | bytes 49156 | tf_op jit(solution)/shard_map/reduce-window
  16.4 5.7 %collective-permute-done.4.refs_2_ = bf16[48,2048]{1,0:T(8,128)(2,1)S(1)} collective-permute-done((bf16[48,2048]{1,0:T(8,128)(2,1)S(1)}, bf16[48,2048]{1,0:T(8,128)(2,1)S(1)}, u32[]{:S(2)}, u32[]{:S(2)}) %collective-permute-start.4) | collective-permute-done | bytes 196640 | tf_op jit(solution)/shard_map/ppermute | solution.py:32
  22.6 1.7 %collective-permute-start.5 = (bf16[48,4096]{1,0:T(8,128)(2,1)S(1)}, bf16[48,4096]{1,0:T(8,128)(2,1)S(1)}, u32[]{:S(2)}, u32[]{:S(2)}) collective-permute-start(bf16[48,4096]{1,0:T(8,128)(2,1)S(1)} %get-tuple-element.47.refs_0_), channel_id=1, source_target_pairs={{0,2},{2,0},{4,6},{6,4},{1,3},{3,1},{5,7},{7,5},{8,10},{10,8},{12,... | collective-permute-start | bytes 1179656 | tf_op jit(solution)/shard_map/ppermute | solution.py:32
  24.3 1.6 %collective-permute-start.7 = (bf16[48,2048]{1,0:T(8,128)(2,1)S(1)}, bf16[48,2048]{1,0:T(8,128)(2,1)S(1)}, u32[]{:S(2)}, u32[]{:S(2)}) collective-permute-start(bf16[48,2048]{1,0:T(8,128)(2,1)S(1)} %collective-permute-done.3.refs_1_), channel_id=1, source_target_pairs={{0,1},{1,0},{2,3},{3,2},{4,5},{5,4},{6,7},{7,6},{8,9},{9,8},{10,11... | collective-permute-start | bytes 589832 | tf_op jit(solution)/shard_map/ppermute | solution.py:32
  26.4 7.8 %collective-permute-done.6.refs_3_ = bf16[48,2048]{1,0:T(8,128)(2,1)S(1)} collective-permute-done((bf16[48,2048]{1,0:T(8,128)(2,1)S(1)}, bf16[48,2048]{1,0:T(8,128)(2,1)S(1)}, u32[]{:S(2)}, u32[]{:S(2)}) %collective-permute-start.6) | collective-permute-done | bytes 196640 | tf_op jit(solution)/shard_map/ppermute | solution.py:32
  34.7 1.5 %collective-permute-start.9 = (bf16[48,2048]{1,0:T(8,128)(2,1)S(1)}, bf16[48,2048]{1,0:T(8,128)(2,1)}, u32[]{:S(2)}, u32[]{:S(2)}) collective-permute-start(bf16[48,2048]{1,0:T(8,128)(2,1)S(1)} %collective-permute-done.6.refs_3_), channel_id=1, source_target_pairs={{0,1},{1,0},{2,3},{3,2},{4,5},{5,4},{6,7},{7,6},{8,9},{9,8},{10,11... | collective-permute-start | bytes 589832 | tf_op jit(solution)/shard_map/ppermute | solution.py:32
  36.5 4.3 %routing.1 = (bf16[896,384]{1,0:T(8,128)(2,1)S(1)}, bf16[896,384]{1,0:T(8,128)(2,1)S(1)}, bf16[384,896]{1,0:T(8,128)(2,1)S(1)}, bf16[384,896]{1,0:T(8,128)(2,1)S(1)}, f32[896,1]{1,0:T(8,128)S(1)}) custom-call(s32[16,384]{1,0:T(8,128)S(1)} %get-tuple-element.89.dest_ref, f32[16,384]{1,0:T(8,128)S(1)} %bitcast.77, s32[384,16]{1,0:T(8,128)S(1)} %copy.29.dest_col_ref, ...), custom_call_target="tpu_custom_call" | custom-call | bytes 2752512 | tf_op jit(solution)/shard_map/routing/pallas_call | solution.py:74
  41.4 1.1 collective-permute-done.9.refs_7_
  42.5 3.0 %order_rows.2.rows_ref = bf16[896,2048]{1,0:T(8,128)(2,1)S(1)} custom-call(bf16[896,384]{1,0:T(8,128)(2,1)S(1)} %get-tuple-element.46.onehot_ref, bf16[48,2048]{1,0:T(8,128)(2,1)S(1)} %get-tuple-element.43.refs_0_, bf16[48,2048]{1,0:T(8,128)(2,1)S(1)} %collective-permute-done.3.refs_1_, bf16[48,2048]{1,0:T(8,128)(2,1)S(1)} %collective-permute-done.4.refs_2_, ...), custom_call_target="tpu_custom_call" | custom-call | flops 1409286144 | bytes 5242880 | tf_op jit(solution)/shard_map/order_rows/pallas_call | solution.py:119
  45.5 2.4 %collective-permute-done.10.refs_2_ = bf16[48,4096]{1,0:T(8,128)(2,1)S(1)} collective-permute-done((bf16[48,4096]{1,0:T(8,128)(2,1)S(1)}, bf16[48,4096]{1,0:T(8,128)(2,1)S(1)}, u32[]{:S(2)}, u32[]{:S(2)}) %collective-permute-start.10) | collective-permute-done | bytes 393248 | tf_op jit(solution)/shard_map/ppermute | solution.py:32
  47.9 0.9 collective-permute-start.14
  49.4 2.0 %collective-permute-start.11 = (bf16[48,4096]{1,0:T(8,128)(2,1)S(1)}, bf16[48,4096]{1,0:T(8,128)(2,1)S(1)}, u32[]{:S(2)}, u32[]{:S(2)}) collective-permute-start(bf16[48,4096]{1,0:T(8,128)(2,1)S(1)} %collective-permute-done.10.refs_2_), channel_id=1, source_target_pairs={{0,2},{2,0},{4,6},{6,4},{1,3},{3,1},{5,7},{7,5},{8,10},{10,8},{12,... | collective-permute-start | bytes 1179656 | tf_op jit(solution)/shard_map/ppermute | solution.py:32
  51.4 15.5 %forward_experts.1.rows_ref = bf16[896,2048]{1,0:T(8,128)(2,1)S(1)} custom-call(bf16[896,2048]{1,0:T(8,128)(2,1)S(1)} %order_rows.2.rows_ref, bf16[8,2048,384]{2,1,0:T(8,128)(2,1)} %bitcast.78, bf16[8,2048,384]{2,1,0:T(8,128)(2,1)} %bitcast.80, bf16[8,384,2048]{2,1,0:T(8,128)(2,1)} %bitcast.82), custom_call_target="tpu_custom_call" | custom-call | flops 4227858432 | bytes 37748736 | tf_op jit(solution)/shard_map/forward_experts/pallas_call | solution.py:209
  66.9 1.8 %token_sums.2 = (bf16[192,2048]{1,0:T(8,128)(2,1)S(1)}, bf16[192,2048]{1,0:T(8,128)(2,1)S(1)}) custom-call(bf16[384,896]{1,0:T(8,128)(2,1)S(1)} %get-tuple-element.53.mix_ref, bf16[896,2048]{1,0:T(8,128)(2,1)S(1)} %forward_experts.1.rows_ref), custom_call_target="tpu_custom_call" | custom-call | flops 1409286144 | bytes 5242880 | tf_op jit(solution)/shard_map/token_sums/pallas_call | solution.py:144
  68.7 1.6 %collective-permute-start.15 = (bf16[192,2048]{1,0:T(8,128)(2,1)S(1)}, bf16[192,2048]{1,0:T(8,128)(2,1)S(1)}, u32[]{:S(2)}, u32[]{:S(2)}) collective-permute-start(bf16[192,2048]{1,0:T(8,128)(2,1)S(1)} %get-tuple-element.56), channel_id=1, source_target_pairs={{0,1},{1,0},{2,3},{3,2},{4,5},{5,4},{6,7},{7,6},{8,9},{9,8},{10,11... | collective-permute-start | bytes 2359304 | tf_op jit(solution)/shard_map/ppermute | solution.py:32
  70.3 4.9 %order_rows.3.rows_ref.grad_ref = bf16[896,4096]{1,0:T(8,128)(2,1)S(1)} custom-call(bf16[896,384]{1,0:T(8,128)(2,1)S(1)} %get-tuple-element.40.onehot_ref, f32[896,1]{1,0:T(8,128)S(1)} %get-tuple-element.41.slot_weight_ref, bf16[48,4096]{1,0:T(8,128)(2,1)S(1)} %get-tuple-element.47.refs_0_, bf16[48,4096]{1,0:T(8,128)(2,1)S(1)} %collective-permute-done.5.refs_1_, ...), custom_call_target="tpu_custom_call" | custom-call | flops 2818572288 | bytes 10485760 | tf_op jit(solution)/shard_map/order_rows/pallas_call | solution.py:119
  75.2 20.5 %backward_experts.1 = (bf16[896,384]{1,0:T(8,128)(2,1)S(1)}, bf16[896,384]{1,0:T(8,128)(2,1)S(1)}, bf16[896,384]{1,0:T(8,128)(2,1)S(1)}, bf16[896,2048]{1,0:T(8,128)(2,1)S(1)}) custom-call(bf16[896,4096]{1,0:T(8,128)(2,1)S(1)} %order_rows.3.rows_ref.grad_ref, bf16[896,4096]{1,0:T(8,128)(2,1)S(1)} %order_rows.3.rows_ref.grad_ref, ...), custom_call_target="tpu_custom_call" | custom-call | flops 7046430720 | bytes 37748736 | tf_op jit(solution)/shard_map/backward_experts/pallas_call | solution.py:228
  95.7 1.8 %token_sums.3 = (bf16[192,2048]{1,0:T(8,128)(2,1)S(1)}, bf16[192,2048]{1,0:T(8,128)(2,1)S(1)}) custom-call(bf16[384,896]{1,0:T(8,128)(2,1)S(1)} %get-tuple-element.51.mix_ref, bf16[896,2048]{1,0:T(8,128)(2,1)S(1)} %get-tuple-element.57.rows_ref), custom_call_target="tpu_custom_call" | custom-call | flops 1409286144 | bytes 5242880 | tf_op jit(solution)/shard_map/token_sums/pallas_call | solution.py:144
  98.5 2.8 %collective-permute-start.19 = (bf16[48,2048]{1,0:T(8,128)(2,1)S(1)}, bf16[48,2048]{1,0:T(8,128)(2,1)S(1)}, u32[]{:S(2)}, u32[]{:S(2)}) collective-permute-start(bf16[48,2048]{1,0:T(8,128)(2,1)S(1)} %get-tuple-element.76), channel_id=1, source_target_pairs={{0,6},{2,4},{4,2},{6,0},{1,7},{3,5},{5,3},{7,1},{8,14},{10,12},{12... | collective-permute-start | bytes 589832 | tf_op jit(solution)/shard_map/ppermute | solution.py:32
  101.2 1.7 %collective-permute-start.17 = (bf16[48,2048]{1,0:T(8,128)(2,1)S(1)}, bf16[48,2048]{1,0:T(8,128)(2,1)S(1)}, u32[]{:S(2)}, u32[]{:S(2)}) collective-permute-start(bf16[48,2048]{1,0:T(8,128)(2,1)S(1)} %get-tuple-element.78), channel_id=1, source_target_pairs={{0,2},{2,0},{4,6},{6,4},{1,3},{3,1},{5,7},{7,5},{8,10},{10,8},{12,... | collective-permute-start | bytes 589832 | tf_op jit(solution)/shard_map/ppermute | solution.py:32
  102.9 14.3 %weight_grads.1 = (bf16[8,2048,384]{2,1,0:T(8,128)(2,1)}, bf16[8,2048,384]{2,1,0:T(8,128)(2,1)}, bf16[8,384,2048]{2,1,0:T(8,128)(2,1)}) custom-call(bf16[896,4096]{1,0:T(8,128)(2,1)S(1)} %order_rows.3.rows_ref.grad_ref, bf16[896,4096]{1,0:T(8,128)(2,1)S(1)} %order_rows.3.rows_ref.grad_ref, bf16[896,384]{1,0:T(8,128)(2,1)S(1)} %get-tuple-element.49.hidden_ref, ...), custom_call_target="tpu_custom_call" | custom-call | flops 4227858432 | bytes 37748736 | tf_op jit(solution)/shard_map/weight_grads/pallas_call | solution.py:246
  118.0 2.4 %collective-permute-start.24 = (bf16[48,2048]{1,0:T(8,128)(2,1)S(1)}, bf16[48,2048]{1,0:T(8,128)(2,1)S(1)}, u32[]{:S(2)}, u32[]{:S(2)}) collective-permute-start(bf16[48,2048]{1,0:T(8,128)(2,1)S(1)} %get-tuple-element.74), channel_id=1, source_target_pairs={{0,6},{2,4},{4,2},{6,0},{1,7},{3,5},{5,3},{7,1},{8,14},{10,12},{12... | collective-permute-start | bytes 589832 | tf_op jit(solution)/shard_map/ppermute | solution.py:32
  121.4 2.5 %collective-permute-start.20 = (bf16[48,2048]{1,0:T(8,128)(2,1)S(1)}, bf16[48,2048]{1,0:T(8,128)(2,1)S(1)}, u32[]{:S(2)}, u32[]{:S(2)}) collective-permute-start(bf16[48,2048]{1,0:T(8,128)(2,1)S(1)} %add_convert_fusion.2), channel_id=1, source_target_pairs={{0,8},{8,16},{16,24},{24,0},{1,9},{9,17},{17,25},{25,1},{2,10},{10... | collective-permute-start | bytes 589832 | tf_op jit(solution)/shard_map/ppermute | solution.py:27
  123.9 2.3 %collective-permute-done.24 = bf16[48,2048]{1,0:T(8,128)(2,1)S(1)} collective-permute-done((bf16[48,2048]{1,0:T(8,128)(2,1)S(1)}, bf16[48,2048]{1,0:T(8,128)(2,1)S(1)}, u32[]{:S(2)}, u32[]{:S(2)}) %collective-permute-start.24) | collective-permute-done | bytes 196640 | tf_op jit(solution)/shard_map/ppermute | solution.py:32
  126.2 4.9 %collective-permute-done.23 = bf16[48,2048]{1,0:T(8,128)(2,1)S(1)} collective-permute-done((bf16[48,2048]{1,0:T(8,128)(2,1)S(1)}, bf16[48,2048]{1,0:T(8,128)(2,1)S(1)}, u32[]{:S(2)}, u32[]{:S(2)}) %collective-permute-start.23) | collective-permute-done | bytes 196640 | tf_op jit(solution)/shard_map/ppermute | solution.py:32
  131.3 2.7 %collective-permute-start.25 = (bf16[48,2048]{1,0:T(8,128)(2,1)S(1)}, bf16[48,2048]{1,0:T(8,128)(2,1)S(1)}, u32[]{:S(2)}, u32[]{:S(2)}) collective-permute-start(bf16[48,2048]{1,0:T(8,128)(2,1)S(1)} %fusion.5), channel_id=1, source_target_pairs={{0,24},{8,0},{16,8},{24,16},{1,25},{9,1},{17,9},{25,17},{2,26},{10... | collective-permute-start | bytes 589832 | tf_op jit(solution)/shard_map/ppermute | solution.py:27
  134.9 3.7 %collective-permute-done.26 = bf16[48,2048]{1,0:T(8,128)(2,1)S(1)} collective-permute-done((bf16[48,2048]{1,0:T(8,128)(2,1)S(1)}, bf16[48,2048]{1,0:T(8,128)(2,1)S(1)}, u32[]{:S(2)}, u32[]{:S(2)}) %collective-permute-start.26) | collective-permute-done | bytes 196640 | tf_op jit(solution)/shard_map/ppermute | solution.py:307
  (64 shorter events, 9.6 us)
Async XLA Ops:
  2.8 11.2 %collective-permute-start.2 = (s32[96,32]{0,1:T(8,128)S(1)}, s32[96,32]{0,1:T(8,128)S(1)}, u32[]{:S(2)}, u32[]{:S(2)}) collective-permute-start(s32[96,32]{0,1:T(8,128)S(1)} %pad_add_fusion.1), channel_id=1, source_target_pairs={{0,6},{2,4},{4,2},{6,0},{1,7},{3,5},{5,3},{7,1},{8,14},{10,12},{12... | collective-permute-start | bytes 36872 | tf_op jit(solution)/shard_map/ppermute | solution.py:32
  7.9 6.2 %collective-permute-start.1 = (s32[96,32]{0,1:T(8,128)S(1)}, s32[96,32]{0,1:T(8,128)S(1)}, u32[]{:S(2)}, u32[]{:S(2)}) collective-permute-start(s32[96,32]{0,1:T(8,128)S(1)} %pad_add_fusion.1), channel_id=1, source_target_pairs={{0,4},{2,6},{4,0},{6,2},{1,5},{3,7},{5,1},{7,3},{8,12},{10,14},{12... | collective-permute-start | bytes 36872 | tf_op jit(solution)/shard_map/ppermute | solution.py:32
  7.9 6.3 %collective-permute-start = (s32[96,32]{0,1:T(8,128)S(1)}, s32[96,32]{0,1:T(8,128)S(1)}, u32[]{:S(2)}, u32[]{:S(2)}) collective-permute-start(s32[96,32]{0,1:T(8,128)S(1)} %pad_add_fusion.1), channel_id=1, source_target_pairs={{0,2},{2,0},{4,6},{6,4},{1,3},{3,1},{5,7},{7,5},{8,10},{10,8},{12,... | collective-permute-start | bytes 36872 | tf_op jit(solution)/shard_map/ppermute | solution.py:32
  9.6 13.0 %collective-permute-start.3 = (bf16[48,2048]{1,0:T(8,128)(2,1)S(1)}, bf16[48,2048]{1,0:T(8,128)(2,1)S(1)}, u32[]{:S(2)}, u32[]{:S(2)}) collective-permute-start(bf16[48,2048]{1,0:T(8,128)(2,1)S(1)} %get-tuple-element.43.refs_0_), channel_id=1, source_target_pairs={{0,2},{2,0},{4,6},{6,4},{1,3},{3,1},{5,7},{7,5},{8,10},{10,8},{12,... | collective-permute-start | bytes 589832 | tf_op jit(solution)/shard_map/ppermute | solution.py:32
  11.0 11.1 %collective-permute-start.4 = (bf16[48,2048]{1,0:T(8,128)(2,1)S(1)}, bf16[48,2048]{1,0:T(8,128)(2,1)S(1)}, u32[]{:S(2)}, u32[]{:S(2)}) collective-permute-start(bf16[48,2048]{1,0:T(8,128)(2,1)S(1)} %get-tuple-element.43.refs_0_), channel_id=1, source_target_pairs={{0,4},{2,6},{4,0},{6,2},{1,5},{3,7},{5,1},{7,3},{8,12},{10,14},{12... | collective-permute-start | bytes 589832 | tf_op jit(solution)/shard_map/ppermute | solution.py:32
  22.1 12.1 %collective-permute-start.6 = (bf16[48,2048]{1,0:T(8,128)(2,1)S(1)}, bf16[48,2048]{1,0:T(8,128)(2,1)S(1)}, u32[]{:S(2)}, u32[]{:S(2)}) collective-permute-start(bf16[48,2048]{1,0:T(8,128)(2,1)S(1)} %collective-permute-done.4.refs_2_), channel_id=1, source_target_pairs={{0,2},{2,0},{4,6},{6,4},{1,3},{3,1},{5,7},{7,5},{8,10},{10,8},{12,... | collective-permute-start | bytes 589832 | tf_op jit(solution)/shard_map/ppermute | solution.py:32
  22.6 18.2 %collective-permute-start.5 = (bf16[48,4096]{1,0:T(8,128)(2,1)S(1)}, bf16[48,4096]{1,0:T(8,128)(2,1)S(1)}, u32[]{:S(2)}, u32[]{:S(2)}) collective-permute-start(bf16[48,4096]{1,0:T(8,128)(2,1)S(1)} %get-tuple-element.47.refs_0_), channel_id=1, source_target_pairs={{0,2},{2,0},{4,6},{6,4},{1,3},{3,1},{5,7},{7,5},{8,10},{10,8},{12,... | collective-permute-start | bytes 1179656 | tf_op jit(solution)/shard_map/ppermute | solution.py:32
  24.3 17.1 %collective-permute-start.7 = (bf16[48,2048]{1,0:T(8,128)(2,1)S(1)}, bf16[48,2048]{1,0:T(8,128)(2,1)S(1)}, u32[]{:S(2)}, u32[]{:S(2)}) collective-permute-start(bf16[48,2048]{1,0:T(8,128)(2,1)S(1)} %collective-permute-done.3.refs_1_), channel_id=1, source_target_pairs={{0,1},{1,0},{2,3},{3,2},{4,5},{5,4},{6,7},{7,6},{8,9},{9,8},{10,11... | collective-permute-start | bytes 589832 | tf_op jit(solution)/shard_map/ppermute | solution.py:32
  25.9 15.6 %collective-permute-start.8 = (bf16[48,2048]{1,0:T(8,128)(2,1)S(1)}, bf16[48,2048]{1,0:T(8,128)(2,1)S(1)}, u32[]{:S(2)}, u32[]{:S(2)}) collective-permute-start(bf16[48,2048]{1,0:T(8,128)(2,1)S(1)} %collective-permute-done.4.refs_2_), channel_id=1, source_target_pairs={{0,1},{1,0},{2,3},{3,2},{4,5},{5,4},{6,7},{7,6},{8,9},{9,8},{10,11... | collective-permute-start | bytes 589832 | tf_op jit(solution)/shard_map/ppermute | solution.py:32
  34.1 13.8 %collective-permute-start.10 = (bf16[48,4096]{1,0:T(8,128)(2,1)S(1)}, bf16[48,4096]{1,0:T(8,128)(2,1)S(1)}, u32[]{:S(2)}, u32[]{:S(2)}) collective-permute-start(bf16[48,4096]{1,0:T(8,128)(2,1)S(1)} %get-tuple-element.47.refs_0_), channel_id=1, source_target_pairs={{0,4},{2,6},{4,0},{6,2},{1,5},{3,7},{5,1},{7,3},{8,12},{10,14},{12... | collective-permute-start | bytes 1179656 | tf_op jit(solution)/shard_map/ppermute | solution.py:32
  34.7 7.8 %collective-permute-start.9 = (bf16[48,2048]{1,0:T(8,128)(2,1)S(1)}, bf16[48,2048]{1,0:T(8,128)(2,1)}, u32[]{:S(2)}, u32[]{:S(2)}) collective-permute-start(bf16[48,2048]{1,0:T(8,128)(2,1)S(1)} %collective-permute-done.6.refs_3_), channel_id=1, source_target_pairs={{0,1},{1,0},{2,3},{3,2},{4,5},{5,4},{6,7},{7,6},{8,9},{9,8},{10,11... | collective-permute-start | bytes 589832 | tf_op jit(solution)/shard_map/ppermute | solution.py:32
  40.8 29.5 %collective-permute-start.12 = (bf16[48,4096]{1,0:T(8,128)(2,1)S(1)}, bf16[48,4096]{1,0:T(8,128)(2,1)S(1)}, u32[]{:S(2)}, u32[]{:S(2)}) collective-permute-start(bf16[48,4096]{1,0:T(8,128)(2,1)S(1)} %collective-permute-done.5.refs_1_), channel_id=1, source_target_pairs={{0,1},{1,0},{2,3},{3,2},{4,5},{5,4},{6,7},{7,6},{8,9},{9,8},{10,11... | collective-permute-start | bytes 1179656 | tf_op jit(solution)/shard_map/ppermute | solution.py:32
  47.9 20.8 %collective-permute-start.14 = (bf16[48,4096]{1,0:T(8,128)(2,1)S(1)}, bf16[48,4096]{1,0:T(8,128)(2,1)S(1)}, u32[]{:S(2)}, u32[]{:S(2)}) collective-permute-start(bf16[48,4096]{1,0:T(8,128)(2,1)S(1)} %collective-permute-done.10.refs_2_), channel_id=1, source_target_pairs={{0,3},{1,2},{2,1},{3,0},{4,7},{5,6},{6,5},{7,4},{8,11},{9,10},{10,... | collective-permute-start | bytes 1179656 | tf_op jit(solution)/shard_map/ppermute | solution.py:272
  48.8 21.5 %collective-permute-start.13 = (bf16[48,4096]{1,0:T(8,128)(2,1)S(1)}, bf16[48,4096]{1,0:T(8,128)(2,1)S(1)}, u32[]{:S(2)}, u32[]{:S(2)}) collective-permute-start(bf16[48,4096]{1,0:T(8,128)(2,1)S(1)} %collective-permute-done.10.refs_2_), channel_id=1, source_target_pairs={{0,1},{1,0},{2,3},{3,2},{4,5},{5,4},{6,7},{7,6},{8,9},{9,8},{10,11... | collective-permute-start | bytes 1179656 | tf_op jit(solution)/shard_map/ppermute | solution.py:32
  49.4 20.9 %collective-permute-start.11 = (bf16[48,4096]{1,0:T(8,128)(2,1)S(1)}, bf16[48,4096]{1,0:T(8,128)(2,1)S(1)}, u32[]{:S(2)}, u32[]{:S(2)}) collective-permute-start(bf16[48,4096]{1,0:T(8,128)(2,1)S(1)} %collective-permute-done.10.refs_2_), channel_id=1, source_target_pairs={{0,2},{2,0},{4,6},{6,4},{1,3},{3,1},{5,7},{7,5},{8,10},{10,8},{12,... | collective-permute-start | bytes 1179656 | tf_op jit(solution)/shard_map/ppermute | solution.py:32
  68.7 27.0 %collective-permute-start.15 = (bf16[192,2048]{1,0:T(8,128)(2,1)S(1)}, bf16[192,2048]{1,0:T(8,128)(2,1)S(1)}, u32[]{:S(2)}, u32[]{:S(2)}) collective-permute-start(bf16[192,2048]{1,0:T(8,128)(2,1)S(1)} %get-tuple-element.56), channel_id=1, source_target_pairs={{0,1},{1,0},{2,3},{3,2},{4,5},{5,4},{6,7},{7,6},{8,9},{9,8},{10,11... | collective-permute-start | bytes 2359304 | tf_op jit(solution)/shard_map/ppermute | solution.py:32
  97.5 19.7 %collective-permute-start.16 = (bf16[192,2048]{1,0:T(8,128)(2,1)S(1)}, bf16[192,2048]{1,0:T(8,128)(2,1)S(1)}, u32[]{:S(2)}, u32[]{:S(2)}) collective-permute-start(bf16[192,2048]{1,0:T(8,128)(2,1)S(1)} %get-tuple-element.62), channel_id=1, source_target_pairs={{0,1},{1,0},{2,3},{3,2},{4,5},{5,4},{6,7},{7,6},{8,9},{9,8},{10,11... | collective-permute-start | bytes 2359304 | tf_op jit(solution)/shard_map/ppermute | solution.py:32
  98.5 18.8 %collective-permute-start.19 = (bf16[48,2048]{1,0:T(8,128)(2,1)S(1)}, bf16[48,2048]{1,0:T(8,128)(2,1)S(1)}, u32[]{:S(2)}, u32[]{:S(2)}) collective-permute-start(bf16[48,2048]{1,0:T(8,128)(2,1)S(1)} %get-tuple-element.76), channel_id=1, source_target_pairs={{0,6},{2,4},{4,2},{6,0},{1,7},{3,5},{5,3},{7,1},{8,14},{10,12},{12... | collective-permute-start | bytes 589832 | tf_op jit(solution)/shard_map/ppermute | solution.py:32
  101.2 16.0 %collective-permute-start.18 = (bf16[48,2048]{1,0:T(8,128)(2,1)S(1)}, bf16[48,2048]{1,0:T(8,128)(2,1)S(1)}, u32[]{:S(2)}, u32[]{:S(2)}) collective-permute-start(bf16[48,2048]{1,0:T(8,128)(2,1)S(1)} %get-tuple-element.77), channel_id=1, source_target_pairs={{0,4},{2,6},{4,0},{6,2},{1,5},{3,7},{5,1},{7,3},{8,12},{10,14},{12... | collective-permute-start | bytes 589832 | tf_op jit(solution)/shard_map/ppermute | solution.py:32
  101.2 16.0 %collective-permute-start.17 = (bf16[48,2048]{1,0:T(8,128)(2,1)S(1)}, bf16[48,2048]{1,0:T(8,128)(2,1)S(1)}, u32[]{:S(2)}, u32[]{:S(2)}) collective-permute-start(bf16[48,2048]{1,0:T(8,128)(2,1)S(1)} %get-tuple-element.78), channel_id=1, source_target_pairs={{0,2},{2,0},{4,6},{6,4},{1,3},{3,1},{5,7},{7,5},{8,10},{10,8},{12,... | collective-permute-start | bytes 589832 | tf_op jit(solution)/shard_map/ppermute | solution.py:32
  117.2 13.9 %copy-start = (bf16[1,96,2048]{2,1,0:T(8,128)(2,1)S(1)}, bf16[1,96,2048]{2,1,0:T(8,128)(2,1)}, u32[]{:S(2)}) copy-start(bf16[1,96,2048]{2,1,0:T(8,128)(2,1)} %param.16) | copy-start | bytes 1179652
  117.6 6.3 %collective-permute-start.22 = (bf16[48,2048]{1,0:T(8,128)(2,1)S(1)}, bf16[48,2048]{1,0:T(8,128)(2,1)S(1)}, u32[]{:S(2)}, u32[]{:S(2)}) collective-permute-start(bf16[48,2048]{1,0:T(8,128)(2,1)S(1)} %get-tuple-element.73), channel_id=1, source_target_pairs={{0,2},{2,0},{4,6},{6,4},{1,3},{3,1},{5,7},{7,5},{8,10},{10,8},{12,... | collective-permute-start | bytes 589832 | tf_op jit(solution)/shard_map/ppermute | solution.py:32
  118.0 8.2 %collective-permute-start.24 = (bf16[48,2048]{1,0:T(8,128)(2,1)S(1)}, bf16[48,2048]{1,0:T(8,128)(2,1)S(1)}, u32[]{:S(2)}, u32[]{:S(2)}) collective-permute-start(bf16[48,2048]{1,0:T(8,128)(2,1)S(1)} %get-tuple-element.74), channel_id=1, source_target_pairs={{0,6},{2,4},{4,2},{6,0},{1,7},{3,5},{5,3},{7,1},{8,14},{10,12},{12... | collective-permute-start | bytes 589832 | tf_op jit(solution)/shard_map/ppermute | solution.py:32
  120.5 10.7 %collective-permute-start.23 = (bf16[48,2048]{1,0:T(8,128)(2,1)S(1)}, bf16[48,2048]{1,0:T(8,128)(2,1)S(1)}, u32[]{:S(2)}, u32[]{:S(2)}) collective-permute-start(bf16[48,2048]{1,0:T(8,128)(2,1)S(1)} %get-tuple-element.75), channel_id=1, source_target_pairs={{0,4},{2,6},{4,0},{6,2},{1,5},{3,7},{5,1},{7,3},{8,12},{10,14},{12... | collective-permute-start | bytes 589832 | tf_op jit(solution)/shard_map/ppermute | solution.py:32
  121.3 12.8 %collective-permute-start.21 = (bf16[48,2048]{1,0:T(8,128)(2,1)S(1)}, bf16[48,2048]{1,0:T(8,128)(2,1)S(1)}, u32[]{:S(2)}, u32[]{:S(2)}) collective-permute-start(bf16[48,2048]{1,0:T(8,128)(2,1)S(1)} %add_convert_fusion.2), channel_id=1, source_target_pairs={{0,9},{1,8},{8,17},{9,16},{16,25},{17,24},{24,1},{25,0},{2,11},{3,... | collective-permute-start | bytes 589832 | tf_op jit(solution)/shard_map/ppermute | solution.py:307
  121.4 12.7 %collective-permute-start.20 = (bf16[48,2048]{1,0:T(8,128)(2,1)S(1)}, bf16[48,2048]{1,0:T(8,128)(2,1)S(1)}, u32[]{:S(2)}, u32[]{:S(2)}) collective-permute-start(bf16[48,2048]{1,0:T(8,128)(2,1)S(1)} %add_convert_fusion.2), channel_id=1, source_target_pairs={{0,8},{8,16},{16,24},{24,0},{1,9},{9,17},{17,25},{25,1},{2,10},{10... | collective-permute-start | bytes 589832 | tf_op jit(solution)/shard_map/ppermute | solution.py:27
  131.3 7.3 %collective-permute-start.26 = (bf16[48,2048]{1,0:T(8,128)(2,1)S(1)}, bf16[48,2048]{1,0:T(8,128)(2,1)S(1)}, u32[]{:S(2)}, u32[]{:S(2)}) collective-permute-start(bf16[48,2048]{1,0:T(8,128)(2,1)S(1)} %fusion.5), channel_id=1, source_target_pairs={{0,25},{1,24},{8,1},{9,0},{16,9},{17,8},{24,17},{25,16},{2,27},{3,... | collective-permute-start | bytes 589832 | tf_op jit(solution)/shard_map/ppermute | solution.py:307
  131.3 7.2 %collective-permute-start.25 = (bf16[48,2048]{1,0:T(8,128)(2,1)S(1)}, bf16[48,2048]{1,0:T(8,128)(2,1)S(1)}, u32[]{:S(2)}, u32[]{:S(2)}) collective-permute-start(bf16[48,2048]{1,0:T(8,128)(2,1)S(1)} %fusion.5), channel_id=1, source_target_pairs={{0,24},{8,0},{16,8},{24,16},{1,25},{9,1},{17,9},{25,17},{2,26},{10... | collective-permute-start | bytes 589832 | tf_op jit(solution)/shard_map/ppermute | solution.py:27

commit v5 on v4

--- a/solution.py
+++ b/solution.py
@@ -287,7 +287,7 @@
     pair = pair.reshape(groups, keep.shape[0] // groups, -1)
     if groups != 4:
         return [lax.all_to_all(pair, "expert", 0, 0, tiled=True)]
-    return [pair[0]] + [swap(pair[r], "expert", r) for r in range(1, groups)]
+    return [pair[0]] + [swap(pair[r], "expert", r) for r in range(groups - 1, 0, -1)]
 
 
 def sums_home(base, sent):

time: 140 us -> 138 us (0.986)
  waiting for transfers between devices: 27.9 us -> 25.2 us
    ppermute x22, waiting for transfers between devices: 24.2 us -> 21.6 us  [swap(): return lax.ppermute(block, axis, [(i, i ^ mask) for i in range(n)])]
  transfers between devices with their start and end apart: 27 -> 27, of which waited for: 7 -> 7; matrix products, arithmetic and copies ran while one was open for 4% -> 4% of each run, Pallas kernels for 46% -> 47%
where the time goes in v5:
time: 138 us
  Pallas kernels  66.1 us (48%)
  starting transfers between devices  36.8 us (27%)
  waiting for transfers between devices  25.2 us (18%)
  other arithmetic  6.39 us (5%)
  local copies, waits for them, and re-layouts  2.07 us (1%)
    ppermute x22, starting transfers between devices, swap(): return lax.ppermute(block, axis, [(i, i ^ mask) for i in range(n)])  30.5 us
    ppermute x22, waiting for transfers between devices, swap(): return lax.ppermute(block, axis, [(i, i ^ mask) for i in range(n)])  21.6 us
    pallas_call x1, Pallas kernels, backward_experts(): pl.pallas_call(backward_kernel, grid=(local,), in_specs=[wide, grad_wide,...  20.5 us
    pallas_call x1, Pallas kernels, forward_experts(): pl.pallas_call(forward_kernel, grid=(local,), in_specs=[wide, column, col...  15.5 us
    pallas_call x1, Pallas kernels, weight_grads(): pl.pallas_call(weights_kernel, grid=(local,), in_specs=[wide, grad_wide,...  14.3 us
    pallas_call x2, Pallas kernels, in_expert_order(): pl.pallas_call(kernel, grid=(steps,), in_specs=in_specs, out_specs=pl.Blo...  7.91 us
    ppermute x2, starting transfers between devices, rotate(): lax.ppermute(block, axis, [(i, (i + distance) % n) for i in range(n)])  5.26 us
    pallas_call x1, Pallas kernels, routing_matrices(): pl.pallas_call(functools.partial(routing_kernel, slots), out_shape=[jax.S...  4.32 us
  transfers between devices with their start and end apart: 27, of which 7 were waited for; matrix products, arithmetic and copies ran while one was open for 4% of the time, Pallas kernels for 47%

profile of v5, /device:TPU:0, one launch (start us, length us, event | category | flops | bytes accessed | tf_op | source)
XLA Modules:
  0.0 137.6 jit_solution(8081921634441627173)
XLA Ops:
  1.4 1.3 fusion
  2.8 5.1 %collective-permute-start.2 = (s32[96,32]{0,1:T(8,128)S(1)}, s32[96,32]{0,1:T(8,128)S(1)}, u32[]{:S(2)}, u32[]{:S(2)}) collective-permute-start(s32[96,32]{0,1:T(8,128)S(1)} %pad_add_fusion.1), channel_id=1, source_target_pairs={{0,6},{2,4},{4,2},{6,0},{1,7},{3,5},{5,3},{7,1},{8,14},{10,12},{12... | collective-permute-start | bytes 36872 | tf_op jit(solution)/shard_map/ppermute | solution.py:32
  8.5 1.0 dynamic-slice_bitcast_fusion
  9.6 1.5 %collective-permute-start.3 = (bf16[48,2048]{1,0:T(8,128)(2,1)S(1)}, bf16[48,2048]{1,0:T(8,128)(2,1)S(1)}, u32[]{:S(2)}, u32[]{:S(2)}) collective-permute-start(bf16[48,2048]{1,0:T(8,128)(2,1)S(1)} %get-tuple-element.43.refs_0_), channel_id=1, source_target_pairs={{0,2},{2,0},{4,6},{6,4},{1,3},{3,1},{5,7},{7,5},{8,10},{10,8},{12,... | collective-permute-start | bytes 589832 | tf_op jit(solution)/shard_map/ppermute | solution.py:32
  11.0 3.0 %collective-permute-start.4 = (bf16[48,2048]{1,0:T(8,128)(2,1)S(1)}, bf16[48,2048]{1,0:T(8,128)(2,1)S(1)}, u32[]{:S(2)}, u32[]{:S(2)}) collective-permute-start(bf16[48,2048]{1,0:T(8,128)(2,1)S(1)} %get-tuple-element.43.refs_0_), channel_id=1, source_target_pairs={{0,4},{2,6},{4,0},{6,2},{1,5},{3,7},{5,1},{7,3},{8,12},{10,14},{12... | collective-permute-start | bytes 589832 | tf_op jit(solution)/shard_map/ppermute | solution.py:32
  14.4 1.7 %reduce-window.6 = s32[8,2,3,128]{3,0,1,2:T(8,128)S(1)} reduce-window(s32[8,2,3,128]{3,0,1,2:T(8,128)S(1)} %copy_bitcast_fusion, s32[]{:T(128)} %constant.11.clone.1), window={size=1x1x1x128 pad=0_0x0_0x0_0x127_0}, to_apply=%region_1.2 | reduce-window | flops 780288 | bytes 49156 | tf_op jit(solution)/shard_map/reduce-window
  16.4 5.7 %collective-permute-done.4.refs_2_ = bf16[48,2048]{1,0:T(8,128)(2,1)S(1)} collective-permute-done((bf16[48,2048]{1,0:T(8,128)(2,1)S(1)}, bf16[48,2048]{1,0:T(8,128)(2,1)S(1)}, u32[]{:S(2)}, u32[]{:S(2)}) %collective-permute-start.4) | collective-permute-done | bytes 196640 | tf_op jit(solution)/shard_map/ppermute | solution.py:32
  22.6 1.7 %collective-permute-start.5 = (bf16[48,4096]{1,0:T(8,128)(2,1)S(1)}, bf16[48,4096]{1,0:T(8,128)(2,1)S(1)}, u32[]{:S(2)}, u32[]{:S(2)}) collective-permute-start(bf16[48,4096]{1,0:T(8,128)(2,1)S(1)} %get-tuple-element.47.refs_0_), channel_id=1, source_target_pairs={{0,2},{2,0},{4,6},{6,4},{1,3},{3,1},{5,7},{7,5},{8,10},{10,8},{12,... | collective-permute-start | bytes 1179656 | tf_op jit(solution)/shard_map/ppermute | solution.py:32
  24.3 1.6 %collective-permute-start.7 = (bf16[48,2048]{1,0:T(8,128)(2,1)S(1)}, bf16[48,2048]{1,0:T(8,128)(2,1)S(1)}, u32[]{:S(2)}, u32[]{:S(2)}) collective-permute-start(bf16[48,2048]{1,0:T(8,128)(2,1)S(1)} %collective-permute-done.3.refs_1_), channel_id=1, source_target_pairs={{0,1},{1,0},{2,3},{3,2},{4,5},{5,4},{6,7},{7,6},{8,9},{9,8},{10,11... | collective-permute-start | bytes 589832 | tf_op jit(solution)/shard_map/ppermute | solution.py:32
  26.4 7.8 %collective-permute-done.6.refs_3_ = bf16[48,2048]{1,0:T(8,128)(2,1)S(1)} collective-permute-done((bf16[48,2048]{1,0:T(8,128)(2,1)S(1)}, bf16[48,2048]{1,0:T(8,128)(2,1)S(1)}, u32[]{:S(2)}, u32[]{:S(2)}) %collective-permute-start.6) | collective-permute-done | bytes 196640 | tf_op jit(solution)/shard_map/ppermute | solution.py:32
  34.7 1.5 %collective-permute-start.9 = (bf16[48,2048]{1,0:T(8,128)(2,1)S(1)}, bf16[48,2048]{1,0:T(8,128)(2,1)}, u32[]{:S(2)}, u32[]{:S(2)}) collective-permute-start(bf16[48,2048]{1,0:T(8,128)(2,1)S(1)} %collective-permute-done.6.refs_3_), channel_id=1, source_target_pairs={{0,1},{1,0},{2,3},{3,2},{4,5},{5,4},{6,7},{7,6},{8,9},{9,8},{10,11... | collective-permute-start | bytes 589832 | tf_op jit(solution)/shard_map/ppermute | solution.py:32
  36.5 4.3 %routing.1 = (bf16[896,384]{1,0:T(8,128)(2,1)S(1)}, bf16[896,384]{1,0:T(8,128)(2,1)S(1)}, bf16[384,896]{1,0:T(8,128)(2,1)S(1)}, bf16[384,896]{1,0:T(8,128)(2,1)S(1)}, f32[896,1]{1,0:T(8,128)S(1)}) custom-call(s32[16,384]{1,0:T(8,128)S(1)} %get-tuple-element.89.dest_ref, f32[16,384]{1,0:T(8,128)S(1)} %bitcast.77, s32[384,16]{1,0:T(8,128)S(1)} %copy.29.dest_col_ref, ...), custom_call_target="tpu_custom_call" | custom-call | bytes 2752512 | tf_op jit(solution)/shard_map/routing/pallas_call | solution.py:74
  41.4 1.1 collective-permute-done.9.refs_7_
  42.5 3.0 %order_rows.2.rows_ref = bf16[896,2048]{1,0:T(8,128)(2,1)S(1)} custom-call(bf16[896,384]{1,0:T(8,128)(2,1)S(1)} %get-tuple-element.46.onehot_ref, bf16[48,2048]{1,0:T(8,128)(2,1)S(1)} %get-tuple-element.43.refs_0_, bf16[48,2048]{1,0:T(8,128)(2,1)S(1)} %collective-permute-done.3.refs_1_, bf16[48,2048]{1,0:T(8,128)(2,1)S(1)} %collective-permute-done.4.refs_2_, ...), custom_call_target="tpu_custom_call" | custom-call | flops 1409286144 | bytes 5242880 | tf_op jit(solution)/shard_map/order_rows/pallas_call | solution.py:119
  45.5 2.4 %collective-permute-done.10.refs_2_ = bf16[48,4096]{1,0:T(8,128)(2,1)S(1)} collective-permute-done((bf16[48,4096]{1,0:T(8,128)(2,1)S(1)}, bf16[48,4096]{1,0:T(8,128)(2,1)S(1)}, u32[]{:S(2)}, u32[]{:S(2)}) %collective-permute-start.10) | collective-permute-done | bytes 393248 | tf_op jit(solution)/shard_map/ppermute | solution.py:32
  47.9 0.9 collective-permute-start.14
  49.4 2.0 %collective-permute-start.11 = (bf16[48,4096]{1,0:T(8,128)(2,1)S(1)}, bf16[48,4096]{1,0:T(8,128)(2,1)S(1)}, u32[]{:S(2)}, u32[]{:S(2)}) collective-permute-start(bf16[48,4096]{1,0:T(8,128)(2,1)S(1)} %collective-permute-done.10.refs_2_), channel_id=1, source_target_pairs={{0,2},{2,0},{4,6},{6,4},{1,3},{3,1},{5,7},{7,5},{8,10},{10,8},{12,... | collective-permute-start | bytes 1179656 | tf_op jit(solution)/shard_map/ppermute | solution.py:32
  51.4 15.5 %forward_experts.1.rows_ref = bf16[896,2048]{1,0:T(8,128)(2,1)S(1)} custom-call(bf16[896,2048]{1,0:T(8,128)(2,1)S(1)} %order_rows.2.rows_ref, bf16[8,2048,384]{2,1,0:T(8,128)(2,1)} %bitcast.78, bf16[8,2048,384]{2,1,0:T(8,128)(2,1)} %bitcast.80, bf16[8,384,2048]{2,1,0:T(8,128)(2,1)} %bitcast.82), custom_call_target="tpu_custom_call" | custom-call | flops 4227858432 | bytes 37748736 | tf_op jit(solution)/shard_map/forward_experts/pallas_call | solution.py:209
  66.9 1.8 %token_sums.2 = (bf16[192,2048]{1,0:T(8,128)(2,1)S(1)}, bf16[192,2048]{1,0:T(8,128)(2,1)S(1)}) custom-call(bf16[384,896]{1,0:T(8,128)(2,1)S(1)} %get-tuple-element.53.mix_ref, bf16[896,2048]{1,0:T(8,128)(2,1)S(1)} %forward_experts.1.rows_ref), custom_call_target="tpu_custom_call" | custom-call | flops 1409286144 | bytes 5242880 | tf_op jit(solution)/shard_map/token_sums/pallas_call | solution.py:144
  68.7 1.6 %collective-permute-start.15 = (bf16[192,2048]{1,0:T(8,128)(2,1)S(1)}, bf16[192,2048]{1,0:T(8,128)(2,1)S(1)}, u32[]{:S(2)}, u32[]{:S(2)}) collective-permute-start(bf16[192,2048]{1,0:T(8,128)(2,1)S(1)} %get-tuple-element.56), channel_id=1, source_target_pairs={{0,1},{1,0},{2,3},{3,2},{4,5},{5,4},{6,7},{7,6},{8,9},{9,8},{10,11... | collective-permute-start | bytes 2359304 | tf_op jit(solution)/shard_map/ppermute | solution.py:32
  70.3 4.9 %order_rows.3.rows_ref.grad_ref = bf16[896,4096]{1,0:T(8,128)(2,1)S(1)} custom-call(bf16[896,384]{1,0:T(8,128)(2,1)S(1)} %get-tuple-element.40.onehot_ref, f32[896,1]{1,0:T(8,128)S(1)} %get-tuple-element.41.slot_weight_ref, bf16[48,4096]{1,0:T(8,128)(2,1)S(1)} %get-tuple-element.47.refs_0_, bf16[48,4096]{1,0:T(8,128)(2,1)S(1)} %collective-permute-done.5.refs_1_, ...), custom_call_target="tpu_custom_call" | custom-call | flops 2818572288 | bytes 10485760 | tf_op jit(solution)/shard_map/order_rows/pallas_call | solution.py:119
  75.2 20.5 %backward_experts.1 = (bf16[896,384]{1,0:T(8,128)(2,1)S(1)}, bf16[896,384]{1,0:T(8,128)(2,1)S(1)}, bf16[896,384]{1,0:T(8,128)(2,1)S(1)}, bf16[896,2048]{1,0:T(8,128)(2,1)S(1)}) custom-call(bf16[896,4096]{1,0:T(8,128)(2,1)S(1)} %order_rows.3.rows_ref.grad_ref, bf16[896,4096]{1,0:T(8,128)(2,1)S(1)} %order_rows.3.rows_ref.grad_ref, ...), custom_call_target="tpu_custom_call" | custom-call | flops 7046430720 | bytes 37748736 | tf_op jit(solution)/shard_map/backward_experts/pallas_call | solution.py:228
  95.7 1.8 %token_sums.3 = (bf16[192,2048]{1,0:T(8,128)(2,1)S(1)}, bf16[192,2048]{1,0:T(8,128)(2,1)S(1)}) custom-call(bf16[384,896]{1,0:T(8,128)(2,1)S(1)} %get-tuple-element.51.mix_ref, bf16[896,2048]{1,0:T(8,128)(2,1)S(1)} %get-tuple-element.57.rows_ref), custom_call_target="tpu_custom_call" | custom-call | flops 1409286144 | bytes 5242880 | tf_op jit(solution)/shard_map/token_sums/pallas_call | solution.py:144
  98.6 3.2 %collective-permute-start.18 = (bf16[48,2048]{1,0:T(8,128)(2,1)S(1)}, bf16[48,2048]{1,0:T(8,128)(2,1)S(1)}, u32[]{:S(2)}, u32[]{:S(2)}) collective-permute-start(bf16[48,2048]{1,0:T(8,128)(2,1)S(1)} %get-tuple-element.77), channel_id=1, source_target_pairs={{0,4},{2,6},{4,0},{6,2},{1,5},{3,7},{5,1},{7,3},{8,12},{10,14},{12... | collective-permute-start | bytes 589832 | tf_op jit(solution)/shard_map/ppermute | solution.py:32
  101.8 1.1 collective-permute-start.17
  102.9 14.3 %weight_grads.1 = (bf16[8,2048,384]{2,1,0:T(8,128)(2,1)}, bf16[8,2048,384]{2,1,0:T(8,128)(2,1)}, bf16[8,384,2048]{2,1,0:T(8,128)(2,1)}) custom-call(bf16[896,4096]{1,0:T(8,128)(2,1)S(1)} %order_rows.3.rows_ref.grad_ref, bf16[896,4096]{1,0:T(8,128)(2,1)S(1)} %order_rows.3.rows_ref.grad_ref, bf16[896,384]{1,0:T(8,128)(2,1)S(1)} %get-tuple-element.49.hidden_ref, ...), custom_call_target="tpu_custom_call" | custom-call | flops 4227858432 | bytes 37748736 | tf_op jit(solution)/shard_map/weight_grads/pallas_call | solution.py:246
  117.6 2.8 %collective-permute-start.22 = (bf16[48,2048]{1,0:T(8,128)(2,1)S(1)}, bf16[48,2048]{1,0:T(8,128)(2,1)S(1)}, u32[]{:S(2)}, u32[]{:S(2)}) collective-permute-start(bf16[48,2048]{1,0:T(8,128)(2,1)S(1)} %get-tuple-element.73), channel_id=1, source_target_pairs={{0,6},{2,4},{4,2},{6,0},{1,7},{3,5},{5,3},{7,1},{8,14},{10,12},{12... | collective-permute-start | bytes 589832 | tf_op jit(solution)/shard_map/ppermute | solution.py:32
  120.4 1.7 %collective-permute-start.23 = (bf16[48,2048]{1,0:T(8,128)(2,1)S(1)}, bf16[48,2048]{1,0:T(8,128)(2,1)S(1)}, u32[]{:S(2)}, u32[]{:S(2)}) collective-permute-start(bf16[48,2048]{1,0:T(8,128)(2,1)S(1)} %get-tuple-element.75), channel_id=1, source_target_pairs={{0,4},{2,6},{4,0},{6,2},{1,5},{3,7},{5,1},{7,3},{8,12},{10,14},{12... | collective-permute-start | bytes 589832 | tf_op jit(solution)/shard_map/ppermute | solution.py:32
  122.3 2.5 %collective-permute-start.20 = (bf16[48,2048]{1,0:T(8,128)(2,1)S(1)}, bf16[48,2048]{1,0:T(8,128)(2,1)S(1)}, u32[]{:S(2)}, u32[]{:S(2)}) collective-permute-start(bf16[48,2048]{1,0:T(8,128)(2,1)S(1)} %add_convert_fusion.2), channel_id=1, source_target_pairs={{0,8},{8,16},{16,24},{24,0},{1,9},{9,17},{17,25},{25,1},{2,10},{10... | collective-permute-start | bytes 589832 | tf_op jit(solution)/shard_map/ppermute | solution.py:27
  125.3 4.1 %collective-permute-done.24 = bf16[48,2048]{1,0:T(8,128)(2,1)S(1)} collective-permute-done((bf16[48,2048]{1,0:T(8,128)(2,1)S(1)}, bf16[48,2048]{1,0:T(8,128)(2,1)S(1)}, u32[]{:S(2)}, u32[]{:S(2)}) %collective-permute-start.24) | collective-permute-done | bytes 196640 | tf_op jit(solution)/shard_map/ppermute | solution.py:32
  129.6 2.7 %collective-permute-start.25 = (bf16[48,2048]{1,0:T(8,128)(2,1)S(1)}, bf16[48,2048]{1,0:T(8,128)(2,1)S(1)}, u32[]{:S(2)}, u32[]{:S(2)}) collective-permute-start(bf16[48,2048]{1,0:T(8,128)(2,1)S(1)} %fusion.5), channel_id=1, source_target_pairs={{0,24},{8,0},{16,8},{24,16},{1,25},{9,1},{17,9},{25,17},{2,26},{10... | collective-permute-start | bytes 589832 | tf_op jit(solution)/shard_map/ppermute | solution.py:27
  133.1 3.7 %collective-permute-done.26 = bf16[48,2048]{1,0:T(8,128)(2,1)S(1)} collective-permute-done((bf16[48,2048]{1,0:T(8,128)(2,1)S(1)}, bf16[48,2048]{1,0:T(8,128)(2,1)S(1)}, u32[]{:S(2)}, u32[]{:S(2)}) %collective-permute-start.26) | collective-permute-done | bytes 196640 | tf_op jit(solution)/shard_map/ppermute | solution.py:307
  (64 shorter events, 9.0 us)
Async XLA Ops:
  2.8 11.2 %collective-permute-start.2 = (s32[96,32]{0,1:T(8,128)S(1)}, s32[96,32]{0,1:T(8,128)S(1)}, u32[]{:S(2)}, u32[]{:S(2)}) collective-permute-start(s32[96,32]{0,1:T(8,128)S(1)} %pad_add_fusion.1), channel_id=1, source_target_pairs={{0,6},{2,4},{4,2},{6,0},{1,7},{3,5},{5,3},{7,1},{8,14},{10,12},{12... | collective-permute-start | bytes 36872 | tf_op jit(solution)/shard_map/ppermute | solution.py:32
  7.9 6.2 %collective-permute-start.1 = (s32[96,32]{0,1:T(8,128)S(1)}, s32[96,32]{0,1:T(8,128)S(1)}, u32[]{:S(2)}, u32[]{:S(2)}) collective-permute-start(s32[96,32]{0,1:T(8,128)S(1)} %pad_add_fusion.1), channel_id=1, source_target_pairs={{0,4},{2,6},{4,0},{6,2},{1,5},{3,7},{5,1},{7,3},{8,12},{10,14},{12... | collective-permute-start | bytes 36872 | tf_op jit(solution)/shard_map/ppermute | solution.py:32
  7.9 6.3 %collective-permute-start = (s32[96,32]{0,1:T(8,128)S(1)}, s32[96,32]{0,1:T(8,128)S(1)}, u32[]{:S(2)}, u32[]{:S(2)}) collective-permute-start(s32[96,32]{0,1:T(8,128)S(1)} %pad_add_fusion.1), channel_id=1, source_target_pairs={{0,2},{2,0},{4,6},{6,4},{1,3},{3,1},{5,7},{7,5},{8,10},{10,8},{12,... | collective-permute-start | bytes 36872 | tf_op jit(solution)/shard_map/ppermute | solution.py:32
  9.6 13.0 %collective-permute-start.3 = (bf16[48,2048]{1,0:T(8,128)(2,1)S(1)}, bf16[48,2048]{1,0:T(8,128)(2,1)S(1)}, u32[]{:S(2)}, u32[]{:S(2)}) collective-permute-start(bf16[48,2048]{1,0:T(8,128)(2,1)S(1)} %get-tuple-element.43.refs_0_), channel_id=1, source_target_pairs={{0,2},{2,0},{4,6},{6,4},{1,3},{3,1},{5,7},{7,5},{8,10},{10,8},{12,... | collective-permute-start | bytes 589832 | tf_op jit(solution)/shard_map/ppermute | solution.py:32
  11.0 11.1 %collective-permute-start.4 = (bf16[48,2048]{1,0:T(8,128)(2,1)S(1)}, bf16[48,2048]{1,0:T(8,128)(2,1)S(1)}, u32[]{:S(2)}, u32[]{:S(2)}) collective-permute-start(bf16[48,2048]{1,0:T(8,128)(2,1)S(1)} %get-tuple-element.43.refs_0_), channel_id=1, source_target_pairs={{0,4},{2,6},{4,0},{6,2},{1,5},{3,7},{5,1},{7,3},{8,12},{10,14},{12... | collective-permute-start | bytes 589832 | tf_op jit(solution)/shard_map/ppermute | solution.py:32
  22.1 12.1 %collective-permute-start.6 = (bf16[48,2048]{1,0:T(8,128)(2,1)S(1)}, bf16[48,2048]{1,0:T(8,128)(2,1)S(1)}, u32[]{:S(2)}, u32[]{:S(2)}) collective-permute-start(bf16[48,2048]{1,0:T(8,128)(2,1)S(1)} %collective-permute-done.4.refs_2_), channel_id=1, source_target_pairs={{0,2},{2,0},{4,6},{6,4},{1,3},{3,1},{5,7},{7,5},{8,10},{10,8},{12,... | collective-permute-start | bytes 589832 | tf_op jit(solution)/shard_map/ppermute | solution.py:32
  22.6 18.2 %collective-permute-start.5 = (bf16[48,4096]{1,0:T(8,128)(2,1)S(1)}, bf16[48,4096]{1,0:T(8,128)(2,1)S(1)}, u32[]{:S(2)}, u32[]{:S(2)}) collective-permute-start(bf16[48,4096]{1,0:T(8,128)(2,1)S(1)} %get-tuple-element.47.refs_0_), channel_id=1, source_target_pairs={{0,2},{2,0},{4,6},{6,4},{1,3},{3,1},{5,7},{7,5},{8,10},{10,8},{12,... | collective-permute-start | bytes 1179656 | tf_op jit(solution)/shard_map/ppermute | solution.py:32
  24.3 17.1 %collective-permute-start.7 = (bf16[48,2048]{1,0:T(8,128)(2,1)S(1)}, bf16[48,2048]{1,0:T(8,128)(2,1)S(1)}, u32[]{:S(2)}, u32[]{:S(2)}) collective-permute-start(bf16[48,2048]{1,0:T(8,128)(2,1)S(1)} %collective-permute-done.3.refs_1_), channel_id=1, source_target_pairs={{0,1},{1,0},{2,3},{3,2},{4,5},{5,4},{6,7},{7,6},{8,9},{9,8},{10,11... | collective-permute-start | bytes 589832 | tf_op jit(solution)/shard_map/ppermute | solution.py:32
  25.9 15.6 %collective-permute-start.8 = (bf16[48,2048]{1,0:T(8,128)(2,1)S(1)}, bf16[48,2048]{1,0:T(8,128)(2,1)S(1)}, u32[]{:S(2)}, u32[]{:S(2)}) collective-permute-start(bf16[48,2048]{1,0:T(8,128)(2,1)S(1)} %collective-permute-done.4.refs_2_), channel_id=1, source_target_pairs={{0,1},{1,0},{2,3},{3,2},{4,5},{5,4},{6,7},{7,6},{8,9},{9,8},{10,11... | collective-permute-start | bytes 589832 | tf_op jit(solution)/shard_map/ppermute | solution.py:32
  34.1 13.8 %collective-permute-start.10 = (bf16[48,4096]{1,0:T(8,128)(2,1)S(1)}, bf16[48,4096]{1,0:T(8,128)(2,1)S(1)}, u32[]{:S(2)}, u32[]{:S(2)}) collective-permute-start(bf16[48,4096]{1,0:T(8,128)(2,1)S(1)} %get-tuple-element.47.refs_0_), channel_id=1, source_target_pairs={{0,4},{2,6},{4,0},{6,2},{1,5},{3,7},{5,1},{7,3},{8,12},{10,14},{12... | collective-permute-start | bytes 1179656 | tf_op jit(solution)/shard_map/ppermute | solution.py:32
  34.7 7.8 %collective-permute-start.9 = (bf16[48,2048]{1,0:T(8,128)(2,1)S(1)}, bf16[48,2048]{1,0:T(8,128)(2,1)}, u32[]{:S(2)}, u32[]{:S(2)}) collective-permute-start(bf16[48,2048]{1,0:T(8,128)(2,1)S(1)} %collective-permute-done.6.refs_3_), channel_id=1, source_target_pairs={{0,1},{1,0},{2,3},{3,2},{4,5},{5,4},{6,7},{7,6},{8,9},{9,8},{10,11... | collective-permute-start | bytes 589832 | tf_op jit(solution)/shard_map/ppermute | solution.py:32
  40.8 29.5 %collective-permute-start.12 = (bf16[48,4096]{1,0:T(8,128)(2,1)S(1)}, bf16[48,4096]{1,0:T(8,128)(2,1)S(1)}, u32[]{:S(2)}, u32[]{:S(2)}) collective-permute-start(bf16[48,4096]{1,0:T(8,128)(2,1)S(1)} %collective-permute-done.5.refs_1_), channel_id=1, source_target_pairs={{0,1},{1,0},{2,3},{3,2},{4,5},{5,4},{6,7},{7,6},{8,9},{9,8},{10,11... | collective-permute-start | bytes 1179656 | tf_op jit(solution)/shard_map/ppermute | solution.py:32
  47.9 20.8 %collective-permute-start.14 = (bf16[48,4096]{1,0:T(8,128)(2,1)S(1)}, bf16[48,4096]{1,0:T(8,128)(2,1)S(1)}, u32[]{:S(2)}, u32[]{:S(2)}) collective-permute-start(bf16[48,4096]{1,0:T(8,128)(2,1)S(1)} %collective-permute-done.10.refs_2_), channel_id=1, source_target_pairs={{0,3},{1,2},{2,1},{3,0},{4,7},{5,6},{6,5},{7,4},{8,11},{9,10},{10,... | collective-permute-start | bytes 1179656 | tf_op jit(solution)/shard_map/ppermute | solution.py:272
  48.8 21.5 %collective-permute-start.13 = (bf16[48,4096]{1,0:T(8,128)(2,1)S(1)}, bf16[48,4096]{1,0:T(8,128)(2,1)S(1)}, u32[]{:S(2)}, u32[]{:S(2)}) collective-permute-start(bf16[48,4096]{1,0:T(8,128)(2,1)S(1)} %collective-permute-done.10.refs_2_), channel_id=1, source_target_pairs={{0,1},{1,0},{2,3},{3,2},{4,5},{5,4},{6,7},{7,6},{8,9},{9,8},{10,11... | collective-permute-start | bytes 1179656 | tf_op jit(solution)/shard_map/ppermute | solution.py:32
  49.4 20.9 %collective-permute-start.11 = (bf16[48,4096]{1,0:T(8,128)(2,1)S(1)}, bf16[48,4096]{1,0:T(8,128)(2,1)S(1)}, u32[]{:S(2)}, u32[]{:S(2)}) collective-permute-start(bf16[48,4096]{1,0:T(8,128)(2,1)S(1)} %collective-permute-done.10.refs_2_), channel_id=1, source_target_pairs={{0,2},{2,0},{4,6},{6,4},{1,3},{3,1},{5,7},{7,5},{8,10},{10,8},{12,... | collective-permute-start | bytes 1179656 | tf_op jit(solution)/shard_map/ppermute | solution.py:32
  68.7 27.0 %collective-permute-start.15 = (bf16[192,2048]{1,0:T(8,128)(2,1)S(1)}, bf16[192,2048]{1,0:T(8,128)(2,1)S(1)}, u32[]{:S(2)}, u32[]{:S(2)}) collective-permute-start(bf16[192,2048]{1,0:T(8,128)(2,1)S(1)} %get-tuple-element.56), channel_id=1, source_target_pairs={{0,1},{1,0},{2,3},{3,2},{4,5},{5,4},{6,7},{7,6},{8,9},{9,8},{10,11... | collective-permute-start | bytes 2359304 | tf_op jit(solution)/shard_map/ppermute | solution.py:32
  97.5 19.7 %collective-permute-start.16 = (bf16[192,2048]{1,0:T(8,128)(2,1)S(1)}, bf16[192,2048]{1,0:T(8,128)(2,1)S(1)}, u32[]{:S(2)}, u32[]{:S(2)}) collective-permute-start(bf16[192,2048]{1,0:T(8,128)(2,1)S(1)} %get-tuple-element.62), channel_id=1, source_target_pairs={{0,1},{1,0},{2,3},{3,2},{4,5},{5,4},{6,7},{7,6},{8,9},{9,8},{10,11... | collective-permute-start | bytes 2359304 | tf_op jit(solution)/shard_map/ppermute | solution.py:32
  98.5 18.8 %collective-permute-start.19 = (bf16[48,2048]{1,0:T(8,128)(2,1)S(1)}, bf16[48,2048]{1,0:T(8,128)(2,1)S(1)}, u32[]{:S(2)}, u32[]{:S(2)}) collective-permute-start(bf16[48,2048]{1,0:T(8,128)(2,1)S(1)} %get-tuple-element.76), channel_id=1, source_target_pairs={{0,2},{2,0},{4,6},{6,4},{1,3},{3,1},{5,7},{7,5},{8,10},{10,8},{12,... | collective-permute-start | bytes 589832 | tf_op jit(solution)/shard_map/ppermute | solution.py:32
  98.6 18.7 %collective-permute-start.18 = (bf16[48,2048]{1,0:T(8,128)(2,1)S(1)}, bf16[48,2048]{1,0:T(8,128)(2,1)S(1)}, u32[]{:S(2)}, u32[]{:S(2)}) collective-permute-start(bf16[48,2048]{1,0:T(8,128)(2,1)S(1)} %get-tuple-element.77), channel_id=1, source_target_pairs={{0,4},{2,6},{4,0},{6,2},{1,5},{3,7},{5,1},{7,3},{8,12},{10,14},{12... | collective-permute-start | bytes 589832 | tf_op jit(solution)/shard_map/ppermute | solution.py:32
  101.8 15.4 %collective-permute-start.17 = (bf16[48,2048]{1,0:T(8,128)(2,1)S(1)}, bf16[48,2048]{1,0:T(8,128)(2,1)S(1)}, u32[]{:S(2)}, u32[]{:S(2)}) collective-permute-start(bf16[48,2048]{1,0:T(8,128)(2,1)S(1)} %get-tuple-element.78), channel_id=1, source_target_pairs={{0,6},{2,4},{4,2},{6,0},{1,7},{3,5},{5,3},{7,1},{8,14},{10,12},{12... | collective-permute-start | bytes 589832 | tf_op jit(solution)/shard_map/ppermute | solution.py:32
  117.2 12.1 %copy-start = (bf16[1,96,2048]{2,1,0:T(8,128)(2,1)S(1)}, bf16[1,96,2048]{2,1,0:T(8,128)(2,1)}, u32[]{:S(2)}) copy-start(bf16[1,96,2048]{2,1,0:T(8,128)(2,1)} %param.16) | copy-start | bytes 1179652
  117.6 7.7 %collective-permute-start.22 = (bf16[48,2048]{1,0:T(8,128)(2,1)S(1)}, bf16[48,2048]{1,0:T(8,128)(2,1)S(1)}, u32[]{:S(2)}, u32[]{:S(2)}) collective-permute-start(bf16[48,2048]{1,0:T(8,128)(2,1)S(1)} %get-tuple-element.73), channel_id=1, source_target_pairs={{0,6},{2,4},{4,2},{6,0},{1,7},{3,5},{5,3},{7,1},{8,14},{10,12},{12... | collective-permute-start | bytes 589832 | tf_op jit(solution)/shard_map/ppermute | solution.py:32
  120.4 9.0 %collective-permute-start.24 = (bf16[48,2048]{1,0:T(8,128)(2,1)S(1)}, bf16[48,2048]{1,0:T(8,128)(2,1)S(1)}, u32[]{:S(2)}, u32[]{:S(2)}) collective-permute-start(bf16[48,2048]{1,0:T(8,128)(2,1)S(1)} %get-tuple-element.74), channel_id=1, source_target_pairs={{0,2},{2,0},{4,6},{6,4},{1,3},{3,1},{5,7},{7,5},{8,10},{10,8},{12,... | collective-permute-start | bytes 589832 | tf_op jit(solution)/shard_map/ppermute | solution.py:32
  120.4 9.0 %collective-permute-start.23 = (bf16[48,2048]{1,0:T(8,128)(2,1)S(1)}, bf16[48,2048]{1,0:T(8,128)(2,1)S(1)}, u32[]{:S(2)}, u32[]{:S(2)}) collective-permute-start(bf16[48,2048]{1,0:T(8,128)(2,1)S(1)} %get-tuple-element.75), channel_id=1, source_target_pairs={{0,4},{2,6},{4,0},{6,2},{1,5},{3,7},{5,1},{7,3},{8,12},{10,14},{12... | collective-permute-start | bytes 589832 | tf_op jit(solution)/shard_map/ppermute | solution.py:32
  122.2 10.1 %collective-permute-start.21 = (bf16[48,2048]{1,0:T(8,128)(2,1)S(1)}, bf16[48,2048]{1,0:T(8,128)(2,1)S(1)}, u32[]{:S(2)}, u32[]{:S(2)}) collective-permute-start(bf16[48,2048]{1,0:T(8,128)(2,1)S(1)} %add_convert_fusion.2), channel_id=1, source_target_pairs={{0,9},{1,8},{8,17},{9,16},{16,25},{17,24},{24,1},{25,0},{2,11},{3,... | collective-permute-start | bytes 589832 | tf_op jit(solution)/shard_map/ppermute | solution.py:307
  122.3 10.0 %collective-permute-start.20 = (bf16[48,2048]{1,0:T(8,128)(2,1)S(1)}, bf16[48,2048]{1,0:T(8,128)(2,1)S(1)}, u32[]{:S(2)}, u32[]{:S(2)}) collective-permute-start(bf16[48,2048]{1,0:T(8,128)(2,1)S(1)} %add_convert_fusion.2), channel_id=1, source_target_pairs={{0,8},{8,16},{16,24},{24,0},{1,9},{9,17},{17,25},{25,1},{2,10},{10... | collective-permute-start | bytes 589832 | tf_op jit(solution)/shard_map/ppermute | solution.py:27
  129.5 7.3 %collective-permute-start.26 = (bf16[48,2048]{1,0:T(8,128)(2,1)S(1)}, bf16[48,2048]{1,0:T(8,128)(2,1)S(1)}, u32[]{:S(2)}, u32[]{:S(2)}) collective-permute-start(bf16[48,2048]{1,0:T(8,128)(2,1)S(1)} %fusion.5), channel_id=1, source_target_pairs={{0,25},{1,24},{8,1},{9,0},{16,9},{17,8},{24,17},{25,16},{2,27},{3,... | collective-permute-start | bytes 589832 | tf_op jit(solution)/shard_map/ppermute | solution.py:307
  129.6 7.2 %collective-permute-start.25 = (bf16[48,2048]{1,0:T(8,128)(2,1)S(1)}, bf16[48,2048]{1,0:T(8,128)(2,1)S(1)}, u32[]{:S(2)}, u32[]{:S(2)}) collective-permute-start(bf16[48,2048]{1,0:T(8,128)(2,1)S(1)} %fusion.5), channel_id=1, source_target_pairs={{0,24},{8,0},{16,8},{24,16},{1,25},{9,1},{17,9},{25,17},{2,26},{10... | collective-permute-start | bytes 589832 | tf_op jit(solution)/shard_map/ppermute | solution.py:27
